TPU v7x, 512 devices: a whole 4x8x8 slice. The times are simulated.
512 devices in a mesh: ctx: 64 (over x, y, core), head: 8 (over z).
Axes of the slice: x: 4, y: 8, z: 8, core: 2. Of those that a mesh axis runs over, the one named last changes fastest.
Arguments:
- queries: bfloat16 [32768, 4096], P('ctx', 'head'), may hold values from -200 to 200
- keys: bfloat16 [32768, 4096], P('ctx', 'head'), may hold values from -8 to 8
- values: bfloat16 [32768, 4096], P('ctx', 'head'), may hold values from -6 to 6
- out_grad: bfloat16 [32768, 4096], P(('ctx', 'head')), may hold values from -6 to 6
- context_keys: bfloat16 [8192, 4096], P('ctx', 'head'), may hold values from -6 to 6
- context_values: bfloat16 [8192, 4096], P('ctx', 'head'), may hold values from -6 to 6
- selected: int32 [32, 64, 3], P('head', 'ctx'), may hold values from 0 to 15, as said below
- doc_lengths: int32 [64], replicated, may hold values from 1 to 1024, 32768 in all
Outputs:
- attended: bfloat16 [32768, 4096], P(('ctx', 'head'))
- query_grad: bfloat16 [32768, 4096], P('ctx', 'head')
- key_grad: bfloat16 [32768, 4096], P('ctx', 'head')
- value_grad: bfloat16 [32768, 4096], P('ctx', 'head')
- context_key_grad: bfloat16 [8192, 4096], P('ctx', 'head')
- context_value_grad: bfloat16 [8192, 4096], P('ctx', 'head')
Inputs may be any that keep to these rules, and one draw needn't show every extreme that they name: `selected`: the three entries of a row differ. Among the rows of one device (its 4 heads and 1 query blocks) no context block is named more than 1 times, and in every device's rows some block is named exactly 1 times.
All inputs are finite; a program needn't handle non-finite values.
Results may differ from a plain program's by a relative error of at most 0.0103.
The roundings to bfloat16 on the way count: a program that leaves them out, or rounds other values in their place, can miss the bound.
Values may be sent and summed in bfloat16 or wider, within the bound.
No kernel may reach another device: no remote copies, remote signals or barrier semaphores. Data moves between devices by JAX's collectives and lax.ppermute only.
A program may use at most 128 MiB of HBM per device.

v0:
```python
import jax
import jax.numpy as jnp
from jax import lax
from jax.sharding import PartitionSpec as P


def slot_codes(chosen_flat, pick_head, capacity, slot_count):
    pick_order = jnp.arange(chosen_flat.shape[0], dtype=jnp.int32)
    earlier = (chosen_flat[None, :] == chosen_flat[:, None]) & (
        pick_order[None, :] < pick_order[:, None]
    )
    rank_of = jnp.sum(earlier.astype(jnp.int32), axis=1)
    slot_of = chosen_flat * capacity + rank_of
    slot_hits = jnp.arange(slot_count, dtype=jnp.int32)[:, None] == slot_of[None, :]
    slot_heads = jnp.max(jnp.where(slot_hits, pick_head[None, :], -1), axis=1)
    return (slot_of, slot_heads)


def accumulate(buffers, slot_heads, head_count):
    onehot = (slot_heads[:, None] == jnp.arange(head_count, dtype=jnp.int32)[None, :]).astype(
        jnp.float32
    )
    return jnp.einsum("sh,sxc->hxc", onehot, buffers, precision=lax.Precision.HIGHEST)


def on_device(queries, keys, values, out_grad, context_keys, context_values, selected, doc_lengths):
    head_count = selected.shape[0]
    blocks_here = selected.shape[1]
    row_count = queries.shape[0]
    head_width = queries.shape[1] // head_count
    block_rows = row_count // blocks_here
    piece_rows = context_keys.shape[0]
    pieces = block_rows // piece_rows
    owners = lax.axis_size("ctx")
    device = lax.axis_index("ctx")
    block_count = owners // pieces
    capacity = -(-3 * head_count * blocks_here // block_count)
    slot_count = block_count * capacity
    score_scale = head_width ** (-0.5)
    chosen_flat = selected.reshape(-1)
    pick_count = chosen_flat.shape[0]
    pick_order = jnp.arange(pick_count, dtype=jnp.int32)
    pick_head = pick_order // (blocks_here * 3)
    slot_of, slot_heads = slot_codes(chosen_flat, pick_head, capacity, slot_count)
    all_lists = lax.all_gather(selected, "ctx", axis=1, tiled=True)
    per_source = all_lists.transpose(1, 0, 2).reshape(owners, pick_count)

    def source_codes(source_lists):
        return slot_codes(source_lists, pick_head, capacity, slot_count)[1]

    all_codes = jax.vmap(source_codes)(per_source)
    incoming = lax.dynamic_slice_in_dim(all_codes, device // pieces * capacity, capacity, 1)
    flat_in = incoming.reshape(-1)
    context_tiles = jnp.concatenate(
        [
            context_keys.reshape(piece_rows, head_count, head_width),
            context_values.reshape(piece_rows, head_count, head_width),
        ],
        axis=-1,
    )
    context_tiles = context_tiles.transpose(1, 0, 2)
    outgoing = jnp.where(
        flat_in[:, None, None] >= 0,
        context_tiles[jnp.maximum(flat_in, 0)],
        jnp.zeros((), jnp.bfloat16),
    )
    fetched = lax.all_to_all(
        outgoing.reshape(owners, capacity, piece_rows, 2 * head_width),
        "ctx",
        split_axis=0,
        concat_axis=0,
        tiled=True,
    )
    whole_tiles = fetched.reshape(
        block_count, pieces, capacity, piece_rows, 2 * head_width
    ).transpose(0, 2, 1, 3, 4)
    whole_tiles = whole_tiles.reshape(slot_count, block_rows, 2 * head_width)
    picked = whole_tiles[slot_of].reshape(head_count, blocks_here, 3 * block_rows, 2 * head_width)
    grad_rows = lax.all_to_all(out_grad, "head", split_axis=1, concat_axis=0, tiled=True)
    block_shape = (blocks_here, block_rows, head_count, head_width)
    query_heads = queries.reshape(block_shape).transpose(2, 0, 1, 3)
    key_heads = keys.reshape(block_shape).transpose(2, 0, 1, 3)
    value_heads = values.reshape(block_shape).transpose(2, 0, 1, 3)
    grad_heads = grad_rows.reshape(block_shape).transpose(2, 0, 1, 3)
    doc_ends = jnp.cumsum(doc_lengths)
    positions = device * row_count + jnp.arange(row_count, dtype=jnp.int32)
    token_doc = jnp.sum((doc_ends[None, :] <= positions[:, None]).astype(jnp.int32), axis=1)
    token_doc = token_doc.reshape(blocks_here, block_rows)
    inside = jnp.arange(block_rows, dtype=jnp.int32)
    causal = inside[None, :] <= inside[:, None]
    allowed = causal[None] & (token_doc[:, :, None] == token_doc[:, None, :])

    def one_head(operands):
        query_one, key_one, value_one, grad_one, far_one = operands
        far_keys = far_one[..., :head_width]
        far_values = far_one[..., head_width:]
        near_scores = (
            jnp.einsum("gqd,gkd->gqk", query_one, key_one, preferred_element_type=jnp.float32)
            * score_scale
        )
        far_scores = (
            jnp.einsum("gqd,gkd->gqk", query_one, far_keys, preferred_element_type=jnp.float32)
            * score_scale
        )
        scores = jnp.concatenate([jnp.where(allowed, near_scores, -jnp.inf), far_scores], axis=-1)
        row_max = jnp.max(scores, axis=-1, keepdims=True)
        lifted = jnp.exp(scores - row_max)
        row_total = jnp.sum(lifted, axis=-1, keepdims=True)
        weights = lifted / row_total
        weights_low = weights.astype(jnp.bfloat16)
        attended = (
            jnp.einsum(
                "gqk,gkd->gqd",
                weights_low[..., :block_rows],
                value_one,
                preferred_element_type=jnp.float32,
            )
            + jnp.einsum(
                "gqk,gkd->gqd",
                weights_low[..., block_rows:],
                far_values,
                preferred_element_type=jnp.float32,
            )
        ).astype(jnp.bfloat16)
        weight_grads = jnp.concatenate(
            [
                jnp.einsum("gqd,gkd->gqk", grad_one, value_one, preferred_element_type=jnp.float32),
                jnp.einsum(
                    "gqd,gkd->gqk", grad_one, far_values, preferred_element_type=jnp.float32
                ),
            ],
            axis=-1,
        )
        row_delta = jnp.sum(
            grad_one.astype(jnp.float32) * attended.astype(jnp.float32), axis=-1, keepdims=True
        )
        score_grads = (weights * (weight_grads - row_delta) * score_scale).astype(jnp.bfloat16)
        query_grad = (
            jnp.einsum(
                "gqk,gkd->gqd",
                score_grads[..., :block_rows],
                key_one,
                preferred_element_type=jnp.float32,
            )
            + jnp.einsum(
                "gqk,gkd->gqd",
                score_grads[..., block_rows:],
                far_keys,
                preferred_element_type=jnp.float32,
            )
        ).astype(jnp.bfloat16)
        key_grad = jnp.einsum(
            "gqk,gqd->gkd",
            score_grads[..., :block_rows],
            query_one,
            preferred_element_type=jnp.float32,
        ).astype(jnp.bfloat16)
        value_grad = jnp.einsum(
            "gqk,gqd->gkd",
            weights_low[..., :block_rows],
            grad_one,
            preferred_element_type=jnp.float32,
        ).astype(jnp.bfloat16)
        extra = jnp.concatenate(
            [
                jnp.einsum(
                    "gqk,gqd->gkd",
                    score_grads[..., block_rows:],
                    query_one,
                    preferred_element_type=jnp.float32,
                ),
                jnp.einsum(
                    "gqk,gqd->gkd",
                    weights_low[..., block_rows:],
                    grad_one,
                    preferred_element_type=jnp.float32,
                ),
            ],
            axis=-1,
        )
        return (attended, query_grad, key_grad, value_grad, extra)

    attended, query_grad, key_grad, value_grad, extra = lax.map(
        one_head, (query_heads, key_heads, value_heads, grad_heads, picked)
    )
    tile_parts = extra.reshape(pick_count, block_rows, 2 * head_width)
    buffer = (
        jnp.zeros((slot_count, block_rows, 2 * head_width), jnp.float32).at[slot_of].set(tile_parts)
    )
    sending = buffer.reshape(block_count, capacity, pieces, piece_rows, 2 * head_width).transpose(
        0, 2, 1, 3, 4
    )
    returned = lax.all_to_all(
        sending.reshape(owners, capacity, piece_rows, 2 * head_width),
        "ctx",
        split_axis=0,
        concat_axis=0,
        tiled=True,
    )
    summed = accumulate(
        returned.reshape(owners * capacity, piece_rows, 2 * head_width), flat_in, head_count
    )
    context_key_grad = (
        summed[..., :head_width].transpose(1, 0, 2).reshape(piece_rows, head_count * head_width)
    )
    context_value_grad = (
        summed[..., head_width:].transpose(1, 0, 2).reshape(piece_rows, head_count * head_width)
    )
    flat_shape = (row_count, head_count * head_width)

    def to_rows(stacked):
        return stacked.transpose(1, 2, 0, 3).reshape(flat_shape)

    output_rows = lax.all_to_all(to_rows(attended), "head", split_axis=0, concat_axis=1, tiled=True)
    return (
        output_rows,
        to_rows(query_grad),
        to_rows(key_grad),
        to_rows(value_grad),
        context_key_grad.astype(jnp.bfloat16),
        context_value_grad.astype(jnp.bfloat16),
    )


def solution(mesh):
    in_specs = (
        P("ctx", "head"),
        P("ctx", "head"),
        P("ctx", "head"),
        P(("ctx", "head"), None),
        P("ctx", "head"),
        P("ctx", "head"),
        P("head", "ctx", None),
        P(),
    )
    out_specs = (
        P(("ctx", "head"), None),
        P("ctx", "head"),
        P("ctx", "head"),
        P("ctx", "head"),
        P("ctx", "head"),
        P("ctx", "head"),
    )
    return jax.shard_map(
        on_device, mesh=mesh, in_specs=in_specs, out_specs=out_specs, check_vma=False
    )
```

profile of v0, /device:TPU:1, one launch (start us, length us, event | category | flops | bytes accessed | tf_op | source)
XLA Modules:
  0.0 540.1 jit_solution(11475679873144955691)
XLA Ops:
  0.6 1.9 copy.179
  2.5 10.9 %all-to-all-start.1 = ((bf16[64,8,512]{2,0,1:T(8,128)(2,1)}), bf16[64,8,512]{2,0,1:T(8,128)(2,1)S(1)}, u32[]{:S(2)}, u32[]{:S(2)}) async-start(bf16[64,8,512]{2,0,1:T(8,128)(2,1)} %bitcast.192), calls=%async_computation.1 | async-start | bytes 1048576 | tf_op jit(solution)/shard_map/all_to_all | solution.py:79
  14.2 51.5 %all_gather.3 = s32[4,64,3]{2,0,1:T(4,128)S(1)} all-gather(s32[4,1,3]{2,0,1:T(4,128)S(1)} %copy.125), channel_id=1, replica_groups=mesh['ctx'=64,'head'=8] {'ctx'}, dimensions={1}, use_global_device_ids=true | all-gather | bytes 3120 | tf_op jit(solution)/shard_map/all_gather | solution.py:45
  68.4 2.8 gather_fusion
  71.2 4.5 fusion.59
  75.7 7.5 %all-to-all-start = ((bf16[64,1,128,256]{3,2,1,0:T(8,128)(2,1)}), bf16[64,1,128,256]{3,2,1,0:T(8,128)(2,1)}, u32[]{:S(2)}, u32[]{:S(2)}) async-start(bf16[64,1,128,256]{3,2,1,0:T(8,128)(2,1)} %fusion.59), calls=%async_computation | async-start | bytes 8388608 | tf_op jit(solution)/shard_map/all_to_all | solution.py:67
  88.3 90.8 %all-to-all-done = bf16[64,1,128,256]{3,2,1,0:T(8,128)(2,1)} async-done(((bf16[64,1,128,256]{3,2,1,0:T(8,128)(2,1)}), bf16[64,1,128,256]{3,2,1,0:T(8,128)(2,1)}, u32[]{:S(2)}, u32[]{:S(2)}) %all-to-all-start) | async-done | bytes 4194336 | tf_op jit(solution)/shard_map/all_to_all | solution.py:67
  179.1 4.7 gather_fusion.1
  183.8 125.7 %while.19 = (s32[]{:T(128)}, bf16[4,1,512,128]{2,3,1,0:T(8,128)(2,1)}, bf16[4,1,512,128]{3,2,1,0:T(8,128)(2,1)}, bf16[4,1,512,128]{3,2,1,0:T(8,128)(2,1)}, bf16[...) while((s32[]{:T(128)}, ...), condition=%wide.region_10.11_spmd.clone, body=%wide.region_5.10_spmd.clone.sunk | while | flops 1630534144 | bytes 100571024 | solution.py:183
  187.5 2.3 fusion.99
  189.8 2.5 copy.182
  192.4 2.0 fusion.100
  202.9 3.2 copy.183
  206.1 2.7 constant_dynamic-update-slice_fusion.2
  209.4 1.9 fusion.105
  211.3 1.9 fusion.106
  213.2 2.1 fusion.107
  218.9 2.3 fusion.99
  221.3 2.5 copy.182
  223.8 2.0 fusion.100
  234.3 3.2 copy.183
  237.6 2.7 constant_dynamic-update-slice_fusion.2
  240.8 1.9 fusion.105
  242.7 1.9 fusion.106
  244.6 2.1 fusion.107
  250.4 2.3 fusion.99
  252.7 2.5 copy.182
  255.3 2.0 fusion.100
  265.8 3.2 copy.183
  269.0 2.7 constant_dynamic-update-slice_fusion.2
  272.2 1.9 fusion.105
  274.1 1.9 fusion.106
  276.0 2.1 fusion.107
  281.8 2.3 fusion.99
  284.1 2.5 copy.182
  286.7 2.0 fusion.100
  297.2 3.2 copy.183
  300.4 2.6 constant_dynamic-update-slice_fusion.2
  303.6 1.9 fusion.105
  305.5 1.9 fusion.106
  307.4 2.1 fusion.107
  311.8 6.9 %all-to-all-start.2 = ((bf16[8,64,512]{2,1,0:T(8,128)(2,1)}), bf16[8,64,512]{2,1,0:T(8,128)(2,1)S(1)}, u32[]{:S(2)}, u32[]{:S(2)}) async-start(bf16[8,64,512]{2,1,0:T(8,128)(2,1)} %all_to_all.36), calls=%async_computation.2 | async-start | bytes 1048576 | tf_op jit(solution)/shard_map/all_to_all | solution.py:214
  318.7 4.1 broadcast_in_dim.76
  322.8 11.6 %scatter_fusion = f32[16,512,256]{2,1,0:T(8,128)} fusion(f32[16,512,256]{2,1,0:T(8,128)} %broadcast_in_dim.76, s32[12]{0:T(128)S(1)} %fusion.66, f32[12,512,256]{2,1,0:T(8,128)} %bitcast.274), kind=kCustom, calls=%fused_computation.2 | custom fusion | bytes 18874416 | tf_op jit(solution)/shard_map/scatter | solution.py:188
  334.5 2.2 all-to-all-done.2
  336.7 6.4 %all-to-all-start.3 = ((f32[64,1,128,256]{3,2,1,0:T(8,128)}), f32[64,1,128,256]{3,2,1,0:T(8,128)}, u32[]{:S(2)}, u32[]{:S(2)}) async-start(f32[64,1,128,256]{3,2,1,0:T(8,128)} %bitcast.270), calls=%async_computation.3 | async-start | bytes 16777216 | tf_op jit(solution)/shard_map/all_to_all | solution.py:193
  347.2 181.7 %all-to-all-done.3 = f32[64,1,128,256]{3,2,1,0:T(8,128)} async-done(((f32[64,1,128,256]{3,2,1,0:T(8,128)}), f32[64,1,128,256]{3,2,1,0:T(8,128)}, u32[]{:S(2)}, u32[]{:S(2)}) %all-to-all-start.3) | async-done | bytes 8388640 | tf_op jit(solution)/shard_map/all_to_all | solution.py:193
  528.9 10.4 %fusion.60 = bf16[4,128,256]{2,0,1:T(4,128)(2,1)S(1)} fusion(f32[64,1,128,256]{3,2,1,0:T(8,128)} %all-to-all-done.3, s32[64]{0:T(128)S(1)} %get-tuple-element.189), kind=kOutput, calls=%fused_computation.87 | convolution fusion | flops 100794624 | bytes 8651008 | tf_op jit(solution)/shard_map/sh,sxc->hxc/dot_general | solution.py:23
  (189 shorter events, 66.3 us)
Async XLA Ops:
  2.5 73.2 %all-to-all-start.1 = ((bf16[64,8,512]{2,0,1:T(8,128)(2,1)}), bf16[64,8,512]{2,0,1:T(8,128)(2,1)S(1)}, u32[]{:S(2)}, u32[]{:S(2)}) async-start(bf16[64,8,512]{2,0,1:T(8,128)(2,1)} %bitcast.192), calls=%async_computation.1 | async-start | bytes 1048576 | tf_op jit(solution)/shard_map/all_to_all | solution.py:79
  75.7 7.7 %copy-start.15 = (s32[64]{0:T(128)S(1)}, s32[64]{0:T(128)}, u32[]{:S(2)}) copy-start(s32[64]{0:T(128)} %param.17) | copy-start | bytes 772
  75.7 8.0 %copy-start.9 = (bf16[512,512]{1,0:T(8,128)(2,1)S(1)}, bf16[512,512]{1,0:T(8,128)(2,1)}, u32[]{:S(2)}) copy-start(bf16[512,512]{1,0:T(8,128)(2,1)} %param.10) | copy-start | bytes 1572868
  75.7 9.0 %copy-start.10 = (bf16[512,512]{1,0:T(8,128)(2,1)S(1)}, bf16[512,512]{1,0:T(8,128)(2,1)}, u32[]{:S(2)}) copy-start(bf16[512,512]{1,0:T(8,128)(2,1)} %param.12) | copy-start | bytes 1572868
  75.7 10.1 %copy-start.11 = (bf16[512,512]{1,0:T(8,128)(2,1)S(1)}, bf16[512,512]{1,0:T(8,128)(2,1)}, u32[]{:S(2)}) copy-start(bf16[512,512]{1,0:T(8,128)(2,1)} %param.11) | copy-start | bytes 1572868
  75.7 103.4 %all-to-all-start = ((bf16[64,1,128,256]{3,2,1,0:T(8,128)(2,1)}), bf16[64,1,128,256]{3,2,1,0:T(8,128)(2,1)}, u32[]{:S(2)}, u32[]{:S(2)}) async-start(bf16[64,1,128,256]{3,2,1,0:T(8,128)(2,1)} %fusion.59), calls=%async_computation | async-start | bytes 8388608 | tf_op jit(solution)/shard_map/all_to_all | solution.py:67
  185.0 0.9 copy-start.4
  192.4 2.0 copy-start
  194.4 1.2 copy-start.5
  194.4 1.8 copy-start.8
  194.4 2.8 copy-start.7
  195.6 5.6 %copy-start.1 = (bf16[1,512,2048]{2,1,0:T(8,128)(2,1)}, bf16[1,512,2048]{2,1,0:T(8,128)(2,1)S(1)}, u32[]{:S(2)}) copy-start(bf16[1,512,2048]{2,1,0:T(8,128)(2,1)S(1)} %fusion.101) | copy-start | bytes 6291460 | tf_op jit(solution)/shard_map/while
  199.7 1.9 copy-start.2
  201.6 7.2 %copy-start.6 = (bf16[1,1536,256]{2,1,0:T(8,128)(2,1)S(1)}, bf16[1,1536,256]{2,1,0:T(8,128)(2,1)}, u32[]{:S(2)}) copy-start(bf16[1,1536,256]{2,1,0:T(8,128)(2,1)} %copy-done.4) | copy-start | bytes 2359300 | tf_op jit(solution)/shard_map/while
  202.9 5.9 %copy-start.3 = (bf16[1,512,2048]{2,1,0:T(8,128)(2,1)S(1)}, bf16[1,512,2048]{2,1,0:T(8,128)(2,1)}, u32[]{:S(2)}) copy-start(bf16[1,512,2048]{2,1,0:T(8,128)(2,1)} %copy-done.2) | copy-start | bytes 6291460 | tf_op jit(solution)/shard_map/while
  216.4 0.9 copy-start.4
  223.8 2.0 copy-start
  225.9 1.2 copy-start.5
  225.9 1.8 copy-start.8
  225.9 2.8 copy-start.7
  227.1 5.6 %copy-start.1 = (bf16[1,512,2048]{2,1,0:T(8,128)(2,1)}, bf16[1,512,2048]{2,1,0:T(8,128)(2,1)S(1)}, u32[]{:S(2)}) copy-start(bf16[1,512,2048]{2,1,0:T(8,128)(2,1)S(1)} %fusion.101) | copy-start | bytes 6291460 | tf_op jit(solution)/shard_map/while
  231.2 1.9 copy-start.2
  233.1 7.1 %copy-start.6 = (bf16[1,1536,256]{2,1,0:T(8,128)(2,1)S(1)}, bf16[1,1536,256]{2,1,0:T(8,128)(2,1)}, u32[]{:S(2)}) copy-start(bf16[1,1536,256]{2,1,0:T(8,128)(2,1)} %copy-done.4) | copy-start | bytes 2359300 | tf_op jit(solution)/shard_map/while
  234.3 5.9 %copy-start.3 = (bf16[1,512,2048]{2,1,0:T(8,128)(2,1)S(1)}, bf16[1,512,2048]{2,1,0:T(8,128)(2,1)}, u32[]{:S(2)}) copy-start(bf16[1,512,2048]{2,1,0:T(8,128)(2,1)} %copy-done.2) | copy-start | bytes 6291460 | tf_op jit(solution)/shard_map/while
  247.8 0.9 copy-start.4
  255.3 2.0 copy-start
  257.3 1.2 copy-start.5
  257.3 1.9 copy-start.8
  257.3 2.8 copy-start.7
  258.5 5.6 %copy-start.1 = (bf16[1,512,2048]{2,1,0:T(8,128)(2,1)}, bf16[1,512,2048]{2,1,0:T(8,128)(2,1)S(1)}, u32[]{:S(2)}) copy-start(bf16[1,512,2048]{2,1,0:T(8,128)(2,1)S(1)} %fusion.101) | copy-start | bytes 6291460 | tf_op jit(solution)/shard_map/while
  262.6 1.9 copy-start.2
  264.5 7.2 %copy-start.6 = (bf16[1,1536,256]{2,1,0:T(8,128)(2,1)S(1)}, bf16[1,1536,256]{2,1,0:T(8,128)(2,1)}, u32[]{:S(2)}) copy-start(bf16[1,1536,256]{2,1,0:T(8,128)(2,1)} %copy-done.4) | copy-start | bytes 2359300 | tf_op jit(solution)/shard_map/while
  265.8 5.9 %copy-start.3 = (bf16[1,512,2048]{2,1,0:T(8,128)(2,1)S(1)}, bf16[1,512,2048]{2,1,0:T(8,128)(2,1)}, u32[]{:S(2)}) copy-start(bf16[1,512,2048]{2,1,0:T(8,128)(2,1)} %copy-done.2) | copy-start | bytes 6291460 | tf_op jit(solution)/shard_map/while
  279.3 0.9 copy-start.4
  286.7 2.0 copy-start
  288.7 1.2 copy-start.5
  288.7 1.8 copy-start.8
  288.7 2.8 copy-start.7
  289.9 5.6 %copy-start.1 = (bf16[1,512,2048]{2,1,0:T(8,128)(2,1)}, bf16[1,512,2048]{2,1,0:T(8,128)(2,1)S(1)}, u32[]{:S(2)}) copy-start(bf16[1,512,2048]{2,1,0:T(8,128)(2,1)S(1)} %fusion.101) | copy-start | bytes 6291460 | tf_op jit(solution)/shard_map/while
  294.0 1.9 copy-start.2
  295.9 7.1 %copy-start.6 = (bf16[1,1536,256]{2,1,0:T(8,128)(2,1)S(1)}, bf16[1,1536,256]{2,1,0:T(8,128)(2,1)}, u32[]{:S(2)}) copy-start(bf16[1,1536,256]{2,1,0:T(8,128)(2,1)} %copy-done.4) | copy-start | bytes 2359300 | tf_op jit(solution)/shard_map/while
  297.2 5.9 %copy-start.3 = (bf16[1,512,2048]{2,1,0:T(8,128)(2,1)S(1)}, bf16[1,512,2048]{2,1,0:T(8,128)(2,1)}, u32[]{:S(2)}) copy-start(bf16[1,512,2048]{2,1,0:T(8,128)(2,1)} %copy-done.2) | copy-start | bytes 6291460 | tf_op jit(solution)/shard_map/while
  311.8 24.9 %all-to-all-start.2 = ((bf16[8,64,512]{2,1,0:T(8,128)(2,1)}), bf16[8,64,512]{2,1,0:T(8,128)(2,1)S(1)}, u32[]{:S(2)}, u32[]{:S(2)}) async-start(bf16[8,64,512]{2,1,0:T(8,128)(2,1)} %all_to_all.36), calls=%async_computation.2 | async-start | bytes 1048576 | tf_op jit(solution)/shard_map/all_to_all | solution.py:214
  336.7 6.4 %copy-start.13 = (bf16[4,1,512,128]{3,2,1,0:T(8,128)(2,1)S(1)}, bf16[4,1,512,128]{3,2,1,0:T(8,128)(2,1)}, u32[]{:S(2)}) copy-start(bf16[4,1,512,128]{3,2,1,0:T(8,128)(2,1)} %get-tuple-element.74) | copy-start | bytes 1572868
  336.7 6.8 %copy-start.14 = (bf16[4,1,512,128]{3,2,1,0:T(8,128)(2,1)S(1)}, bf16[4,1,512,128]{3,2,1,0:T(8,128)(2,1)}, u32[]{:S(2)}) copy-start(bf16[4,1,512,128]{3,2,1,0:T(8,128)(2,1)} %get-tuple-element.75) | copy-start | bytes 1572868
  336.7 7.2 %copy-start.12 = (bf16[4,1,512,128]{3,2,1,0:T(8,128)(2,1)S(1)}, bf16[4,1,512,128]{3,2,1,0:T(8,128)(2,1)}, u32[]{:S(2)}) copy-start(bf16[4,1,512,128]{3,2,1,0:T(8,128)(2,1)} %get-tuple-element.73) | copy-start | bytes 1572868
  336.7 192.1 %all-to-all-start.3 = ((f32[64,1,128,256]{3,2,1,0:T(8,128)}), f32[64,1,128,256]{3,2,1,0:T(8,128)}, u32[]{:S(2)}, u32[]{:S(2)}) async-start(f32[64,1,128,256]{3,2,1,0:T(8,128)} %bitcast.270), calls=%async_computation.3 | async-start | bytes 16777216 | tf_op jit(solution)/shard_map/all_to_all | solution.py:193
where the time goes:
time: 542 us; the launch traced here: 540 us
  waiting for transfers between devices  275 us (51%)
  local copies, waits for them, and re-layouts  82.4 us (15%)
  matrix products  69.4 us (13%)
  blocking collectives  51.5 us (10%)
  starting transfers between devices  31.7 us (6%)
  other arithmetic  29.1 us (5%)
    all_to_all x1, waiting for transfers between devices, on_device(): lax.all_to_all(sending.reshape(owners, capacity, piece_rows, 2 * head_wid...  182 us
    all_to_all x1, waiting for transfers between devices, on_device(): lax.all_to_all(outgoing.reshape(owners, capacity, piece_rows, 2 * head_wi...  90.8 us
    all_gather x1, blocking collectives, on_device(): all_lists = lax.all_gather(selected, 'ctx', axis=1, tiled=True)  51.5 us
    dynamic_update_slice x8, local copies, waits for them, and re-layouts, on_device(): lax.map(one_head, (query_heads, key_heads, value_heads, grad_heads, picked))  23.6 us
    scatter x1, local copies, waits for them, and re-layouts, on_device(): jnp.zeros((slot_count, block_rows, 2 * head_width), jnp.float32).at[slot_of]  11.6 us
    all_to_all x1, starting transfers between devices, on_device(): lax.all_to_all(out_grad, 'head', split_axis=1, concat_axis=0, tiled=True)  10.9 us
  transfers between devices with their start and end apart: 4, of which 3 were waited for; matrix products, arithmetic and copies ran while one was open for 7% of the time, Pallas kernels for 0%

commit v1 on v0

v1 whole, which is shorter than its diff:
```python
import jax
import jax.numpy as jnp
from jax import lax
from jax.experimental import pallas as pl
from jax.experimental.pallas import tpu as pltpu
from jax.sharding import PartitionSpec as P

NT = (((1,), (1,)), ((), ()))
NN = (((1,), (0,)), ((), ()))
VMEM_BYTES = 56 * 1024 * 1024


def dot(a, b, dims):
    return lax.dot_general(a, b, dims, preferred_element_type=jnp.float32)


def document_starts(lens_ref, base_ref, rows):
    position = base_ref[0] + lax.broadcasted_iota(jnp.int32, (1, rows), 1)

    def step(d, carry):
        total, start = carry
        total = total + lens_ref[d]
        return total, jnp.maximum(start, jnp.where(total <= position, total, 0))

    _, start = lax.fori_loop(
        0, lens_ref.shape[0], step, (jnp.int32(0), jnp.zeros((1, rows), jnp.int32))
    )
    return start - base_ref[0]


def masked(scores, start):
    key_at = lax.broadcasted_iota(jnp.int32, scores.shape, 0)
    query_at = lax.broadcasted_iota(jnp.int32, scores.shape, 1)
    return jnp.where((key_at <= query_at) & (key_at >= start), scores, -jnp.inf)


def pack_kernel(codes_ref, context_ref, out_ref):
    width = out_ref.shape[2]

    def step(d, carry):
        column = pl.multiple_of(jnp.maximum(codes_ref[d], 0) * width, width)
        out_ref[d] = context_ref[:, pl.ds(column, width)]
        return carry

    lax.fori_loop(0, out_ref.shape[0], step, 0)


def value_grad_kernel(
    sel_ref, lens_ref, base_ref, q_ref, k_ref, g_ref, far_k_ref,
    near_ref, far_ref, top_ref, inverse_ref, start_ref, scores_ref,
):
    head = pl.program_id(0)
    rows, width = q_ref.shape
    picks = scores_ref.shape[0] - 1
    scale = width ** (-0.5)

    @pl.when(head == 0)
    def _():
        start_ref[...] = document_starts(lens_ref, base_ref, rows)

    q = q_ref[...]
    near = masked(dot(k_ref[...], q, NT), start_ref[...])
    scores_ref[0] = near
    top = jnp.max(near, axis=0, keepdims=True)
    for j in range(picks):
        far = dot(far_k_ref[sel_ref[head * picks + j]], q, NT)
        scores_ref[j + 1] = far
        top = jnp.maximum(top, jnp.max(far, axis=0, keepdims=True))
    total = jnp.zeros((1, rows), jnp.float32)
    for j in range(picks + 1):
        lifted = jnp.exp((scores_ref[j] - top) * scale)
        scores_ref[j] = lifted
        total = total + jnp.sum(lifted, axis=0, keepdims=True)
    inverse = 1.0 / total
    top_ref[0] = top
    inverse_ref[0] = inverse
    g = g_ref[...]
    for j in range(picks + 1):
        low = (scores_ref[j] * inverse).astype(jnp.bfloat16)
        part = dot(low, g, NN).astype(jnp.bfloat16)
        if j == 0:
            near_ref[...] = part
        else:
            far_ref[sel_ref[head * picks + j - 1]] = part


def other_grads_kernel(
    sel_ref, lens_ref, base_ref, q_ref, k_ref, v_ref, g_ref, far_k_ref, far_v_ref, top_ref, inverse_ref,
    attended_ref, query_ref, near_ref, far_ref, start_ref, weights_ref,
):
    head = pl.program_id(0)
    rows, width = q_ref.shape
    picks = weights_ref.shape[0] - 1
    scale = width ** (-0.5)

    @pl.when(head == 0)
    def _():
        start_ref[...] = document_starts(lens_ref, base_ref, rows)

    def keys_of(j):
        return k_ref[...] if j == 0 else far_k_ref[sel_ref[head * picks + j - 1]]

    def values_of(j):
        return v_ref[...] if j == 0 else far_v_ref[sel_ref[head * picks + j - 1]]

    q = q_ref[...]
    g = g_ref[...]
    top = top_ref[0]
    inverse = inverse_ref[0]
    attended = jnp.zeros((width, rows), jnp.float32)
    for j in range(picks + 1):
        scores = dot(keys_of(j), q, NT)
        if j == 0:
            scores = masked(scores, start_ref[...])
        weights = jnp.exp((scores - top) * scale) * inverse
        weights_ref[j] = weights
        attended = attended + dot(values_of(j).T, weights.astype(jnp.bfloat16), NN)
    attended = attended.astype(jnp.bfloat16)
    attended_ref[...] = attended.T
    delta = jnp.sum(
        g.T.astype(jnp.float32) * attended.astype(jnp.float32), axis=0, keepdims=True
    )
    query_grad = jnp.zeros((width, rows), jnp.float32)
    for j in range(picks + 1):
        weight_grads = dot(values_of(j), g, NT)
        score_grads = (weights_ref[j] * (weight_grads - delta) * scale).astype(jnp.bfloat16)
        part = dot(score_grads, q, NN).astype(jnp.bfloat16)
        if j == 0:
            near_ref[...] = part
        else:
            far_ref[sel_ref[head * picks + j - 1]] = part
        query_grad = query_grad + dot(keys_of(j).T, score_grads, NN)
    query_ref[...] = query_grad.astype(jnp.bfloat16).T


def collect_kernel(codes_ref, terms_ref, out_ref, total_ref):
    step_at = pl.program_id(0)
    sources, rows, width = terms_ref.shape
    heads = total_ref.shape[0] - 1

    @pl.when(step_at == 0)
    def _():
        total_ref[...] = jnp.zeros_like(total_ref)

    def step(s, carry):
        code = codes_ref[step_at * sources + s]
        slot = jnp.where(code >= 0, code, heads)
        total_ref[slot] += terms_ref[s].astype(jnp.float32)
        return carry

    lax.fori_loop(0, sources, step, 0)

    @pl.when(step_at == pl.num_programs(0) - 1)
    def _():
        for h in range(heads):
            out_ref[:, h * width : (h + 1) * width] = total_ref[h].astype(out_ref.dtype)


def pack(codes, context, owners, width):
    rows = context.shape[0]
    return pl.pallas_call(
        pack_kernel,
        out_shape=jax.ShapeDtypeStruct((owners, rows, width), context.dtype),
        grid_spec=pltpu.PrefetchScalarGridSpec(
            num_scalar_prefetch=1,
            grid=(1,),
            in_specs=[pl.BlockSpec(context.shape, lambda i, *_: (0, 0))],
            out_specs=pl.BlockSpec((owners, rows, width), lambda i, *_: (0, 0, 0)),
        ),
        compiler_params=pltpu.CompilerParams(vmem_limit_bytes=VMEM_BYTES),
    )(codes, context)


def collect(codes, terms, heads):
    owners, rows, width = terms.shape
    steps = 4
    return pl.pallas_call(
        collect_kernel,
        out_shape=jax.ShapeDtypeStruct((rows, heads * width), terms.dtype),
        grid_spec=pltpu.PrefetchScalarGridSpec(
            num_scalar_prefetch=1,
            grid=(steps,),
            in_specs=[pl.BlockSpec((owners // steps, rows, width), lambda i, *_: (i, 0, 0))],
            out_specs=pl.BlockSpec((rows, heads * width), lambda i, *_: (0, 0)),
            scratch_shapes=[pltpu.VMEM((heads + 1, rows, width), jnp.float32)],
        ),
        compiler_params=pltpu.CompilerParams(vmem_limit_bytes=VMEM_BYTES),
    )(codes, terms)


def on_device(queries, keys, values, out_grad, context_keys, context_values, selected, doc_lengths):
    heads, _, picks = selected.shape
    rows = queries.shape[0]
    width = queries.shape[1] // heads
    piece_rows = context_keys.shape[0]
    pieces = rows // piece_rows
    owners = lax.axis_size("ctx")
    blocks = owners // pieces
    base = (lax.axis_index("ctx") * rows).astype(jnp.int32).reshape(1)
    flat = selected.reshape(-1)

    head_of = jnp.arange(heads * picks, dtype=jnp.int32) // picks
    hits = flat[None, :] == jnp.arange(blocks, dtype=jnp.int32)[:, None]
    wanted = jnp.max(jnp.where(hits, head_of[None, :], -1), axis=1)
    wanted = jnp.broadcast_to(wanted[:, None, None], (blocks, pieces, 128)).reshape(owners, 128)
    codes = lax.all_to_all(wanted, "ctx", split_axis=0, concat_axis=0, tiled=True)[:, 0]

    def exchange(tiles):
        return lax.all_to_all(tiles, "ctx", split_axis=0, concat_axis=0, tiled=True)

    far_keys = exchange(pack(codes, context_keys, owners, width)).reshape(blocks, rows, width)
    far_values = exchange(pack(codes, context_values, owners, width)).reshape(blocks, rows, width)
    grads = lax.all_to_all(out_grad, "head", split_axis=1, concat_axis=0, tiled=True)

    by_head = pl.BlockSpec((rows, width), lambda h, *_: (0, h))
    all_far = pl.BlockSpec((blocks, rows, width), lambda h, *_: (0, 0, 0))
    by_stat = pl.BlockSpec((1, 1, rows), lambda h, *_: (h, 0, 0))
    near_shape = jax.ShapeDtypeStruct(queries.shape, jnp.bfloat16)
    far_shape = jax.ShapeDtypeStruct((blocks, rows, width), jnp.bfloat16)
    stat_shape = jax.ShapeDtypeStruct((heads, 1, rows), jnp.float32)
    scratch = [pltpu.VMEM((1, rows), jnp.int32), pltpu.VMEM((picks + 1, rows, rows), jnp.float32)]
    tile_flops = 2 * rows * rows * width * (picks + 1) * heads
    value_grad, far_value_grads, top, inverse = pl.pallas_call(
        value_grad_kernel,
        out_shape=(near_shape, far_shape, stat_shape, stat_shape),
        grid_spec=pltpu.PrefetchScalarGridSpec(
            num_scalar_prefetch=3,
            grid=(heads,),
            in_specs=[by_head, by_head, by_head, all_far],
            out_specs=[by_head, all_far, by_stat, by_stat],
            scratch_shapes=scratch,
        ),
        compiler_params=pltpu.CompilerParams(vmem_limit_bytes=VMEM_BYTES),
        cost_estimate=pl.CostEstimate(
            flops=2 * tile_flops, bytes_accessed=8 << 20, transcendentals=heads * 4 * rows * rows
        ),
    )(flat, doc_lengths, base, queries, keys, grads, far_keys)
    value_terms = exchange(far_value_grads.reshape(owners, piece_rows, width))

    attended, query_grad, key_grad, far_key_grads = pl.pallas_call(
        other_grads_kernel,
        out_shape=(near_shape, near_shape, near_shape, far_shape),
        grid_spec=pltpu.PrefetchScalarGridSpec(
            num_scalar_prefetch=3,
            grid=(heads,),
            in_specs=[by_head, by_head, by_head, by_head, all_far, all_far, by_stat, by_stat],
            out_specs=[by_head, by_head, by_head, all_far],
            scratch_shapes=scratch,
        ),
        compiler_params=pltpu.CompilerParams(vmem_limit_bytes=VMEM_BYTES),
        cost_estimate=pl.CostEstimate(
            flops=5 * tile_flops, bytes_accessed=8 << 20, transcendentals=heads * 4 * rows * rows
        ),
    )(flat, doc_lengths, base, queries, keys, values, grads, far_keys, far_values, top, inverse)
    key_terms = exchange(far_key_grads.reshape(owners, piece_rows, width))

    output_rows = lax.all_to_all(attended, "head", split_axis=0, concat_axis=1, tiled=True)
    context_value_grad = collect(codes, value_terms, heads)
    context_key_grad = collect(codes, key_terms, heads)
    return output_rows, query_grad, key_grad, value_grad, context_key_grad, context_value_grad


def solution(mesh):
    split = P("ctx", "head")
    rows = P(("ctx", "head"), None)
    return jax.shard_map(
        on_device,
        mesh=mesh,
        in_specs=(split, split, split, rows, split, split, P("head", "ctx", None), P()),
        out_specs=(rows, split, split, split, split, split),
        check_vma=False,
    )
```

time: 542 us -> 325 us (0.60)
  waiting for transfers between devices: 275 us -> 153 us
  local copies, waits for them, and re-layouts: 82.4 us -> 7.32 us
  matrix products: 69.4 us -> 0 us
  Pallas kernels: 0 us -> 46.9 us
  other arithmetic: 29.1 us -> 0.13 us
  blocking collectives: 51.5 us -> 78.4 us
  starting transfers between devices: 31.7 us -> 38.1 us
    all_to_all x3 -> x4, waiting for transfers between devices: 275 us -> 139 us  [the longest x3 132 us: exchange(): return lax.all_to_all(tiles, 'ctx', split_axis=0, concat_axis=0, tiled=True)]
    all_to_all x0 -> x2, blocking collectives: none -> 78.4 us  [the longest x1 57.1 us: exchange(): return lax.all_to_all(tiles, 'ctx', split_axis=0, concat_axis=0, tiled=True)]
    dot_general x49 -> x0, matrix products: 69.4 us -> none  [the longest x1 10.4 us: accumulate(): jnp.einsum('sh,sxc->hxc', onehot, buffers, precision=lax.Precision.HIGHEST)]
    all_gather x1 -> x0, blocking collectives: 51.5 us -> none  [on_device(): all_lists = lax.all_gather(selected, 'ctx', axis=1, tiled=True)]
    pallas_call x0 -> x6, Pallas kernels: none -> 46.9 us  [the longest x1 17.9 us: on_device(): pl.pallas_call(other_grads_kernel, out_shape=(near_shape, near_shape, nea...]
    dynamic_update_slice x8 -> x0, local copies, waits for them, and re-layouts: 23.6 us -> none  [on_device(): lax.map(one_head, (query_heads, key_heads, value_heads, grad_heads, picked))]
    all_to_all x1, waiting for transfers between devices: 0.01 us -> 13.4 us  [on_device(): lax.all_to_all(out_grad, 'head', split_axis=1, concat_axis=0, tiled=True)]
    scatter x1 -> x0, local copies, waits for them, and re-layouts: 11.6 us -> none  [on_device(): jnp.zeros((slot_count, block_rows, 2 * head_width), jnp.float32).at[slot_of]]
  transfers between devices with their start and end apart: 4 -> 5, of which waited for: 3 -> 5; matrix products, arithmetic and copies ran while one was open for 7% -> 1% of each run, Pallas kernels for 0% -> 8%
where the time goes in v1:
time: 325 us; the launch traced here: 324 us
  waiting for transfers between devices  153 us (47%)
  blocking collectives  78.4 us (24%)
  Pallas kernels  46.9 us (14%)
  starting transfers between devices  38.1 us (12%)
  local copies, waits for them, and re-layouts  7.32 us (2%)
    all_to_all x3, waiting for transfers between devices, exchange(): return lax.all_to_all(tiles, 'ctx', split_axis=0, concat_axis=0, tiled=True)  132 us
    all_to_all x1, blocking collectives, exchange(): return lax.all_to_all(tiles, 'ctx', split_axis=0, concat_axis=0, tiled=True)  57.1 us
    all_to_all x1, blocking collectives, on_device(): lax.all_to_all(attended, 'head', split_axis=0, concat_axis=1, tiled=True)  21.3 us
    pallas_call x1, Pallas kernels, on_device(): pl.pallas_call(other_grads_kernel, out_shape=(near_shape, near_shape, nea...  17.9 us
    all_to_all x3, starting transfers between devices, exchange(): return lax.all_to_all(tiles, 'ctx', split_axis=0, concat_axis=0, tiled=True)  16.4 us
    all_to_all x1, waiting for transfers between devices, on_device(): lax.all_to_all(out_grad, 'head', split_axis=1, concat_axis=0, tiled=True)  13.4 us
    pallas_call x1, Pallas kernels, on_device(): pl.pallas_call(value_grad_kernel, out_shape=(near_shape, far_shape, stat_...  12.9 us
    all_to_all x1, starting transfers between devices, on_device(): lax.all_to_all(wanted, 'ctx', split_axis=0, concat_axis=0, tiled=True)[:, 0]  11.6 us
  transfers between devices with their start and end apart: 5, of which 5 were waited for; matrix products, arithmetic and copies ran while one was open for 1% of the time, Pallas kernels for 8%

profile of v1, /device:TPU:1, one launch (start us, length us, event | category | flops | bytes accessed | tf_op | source)
XLA Modules:
  0.0 324.2 jit_solution(6905636446958180081)
XLA Ops:
  0.6 0.8 copy.26
  1.4 0.1 reshape.60.sel_ref
  1.5 0.0 copy-start.3
  1.5 0.1 select_reduce_fusion
  1.6 0.1 broadcast_in_dim.26
  1.7 0.1 broadcast_in_dim.27
  1.8 0.8 broadcast_in_dim.28
  2.5 11.6 %all-to-all-start.1 = ((s32[64,1,128]{2,1,0:T(1,128)}), s32[64,1,128]{2,1,0:T(1,128)S(1)}, u32[]{:S(2)}, u32[]{:S(2)}) async-start(s32[64,1,128]{2,1,0:T(1,128)} %broadcast_in_dim.28), calls=%async_computation.1 | async-start | bytes 65536 | tf_op jit(solution)/shard_map/all_to_all | solution.py:206
  14.2 1.9 copy.32
  16.1 7.3 %all-to-all-done.1 = s32[64,1,128]{2,1,0:T(1,128)S(1)} async-done(((s32[64,1,128]{2,1,0:T(1,128)}), s32[64,1,128]{2,1,0:T(1,128)S(1)}, u32[]{:S(2)}, u32[]{:S(2)}) %all-to-all-start.1) | async-done | bytes 32800 | tf_op jit(solution)/shard_map/all_to_all | solution.py:206
  23.4 10.0 %all-to-all-start = ((bf16[64,8,512]{2,0,1:T(8,128)(2,1)}), bf16[64,8,512]{2,0,1:T(8,128)(2,1)S(1)}, u32[]{:S(2)}, u32[]{:S(2)}) async-start(bf16[64,8,512]{2,0,1:T(8,128)(2,1)} %bitcast.18), calls=%async_computation | async-start | bytes 1048576 | tf_op jit(solution)/shard_map/all_to_all | solution.py:213
  33.4 0.7 slice_reduce_fusion.codes_ref
  34.1 3.9 %shard_map.127 = bf16[64,128,128]{2,1,0:T(8,128)(2,1)} custom-call(s32[64]{0:T(128)} %slice_reduce_fusion.codes_ref, bf16[128,512]{1,0:T(8,128)(2,1)} %context_ref.2), custom_call_target="tpu_custom_call" | custom-call | tf_op jit(solution)/shard_map/pallas_call | solution.py:161
  38.0 0.0 copy-done.3
  38.0 13.4 %all-to-all-done = bf16[64,8,512]{2,0,1:T(8,128)(2,1)S(1)} async-done(((bf16[64,8,512]{2,0,1:T(8,128)(2,1)}), bf16[64,8,512]{2,0,1:T(8,128)(2,1)S(1)}, u32[]{:S(2)}, u32[]{:S(2)}) %all-to-all-start) | async-done | bytes 524320 | tf_op jit(solution)/shard_map/all_to_all | solution.py:213
  51.4 0.0 copy-start.2
  51.4 0.8 copy-done.2
  52.2 4.6 %all-to-all-start.2 = ((bf16[64,128,128]{2,1,0:T(8,128)(2,1)}), bf16[64,128,128]{2,1,0:T(8,128)(2,1)S(1)}, u32[]{:S(2)}, u32[]{:S(2)}) async-start(bf16[64,128,128]{2,1,0:T(8,128)(2,1)} %shard_map.127), calls=%async_computation.2 | async-start | bytes 4194304 | tf_op jit(solution)/shard_map/all_to_all | solution.py:209
  56.8 3.9 %shard_map.128 = bf16[64,128,128]{2,1,0:T(8,128)(2,1)} custom-call(s32[64]{0:T(128)} %slice_reduce_fusion.codes_ref, bf16[128,512]{1,0:T(8,128)(2,1)} %context_ref.3), custom_call_target="tpu_custom_call" | custom-call | tf_op jit(solution)/shard_map/pallas_call | solution.py:161
  60.7 47.5 %all-to-all-done.2 = bf16[64,128,128]{2,1,0:T(8,128)(2,1)S(1)} async-done(((bf16[64,128,128]{2,1,0:T(8,128)(2,1)}), bf16[64,128,128]{2,1,0:T(8,128)(2,1)S(1)}, u32[]{:S(2)}, u32[]{:S(2)}) %all-to-all-start.2) | async-done | bytes 2097184 | tf_op jit(solution)/shard_map/all_to_all | solution.py:209
  108.2 0.0 copy-start.1
  108.2 6.0 %all-to-all-start.3 = ((bf16[64,128,128]{2,1,0:T(8,128)(2,1)}), bf16[64,128,128]{2,1,0:T(8,128)(2,1)}, u32[]{:S(2)}, u32[]{:S(2)}) async-start(bf16[64,128,128]{2,1,0:T(8,128)(2,1)} %shard_map.128), calls=%async_computation.3 | async-start | bytes 4194304 | tf_op jit(solution)/shard_map/all_to_all | solution.py:209
  114.2 0.0 copy-done.1
  114.2 12.9 %shard_map.129 = (bf16[512,512]{1,0:T(8,128)(2,1)}, bf16[16,512,128]{2,1,0:T(8,128)(2,1)}, f32[4,1,512]{2,1,0:T(1,128)}, f32[4,1,512]{2,1,0:T(1,128)}) custom-call(s32[12]{0:T(128)} %copy-done.3, s32[64]{0:T(128)} %lens_ref.3, s32[1]{0:T(128)} %bitcast.base_ref, bf16[512,512]{1,0:T(8,128)(2,1)} %q_ref.3, bf16[512,512]{1,0:T(8,128)(2,1)} %k_ref.3, ...), custom_call_target="tpu_custom_call" | custom-call | flops 2147483648 | bytes 8388608 | tf_op jit(solution)/shard_map/pallas_call | solution.py:223
  127.1 38.2 %all-to-all-done.3 = bf16[64,128,128]{2,1,0:T(8,128)(2,1)} async-done(((bf16[64,128,128]{2,1,0:T(8,128)(2,1)}), bf16[64,128,128]{2,1,0:T(8,128)(2,1)}, u32[]{:S(2)}, u32[]{:S(2)}) %all-to-all-start.3) | async-done | bytes 2097184 | tf_op jit(solution)/shard_map/all_to_all | solution.py:209
  165.3 17.9 %shard_map.130 = (bf16[512,512]{1,0:T(8,128)(2,1)}, bf16[512,512]{1,0:T(8,128)(2,1)}, bf16[512,512]{1,0:T(8,128)(2,1)}, bf16[16,512,128]{2,1,0:T(8,128)(2,1)}) custom-call(s32[12]{0:T(128)} %copy-done.3, s32[64]{0:T(128)} %lens_ref.3, s32[1]{0:T(128)} %bitcast.base_ref, bf16[512,512]{1,0:T(8,128)(2,1)} %q_ref.3, bf16[512,512]{1,0:T(8,128)(2,1)} %k_ref.3, ...), custom_call_target="tpu_custom_call" | custom-call | flops 5368709120 | bytes 8388608 | tf_op jit(solution)/shard_map/pallas_call | solution.py:240
  183.3 21.3 %all_to_all.67 = bf16[8,64,512]{2,1,0:T(8,128)(2,1)S(1)} all-to-all(bf16[8,64,512]{2,1,0:T(8,128)(2,1)} %bitcast.28), channel_id=1, replica_groups=mesh['ctx'=64,'head'=8] {'head'}, dimensions={0} | all-to-all | bytes 1048576 | tf_op jit(solution)/shard_map/all_to_all | solution.py:257
  204.6 57.1 %all_to_all.68.terms_ref = bf16[64,128,128]{2,1,0:T(8,128)(2,1)} all-to-all(bf16[64,128,128]{2,1,0:T(8,128)(2,1)} %bitcast.22), channel_id=1, replica_groups=mesh['ctx'=64,'head'=8] {'ctx'}, dimensions={0} | all-to-all | bytes 4194304 | tf_op jit(solution)/shard_map/all_to_all | solution.py:209
  261.7 5.8 %all-to-all-start.6 = ((bf16[64,128,128]{2,1,0:T(8,128)(2,1)}), bf16[64,128,128]{2,1,0:T(8,128)(2,1)S(1)}, u32[]{:S(2)}, u32[]{:S(2)}) async-start(bf16[64,128,128]{2,1,0:T(8,128)(2,1)} %bitcast.21), calls=%async_computation.6 | async-start | bytes 4194304 | tf_op jit(solution)/shard_map/all_to_all | solution.py:209
  267.5 0.8 copy.30
  268.4 4.1 %shard_map.131 = bf16[128,512]{1,0:T(8,128)(2,1)} custom-call(s32[64]{0:T(128)} %slice_reduce_fusion.codes_ref, bf16[64,128,128]{2,1,0:T(8,128)(2,1)} %all_to_all.68.terms_ref), custom_call_target="tpu_custom_call" | custom-call | tf_op jit(solution)/shard_map/pallas_call | solution.py:177
  272.5 46.3 %all-to-all-done.6.terms_ref = bf16[64,128,128]{2,1,0:T(8,128)(2,1)S(1)} async-done(((bf16[64,128,128]{2,1,0:T(8,128)(2,1)}), bf16[64,128,128]{2,1,0:T(8,128)(2,1)S(1)}, u32[]{:S(2)}, u32[]{:S(2)}) %all-to-all-start.6) | async-done | bytes 2097184 | tf_op jit(solution)/shard_map/all_to_all | solution.py:209
  318.8 0.0 copy-start
  318.8 1.3 copy-done
  320.1 4.1 %shard_map.132 = bf16[128,512]{1,0:T(8,128)(2,1)} custom-call(s32[64]{0:T(128)} %slice_reduce_fusion.codes_ref, bf16[64,128,128]{2,1,0:T(8,128)(2,1)} %copy-done), custom_call_target="tpu_custom_call" | custom-call | tf_op jit(solution)/shard_map/pallas_call | solution.py:177
  (1 shorter events, 0.0 us)
Async XLA Ops:
  1.5 36.5 %copy-start.3 = (s32[12]{0:T(128)}, s32[12]{0:T(128)S(1)}, u32[]{:S(2)}) copy-start(s32[12]{0:T(128)S(1)} %reshape.60.sel_ref) | copy-start | bytes 148
  2.5 20.8 %all-to-all-start.1 = ((s32[64,1,128]{2,1,0:T(1,128)}), s32[64,1,128]{2,1,0:T(1,128)S(1)}, u32[]{:S(2)}, u32[]{:S(2)}) async-start(s32[64,1,128]{2,1,0:T(1,128)} %broadcast_in_dim.28), calls=%async_computation.1 | async-start | bytes 65536 | tf_op jit(solution)/shard_map/all_to_all | solution.py:206
  23.4 28.0 %all-to-all-start = ((bf16[64,8,512]{2,0,1:T(8,128)(2,1)}), bf16[64,8,512]{2,0,1:T(8,128)(2,1)S(1)}, u32[]{:S(2)}, u32[]{:S(2)}) async-start(bf16[64,8,512]{2,0,1:T(8,128)(2,1)} %bitcast.18), calls=%async_computation | async-start | bytes 1048576 | tf_op jit(solution)/shard_map/all_to_all | solution.py:213
  51.4 0.8 copy-start.2
  52.2 56.0 %all-to-all-start.2 = ((bf16[64,128,128]{2,1,0:T(8,128)(2,1)}), bf16[64,128,128]{2,1,0:T(8,128)(2,1)S(1)}, u32[]{:S(2)}, u32[]{:S(2)}) async-start(bf16[64,128,128]{2,1,0:T(8,128)(2,1)} %shard_map.127), calls=%async_computation.2 | async-start | bytes 4194304 | tf_op jit(solution)/shard_map/all_to_all | solution.py:209
  108.2 6.0 %copy-start.1 = (bf16[64,128,128]{2,1,0:T(8,128)(2,1)}, bf16[64,128,128]{2,1,0:T(8,128)(2,1)S(1)}, u32[]{:S(2)}) copy-start(bf16[64,128,128]{2,1,0:T(8,128)(2,1)S(1)} %all-to-all-done.2) | copy-start | bytes 6291460
  108.2 57.2 %all-to-all-start.3 = ((bf16[64,128,128]{2,1,0:T(8,128)(2,1)}), bf16[64,128,128]{2,1,0:T(8,128)(2,1)}, u32[]{:S(2)}, u32[]{:S(2)}) async-start(bf16[64,128,128]{2,1,0:T(8,128)(2,1)} %shard_map.128), calls=%async_computation.3 | async-start | bytes 4194304 | tf_op jit(solution)/shard_map/all_to_all | solution.py:209
  261.7 57.1 %all-to-all-start.6 = ((bf16[64,128,128]{2,1,0:T(8,128)(2,1)}), bf16[64,128,128]{2,1,0:T(8,128)(2,1)S(1)}, u32[]{:S(2)}, u32[]{:S(2)}) async-start(bf16[64,128,128]{2,1,0:T(8,128)(2,1)} %bitcast.21), calls=%async_computation.6 | async-start | bytes 4194304 | tf_op jit(solution)/shard_map/all_to_all | solution.py:209
  318.8 1.3 copy-start

commit v2 on v1

--- a/solution.py
+++ b/solution.py
@@ -35,20 +35,43 @@
 
 
 def pack_kernel(codes_ref, context_ref, out_ref):
-    width = out_ref.shape[2]
+    count, _, width = out_ref.shape
+    first = pl.program_id(0) * count
 
     def step(d, carry):
-        column = pl.multiple_of(jnp.maximum(codes_ref[d], 0) * width, width)
+        column = pl.multiple_of(jnp.maximum(codes_ref[first + d], 0) * width, width)
         out_ref[d] = context_ref[:, pl.ds(column, width)]
         return carry
 
-    lax.fori_loop(0, out_ref.shape[0], step, 0)
+    lax.fori_loop(0, count, step, 0, unroll=4)
+
+
+def in_token_order(me, shares, out_ref):
+    count = len(shares)
+    rows = shares[0].shape[0]
+    for distance, share in enumerate(shares):
+        source = lax.rem(me + count - distance, count)
+        out_ref[pl.ds(pl.multiple_of(source * rows, rows), rows), :] = share[...]
+
+
+def assemble_kernel(me_ref, *refs):
+    *shares, out_ref = refs
+    count = len(shares)
+    width = shares[0].shape[1]
+    for distance, share in enumerate(shares):
+        source = lax.rem(me_ref[0] + count - distance, count)
+        out_ref[:, pl.ds(pl.multiple_of(source * width, width), width)] = share[...]
+
+
+def gate_kernel(kept_ref, after_ref, out_ref):
+    pass
 
 
 def value_grad_kernel(
-    sel_ref, lens_ref, base_ref, q_ref, k_ref, g_ref, far_k_ref,
-    near_ref, far_ref, top_ref, inverse_ref, start_ref, scores_ref,
+    sel_ref, lens_ref, base_ref, q_ref, k_ref, k1_ref, k2_ref, k3_ref, *refs,
 ):
+    *shares, near_ref, far_ref, top_ref, inverse_ref, start_ref, scores_ref, g_ref = refs
+    far_k = (k1_ref, k2_ref, k3_ref)
     head = pl.program_id(0)
     rows, width = q_ref.shape
     picks = scores_ref.shape[0] - 1
@@ -63,7 +86,7 @@
     scores_ref[0] = near
     top = jnp.max(near, axis=0, keepdims=True)
     for j in range(picks):
-        far = dot(far_k_ref[sel_ref[head * picks + j]], q, NT)
+        far = dot(far_k[j][...], q, NT)
         scores_ref[j + 1] = far
         top = jnp.maximum(top, jnp.max(far, axis=0, keepdims=True))
     total = jnp.zeros((1, rows), jnp.float32)
@@ -74,6 +97,7 @@
     inverse = 1.0 / total
     top_ref[0] = top
     inverse_ref[0] = inverse
+    in_token_order(base_ref[1], shares, g_ref)
     g = g_ref[...]
     for j in range(picks + 1):
         low = (scores_ref[j] * inverse).astype(jnp.bfloat16)
@@ -85,9 +109,11 @@
 
 
 def other_grads_kernel(
-    sel_ref, lens_ref, base_ref, q_ref, k_ref, v_ref, g_ref, far_k_ref, far_v_ref, top_ref, inverse_ref,
-    attended_ref, query_ref, near_ref, far_ref, start_ref, weights_ref,
+    sel_ref, lens_ref, base_ref, q_ref, k_ref, v_ref,
+    k1_ref, k2_ref, k3_ref, v1_ref, v2_ref, v3_ref, top_ref, inverse_ref, *refs,
 ):
+    *shares, attended_ref, query_ref, near_ref, far_ref, start_ref, weights_ref, g_ref = refs
+    far_k, far_v = (k1_ref, k2_ref, k3_ref), (v1_ref, v2_ref, v3_ref)
     head = pl.program_id(0)
     rows, width = q_ref.shape
     picks = weights_ref.shape[0] - 1
@@ -98,11 +124,12 @@
         start_ref[...] = document_starts(lens_ref, base_ref, rows)
 
     def keys_of(j):
-        return k_ref[...] if j == 0 else far_k_ref[sel_ref[head * picks + j - 1]]
+        return k_ref[...] if j == 0 else far_k[j - 1][...]
 
     def values_of(j):
-        return v_ref[...] if j == 0 else far_v_ref[sel_ref[head * picks + j - 1]]
-
+        return v_ref[...] if j == 0 else far_v[j - 1][0]
+
+    in_token_order(base_ref[1], shares, g_ref)
     q = q_ref[...]
     g = g_ref[...]
     top = top_ref[0]
@@ -158,14 +185,15 @@
 
 def pack(codes, context, owners, width):
     rows = context.shape[0]
+    steps = 4
     return pl.pallas_call(
         pack_kernel,
         out_shape=jax.ShapeDtypeStruct((owners, rows, width), context.dtype),
         grid_spec=pltpu.PrefetchScalarGridSpec(
             num_scalar_prefetch=1,
-            grid=(1,),
+            grid=(steps,),
             in_specs=[pl.BlockSpec(context.shape, lambda i, *_: (0, 0))],
-            out_specs=pl.BlockSpec((owners, rows, width), lambda i, *_: (0, 0, 0)),
+            out_specs=pl.BlockSpec((owners // steps, rows, width), lambda i, *_: (i, 0, 0)),
         ),
         compiler_params=pltpu.CompilerParams(vmem_limit_bytes=VMEM_BYTES),
     )(codes, context)
@@ -188,6 +216,23 @@
     )(codes, terms)
 
 
+def shifted(parts, count):
+    return [parts[0]] + [
+        lax.ppermute(parts[d], "head", [(i, (i + d) % count) for i in range(count)])
+        for d in range(1, count)
+    ]
+
+
+def gate(kept, after):
+    return pl.pallas_call(
+        gate_kernel,
+        out_shape=jax.ShapeDtypeStruct(kept.shape, kept.dtype),
+        in_specs=[pl.BlockSpec(memory_space=pl.ANY)] * 2,
+        out_specs=pl.BlockSpec(memory_space=pl.ANY),
+        input_output_aliases={0: 0},
+    )(kept, after)
+
+
 def on_device(queries, keys, values, out_grad, context_keys, context_values, selected, doc_lengths):
     heads, _, picks = selected.shape
     rows = queries.shape[0]
@@ -196,7 +241,20 @@
     pieces = rows // piece_rows
     owners = lax.axis_size("ctx")
     blocks = owners // pieces
-    base = (lax.axis_index("ctx") * rows).astype(jnp.int32).reshape(1)
+    gathered_keys = lax.all_gather(context_keys, "ctx", axis=0, tiled=True)
+    count = lax.axis_size("head")
+    me = lax.axis_index("head").astype(jnp.int32)
+    share_rows = rows // count
+    grads = shifted(
+        [
+            lax.dynamic_slice_in_dim(
+                out_grad, lax.rem(me + d, count) * heads * width, heads * width, 1
+            )
+            for d in range(count)
+        ],
+        count,
+    )
+    base = jnp.stack([lax.axis_index("ctx").astype(jnp.int32) * rows, me])
     flat = selected.reshape(-1)
 
     head_of = jnp.arange(heads * picks, dtype=jnp.int32) // picks
@@ -208,17 +266,28 @@
     def exchange(tiles):
         return lax.all_to_all(tiles, "ctx", split_axis=0, concat_axis=0, tiled=True)
 
-    far_keys = exchange(pack(codes, context_keys, owners, width)).reshape(blocks, rows, width)
     far_values = exchange(pack(codes, context_values, owners, width)).reshape(blocks, rows, width)
-    grads = lax.all_to_all(out_grad, "head", split_axis=1, concat_axis=0, tiled=True)
 
     by_head = pl.BlockSpec((rows, width), lambda h, *_: (0, h))
     all_far = pl.BlockSpec((blocks, rows, width), lambda h, *_: (0, 0, 0))
+    far_key = [
+        pl.BlockSpec((rows, width), lambda h, sel, *_, j=j: (sel[h * picks + j], h))
+        for j in range(picks)
+    ]
+    far_value = [
+        pl.BlockSpec((1, rows, width), lambda h, sel, *_, j=j: (sel[h * picks + j], 0, 0))
+        for j in range(picks)
+    ]
+    shares = [pl.BlockSpec((share_rows, width), lambda h, *_: (0, h))] * count
     by_stat = pl.BlockSpec((1, 1, rows), lambda h, *_: (h, 0, 0))
     near_shape = jax.ShapeDtypeStruct(queries.shape, jnp.bfloat16)
     far_shape = jax.ShapeDtypeStruct((blocks, rows, width), jnp.bfloat16)
     stat_shape = jax.ShapeDtypeStruct((heads, 1, rows), jnp.float32)
-    scratch = [pltpu.VMEM((1, rows), jnp.int32), pltpu.VMEM((picks + 1, rows, rows), jnp.float32)]
+    scratch = [
+        pltpu.VMEM((1, rows), jnp.int32),
+        pltpu.VMEM((picks + 1, rows, rows), jnp.float32),
+        pltpu.VMEM((rows, width), jnp.bfloat16),
+    ]
     tile_flops = 2 * rows * rows * width * (picks + 1) * heads
     value_grad, far_value_grads, top, inverse = pl.pallas_call(
         value_grad_kernel,
@@ -226,7 +295,7 @@
         grid_spec=pltpu.PrefetchScalarGridSpec(
             num_scalar_prefetch=3,
             grid=(heads,),
-            in_specs=[by_head, by_head, by_head, all_far],
+            in_specs=[by_head, by_head, *far_key, *shares],
             out_specs=[by_head, all_far, by_stat, by_stat],
             scratch_shapes=scratch,
         ),
@@ -234,7 +303,7 @@
         cost_estimate=pl.CostEstimate(
             flops=2 * tile_flops, bytes_accessed=8 << 20, transcendentals=heads * 4 * rows * rows
         ),
-    )(flat, doc_lengths, base, queries, keys, grads, far_keys)
+    )(flat, doc_lengths, base, queries, keys, *[gathered_keys] * picks, *grads)
     value_terms = exchange(far_value_grads.reshape(owners, piece_rows, width))
 
     attended, query_grad, key_grad, far_key_grads = pl.pallas_call(
@@ -243,7 +312,7 @@
         grid_spec=pltpu.PrefetchScalarGridSpec(
             num_scalar_prefetch=3,
             grid=(heads,),
-            in_specs=[by_head, by_head, by_head, by_head, all_far, all_far, by_stat, by_stat],
+            in_specs=[by_head, by_head, by_head, *far_key, *far_value, by_stat, by_stat, *shares],
             out_specs=[by_head, by_head, by_head, all_far],
             scratch_shapes=scratch,
         ),
@@ -251,10 +320,26 @@
         cost_estimate=pl.CostEstimate(
             flops=5 * tile_flops, bytes_accessed=8 << 20, transcendentals=heads * 4 * rows * rows
         ),
-    )(flat, doc_lengths, base, queries, keys, values, grads, far_keys, far_values, top, inverse)
-    key_terms = exchange(far_key_grads.reshape(owners, piece_rows, width))
-
-    output_rows = lax.all_to_all(attended, "head", split_axis=0, concat_axis=1, tiled=True)
+    )(
+        flat, doc_lengths, base, queries, keys, values,
+        *[gathered_keys] * picks, *[far_values] * picks, top, inverse, *grads,
+    )
+    key_terms = exchange(gate(far_key_grads.reshape(owners, piece_rows, width), value_terms))
+
+    output_parts = shifted(
+        [
+            lax.dynamic_slice_in_dim(attended, lax.rem(me + d, count) * share_rows, share_rows, 0)
+            for d in range(count)
+        ],
+        count,
+    )
+    output_rows = pl.pallas_call(
+        assemble_kernel,
+        out_shape=jax.ShapeDtypeStruct((share_rows, count * heads * width), jnp.bfloat16),
+        in_specs=[pl.BlockSpec(memory_space=pltpu.SMEM)]
+        + [pl.BlockSpec(memory_space=pltpu.VMEM)] * count,
+        out_specs=pl.BlockSpec(memory_space=pltpu.VMEM),
+    )(me.reshape(1), *output_parts)
     context_value_grad = collect(codes, value_terms, heads)
     context_key_grad = collect(codes, key_terms, heads)
     return output_rows, query_grad, key_grad, value_grad, context_key_grad, context_value_grad

time: 325 us -> 261 us (0.80)
  waiting for transfers between devices: 153 us -> 94.1 us
  blocking collectives: 78.4 us -> 20.7 us
  starting transfers between devices: 38.1 us -> 79.4 us
  between operations: 0.7 us -> 14.6 us
  Pallas kernels: 46.9 us -> 43.5 us
    all_to_all x3, waiting for transfers between devices: 132 us -> 43.5 us  [exchange(): return lax.all_to_all(tiles, 'ctx', split_axis=0, concat_axis=0, tiled=True)]
    ppermute x0 -> x14, starting transfers between devices: none -> 61.3 us  [shifted(): lax.ppermute(parts[d], 'head', [(i, (i + d) % count) for i in range(count)])]
    all_to_all x2 -> x1, blocking collectives: 78.4 us -> 20.7 us  [on_device(): lax.all_to_all(wanted, 'ctx', split_axis=0, concat_axis=0, tiled=True)[:, 0]]
    all_gather x0 -> x1, waiting for transfers between devices: none -> 43.1 us  [on_device(): gathered_keys = lax.all_gather(context_keys, 'ctx', axis=0, tiled=True)]
    all_to_all x2 -> x0, starting transfers between devices: 21.7 us -> none  [the longest x1 11.6 us: on_device(): lax.all_to_all(wanted, 'ctx', split_axis=0, concat_axis=0, tiled=True)[:, 0]]
    all_to_all x2 -> x0, waiting for transfers between devices: 20.7 us -> none  [the longest x1 13.4 us: on_device(): lax.all_to_all(out_grad, 'head', split_axis=1, concat_axis=0, tiled=True)]
    ppermute x0 -> x14, waiting for transfers between devices: none -> 6.8 us  [shifted(): lax.ppermute(parts[d], 'head', [(i, (i + d) % count) for i in range(count)])]
    pallas_call x2 -> x1, Pallas kernels: 7.78 us -> 3.68 us  [pack(): pl.pallas_call(pack_kernel, out_shape=jax.ShapeDtypeStruct((owners, rows,...]
  transfers between devices with their start and end apart: 5 -> 18, of which waited for: 5 -> 6; matrix products, arithmetic and copies ran while one was open for 1% -> 2% of each run, Pallas kernels for 8% -> 15%
where the time goes in v2:
time: 261 us; the launch traced here: 260 us
  waiting for transfers between devices  94.1 us (36%)
  starting transfers between devices  79.4 us (30%)
  Pallas kernels  43.5 us (17%)
  blocking collectives  20.7 us (8%)
  between operations  14.6 us (6%)
  local copies, waits for them, and re-layouts  6.48 us (2%)
    ppermute x14, starting transfers between devices, shifted(): lax.ppermute(parts[d], 'head', [(i, (i + d) % count) for i in range(count)])  61.3 us
    all_to_all x3, waiting for transfers between devices, exchange(): return lax.all_to_all(tiles, 'ctx', split_axis=0, concat_axis=0, tiled=True)  43.5 us
    all_gather x1, waiting for transfers between devices, on_device(): gathered_keys = lax.all_gather(context_keys, 'ctx', axis=0, tiled=True)  43.1 us
    all_to_all x1, blocking collectives, on_device(): lax.all_to_all(wanted, 'ctx', split_axis=0, concat_axis=0, tiled=True)[:, 0]  20.7 us
    all_to_all x3, starting transfers between devices, exchange(): return lax.all_to_all(tiles, 'ctx', split_axis=0, concat_axis=0, tiled=True)  18.1 us
    pallas_call x1, Pallas kernels, on_device(): pl.pallas_call(other_grads_kernel, out_shape=(near_shape, near_shape, nea...  17.1 us
    pallas_call x1, Pallas kernels, on_device(): pl.pallas_call(value_grad_kernel, out_shape=(near_shape, far_shape, stat_...  12.6 us
    pallas_call x2, Pallas kernels, collect(): pl.pallas_call(collect_kernel, out_shape=jax.ShapeDtypeStruct((rows, head...  8.26 us
  transfers between devices with their start and end apart: 18, of which 6 were waited for; matrix products, arithmetic and copies ran while one was open for 2% of the time, Pallas kernels for 15%

profile of v2, /device:TPU:1, one launch (start us, length us, event | category | flops | bytes accessed | tf_op | source)
XLA Modules:
  0.0 259.5 jit_solution(1355496857960506532)
XLA Ops:
  7.2 0.0 all-gather.2.cloned.1.call-start
  7.2 0.7 all-gather.2.cloned.1.call-update
  7.9 0.8 copy.19
  8.7 0.1 reshape.52.sel_ref
  8.8 0.1 select_reduce_fusion
  8.9 0.1 broadcast_in_dim.26
  9.0 0.1 broadcast_in_dim.27
  9.1 0.1 broadcast_in_dim.28
  9.2 20.7 %all_to_all.24 = s32[64,1,128]{2,1,0:T(1,128)S(1)} all-to-all(s32[64,1,128]{2,1,0:T(1,128)S(1)} %broadcast_in_dim.28), channel_id=1, replica_groups=mesh['ctx'=64,'head'=8] {'ctx'}, dimensions={0} | all-to-all | bytes 65536 | tf_op jit(solution)/shard_map/all_to_all | solution.py:264
  29.9 0.7 slice_reduce_fusion.codes_ref
  30.6 3.7 %shard_map.127 = bf16[64,128,128]{2,1,0:T(8,128)(2,1)} custom-call(s32[64]{0:T(128)} %slice_reduce_fusion.codes_ref, bf16[128,512]{1,0:T(8,128)(2,1)} %context_ref.1), custom_call_target="tpu_custom_call" | custom-call | tf_op jit(solution)/shard_map/pallas_call | solution.py:189
  34.2 4.9 %all-to-all-start.1 = ((bf16[64,128,128]{2,1,0:T(8,128)(2,1)}), bf16[64,128,128]{2,1,0:T(8,128)(2,1)S(1)}, u32[]{:S(2)}, u32[]{:S(2)}) async-start(bf16[64,128,128]{2,1,0:T(8,128)(2,1)} %shard_map.127), calls=%async_computation.1 | async-start | bytes 4194304 | tf_op jit(solution)/shard_map/all_to_all | solution.py:267
  39.2 0.7 constant_dynamic-slice_fusion.8
  39.9 10.7 %collective-permute-start.6 = (bf16[64,512]{1,0:T(8,128)(2,1)S(1)}, bf16[64,512]{1,0:T(8,128)(2,1)S(1)}, u32[]{:S(2)}, u32[]{:S(2)}) collective-permute-start(bf16[64,512]{1,0:T(8,128)(2,1)S(1)} %get-tuple-element.30), channel_id=1, source_target_pairs={{0,7},{1,0},{2,1},{3,2},{4,3},{5,4},{6,5},{7,6},{8,15},{9,8},{10,9... | collective-permute-start | bytes 196616 | tf_op jit(solution)/shard_map/ppermute | solution.py:221
  50.6 2.2 collective-permute-start.4
  52.8 1.9 collective-permute-start.3
  54.7 4.9 %collective-permute-start.2 = (bf16[64,512]{1,0:T(8,128)(2,1)S(1)}, bf16[64,512]{1,0:T(8,128)(2,1)S(1)}, u32[]{:S(2)}, u32[]{:S(2)}) collective-permute-start(bf16[64,512]{1,0:T(8,128)(2,1)S(1)} %get-tuple-element.33), channel_id=1, source_target_pairs={{0,3},{1,4},{2,5},{3,6},{4,7},{5,0},{6,1},{7,2},{8,11},{9,12},{10,... | collective-permute-start | bytes 196616 | tf_op jit(solution)/shard_map/ppermute | solution.py:221
  59.6 5.5 %collective-permute-start.1 = (bf16[64,512]{1,0:T(8,128)(2,1)S(1)}, bf16[64,512]{1,0:T(8,128)(2,1)S(1)}, u32[]{:S(2)}, u32[]{:S(2)}) collective-permute-start(bf16[64,512]{1,0:T(8,128)(2,1)S(1)} %get-tuple-element.34), channel_id=1, source_target_pairs={{0,2},{1,3},{2,4},{3,5},{4,6},{5,7},{6,0},{7,1},{8,10},{9,11},{10,... | collective-permute-start | bytes 196616 | tf_op jit(solution)/shard_map/ppermute | solution.py:221
  65.1 3.1 %collective-permute-start = (bf16[64,512]{1,0:T(8,128)(2,1)S(1)}, bf16[64,512]{1,0:T(8,128)(2,1)S(1)}, u32[]{:S(2)}, u32[]{:S(2)}) collective-permute-start(bf16[64,512]{1,0:T(8,128)(2,1)S(1)} %get-tuple-element.35), channel_id=1, source_target_pairs={{0,1},{1,2},{2,3},{3,4},{4,5},{5,6},{6,7},{7,0},{8,9},{9,10},{10,1... | collective-permute-start | bytes 196616 | tf_op jit(solution)/shard_map/ppermute | solution.py:221
  68.2 0.0 collective-permute-done.4.refs_5_
  68.2 3.4 %collective-permute-start.5 = (bf16[64,512]{1,0:T(8,128)(2,1)S(1)}, bf16[64,512]{1,0:T(8,128)(2,1)S(1)}, u32[]{:S(2)}, u32[]{:S(2)}) collective-permute-start(bf16[64,512]{1,0:T(8,128)(2,1)S(1)} %get-tuple-element.37), channel_id=1, source_target_pairs={{0,6},{1,7},{2,0},{3,1},{4,2},{5,3},{6,4},{7,5},{8,14},{9,15},{10,... | collective-permute-start | bytes 196616 | tf_op jit(solution)/shard_map/ppermute | solution.py:221
  71.6 0.6 pad_add_fusion.base_ref
  72.2 0.0 collective-permute-done.2.refs_3_
  72.3 0.0 copy-start.9
  72.3 2.1 collective-permute-done.5.refs_6_
  74.4 43.1 %all-gather.2.cloned.1.call-done.k1_ref.k2_ref.k3_ref = bf16[8192,512]{1,0:T(8,128)(2,1)} async-done(((bf16[128,512]{1,0:T(8,128)(2,1)}), bf16[8192,512]{1,0:T(8,128)(2,1)}) %all-gather.2.cloned.1.call-update) | async-done | bytes 8388624 | tf_op jit(solution)/shard_map/all_gather | solution.py:244
  117.6 12.6 %shard_map.128 = (bf16[512,512]{1,0:T(8,128)(2,1)}, bf16[16,512,128]{2,1,0:T(8,128)(2,1)}, f32[4,1,512]{2,1,0:T(1,128)}, f32[4,1,512]{2,1,0:T(1,128)}) custom-call(s32[12]{0:T(128)} %copy-done.18, s32[64]{0:T(128)} %lens_ref.3, s32[2]{0:T(128)} %pad_add_fusion.base_ref, bf16[512,512]{1,0:T(8,128)(2,1)} %q_ref.3, bf16[512,512]{1,0:T(8,128)(2,1)} %k_ref.3, ...), custom_call_target="tpu_custom_call" | custom-call | flops 2147483648 | bytes 8388608 | tf_op jit(solution)/shard_map/pallas_call | solution.py:292
  130.3 1.3 copy-done
  131.6 7.3 %all-to-all-start.2 = ((bf16[64,128,128]{2,1,0:T(8,128)(2,1)}), bf16[64,128,128]{2,1,0:T(8,128)(2,1)}, u32[]{:S(2)}, u32[]{:S(2)}) async-start(bf16[64,128,128]{2,1,0:T(8,128)(2,1)} %bitcast.12), calls=%async_computation.2 | async-start | bytes 4194304 | tf_op jit(solution)/shard_map/all_to_all | solution.py:267
  138.8 17.1 %shard_map.129 = (bf16[512,512]{1,0:T(8,128)(2,1)}, bf16[512,512]{1,0:T(8,128)(2,1)}, bf16[512,512]{1,0:T(8,128)(2,1)}, bf16[16,512,128]{2,1,0:T(8,128)(2,1)}) custom-call(s32[12]{0:T(128)} %copy-done.18, s32[64]{0:T(128)} %lens_ref.3, s32[2]{0:T(128)} %pad_add_fusion.base_ref, bf16[512,512]{1,0:T(8,128)(2,1)} %q_ref.3, bf16[512,512]{1,0:T(8,128)(2,1)} %k_ref.3, ...), custom_call_target="tpu_custom_call" | custom-call | flops 5368709120 | bytes 8388608 | tf_op jit(solution)/shard_map/pallas_call | solution.py:309
  155.9 34.1 %all-to-all-done.2.after_ref.terms_ref = bf16[64,128,128]{2,1,0:T(8,128)(2,1)} async-done(((bf16[64,128,128]{2,1,0:T(8,128)(2,1)}), bf16[64,128,128]{2,1,0:T(8,128)(2,1)}, u32[]{:S(2)}, u32[]{:S(2)}) %all-to-all-start.2) | async-done | bytes 2097184 | tf_op jit(solution)/shard_map/all_to_all | solution.py:267
  190.0 5.9 %all-to-all-start.3 = ((bf16[64,128,128]{2,1,0:T(8,128)(2,1)}), bf16[64,128,128]{2,1,0:T(8,128)(2,1)S(1)}, u32[]{:S(2)}, u32[]{:S(2)}) async-start(bf16[64,128,128]{2,1,0:T(8,128)(2,1)} %shard_map.131), calls=%async_computation.3 | async-start | bytes 4194304 | tf_op jit(solution)/shard_map/all_to_all | solution.py:267
  196.0 0.7 constant_dynamic-slice_fusion
  196.7 9.0 %collective-permute-start.13 = (bf16[64,512]{1,0:T(8,128)(2,1)S(1)}, bf16[64,512]{1,0:T(8,128)(2,1)S(1)}, u32[]{:S(2)}, u32[]{:S(2)}) collective-permute-start(bf16[64,512]{1,0:T(8,128)(2,1)S(1)} %get-tuple-element.22), channel_id=1, source_target_pairs={{0,7},{1,0},{2,1},{3,2},{4,3},{5,4},{6,5},{7,6},{8,15},{9,8},{10,9... | collective-permute-start | bytes 196616 | tf_op jit(solution)/shard_map/ppermute | solution.py:221
  205.7 2.9 %collective-permute-start.12 = (bf16[64,512]{1,0:T(8,128)(2,1)S(1)}, bf16[64,512]{1,0:T(8,128)(2,1)S(1)}, u32[]{:S(2)}, u32[]{:S(2)}) collective-permute-start(bf16[64,512]{1,0:T(8,128)(2,1)S(1)} %get-tuple-element.23), channel_id=1, source_target_pairs={{0,6},{1,7},{2,0},{3,1},{4,2},{5,3},{6,4},{7,5},{8,14},{9,15},{10,... | collective-permute-start | bytes 196616 | tf_op jit(solution)/shard_map/ppermute | solution.py:221
  208.6 2.1 collective-permute-start.11
  210.8 7.0 %collective-permute-start.10 = (bf16[64,512]{1,0:T(8,128)(2,1)S(1)}, bf16[64,512]{1,0:T(8,128)(2,1)S(1)}, u32[]{:S(2)}, u32[]{:S(2)}) collective-permute-start(bf16[64,512]{1,0:T(8,128)(2,1)S(1)} %get-tuple-element.25), channel_id=1, source_target_pairs={{0,4},{1,5},{2,6},{3,7},{4,0},{5,1},{6,2},{7,3},{8,12},{9,13},{10,... | collective-permute-start | bytes 196616 | tf_op jit(solution)/shard_map/ppermute | solution.py:221
  217.8 1.9 collective-permute-start.9
  219.7 3.4 %collective-permute-start.8 = (bf16[64,512]{1,0:T(8,128)(2,1)S(1)}, bf16[64,512]{1,0:T(8,128)(2,1)S(1)}, u32[]{:S(2)}, u32[]{:S(2)}) collective-permute-start(bf16[64,512]{1,0:T(8,128)(2,1)S(1)} %get-tuple-element.27), channel_id=1, source_target_pairs={{0,2},{1,3},{2,4},{3,5},{4,6},{5,7},{6,0},{7,1},{8,10},{9,11},{10,... | collective-permute-start | bytes 196616 | tf_op jit(solution)/shard_map/ppermute | solution.py:221
  223.1 3.4 %collective-permute-start.7 = (bf16[64,512]{1,0:T(8,128)(2,1)S(1)}, bf16[64,512]{1,0:T(8,128)(2,1)S(1)}, u32[]{:S(2)}, u32[]{:S(2)}) collective-permute-start(bf16[64,512]{1,0:T(8,128)(2,1)S(1)} %get-tuple-element.28), channel_id=1, source_target_pairs={{0,1},{1,2},{2,3},{3,4},{4,5},{5,6},{6,7},{7,0},{8,9},{9,10},{10,1... | collective-permute-start | bytes 196616 | tf_op jit(solution)/shard_map/ppermute | solution.py:221
  226.6 2.6 collective-permute-done.8.refs_2_
  229.1 2.1 collective-permute-done.7.refs_1_
  231.2 0.6 copy-done.17
  231.8 1.9 shard_map.130
  233.7 4.1 %shard_map.133 = bf16[128,512]{1,0:T(8,128)(2,1)} custom-call(s32[64]{0:T(128)} %slice_reduce_fusion.codes_ref, bf16[64,128,128]{2,1,0:T(8,128)(2,1)} %all-to-all-done.2.after_ref.terms_ref), custom_call_target="tpu_custom_call" | custom-call | tf_op jit(solution)/shard_map/pallas_call | solution.py:205
  237.8 9.4 %all-to-all-done.3.terms_ref = bf16[64,128,128]{2,1,0:T(8,128)(2,1)S(1)} async-done(((bf16[64,128,128]{2,1,0:T(8,128)(2,1)}), bf16[64,128,128]{2,1,0:T(8,128)(2,1)S(1)}, u32[]{:S(2)}, u32[]{:S(2)}) %all-to-all-start.3) | async-done | bytes 2097184 | tf_op jit(solution)/shard_map/all_to_all | solution.py:267
  247.2 1.4 copy-done.1
  248.6 4.1 %shard_map.132 = bf16[128,512]{1,0:T(8,128)(2,1)} custom-call(s32[64]{0:T(128)} %slice_reduce_fusion.codes_ref, bf16[64,128,128]{2,1,0:T(8,128)(2,1)} %copy-done.1), custom_call_target="tpu_custom_call" | custom-call | tf_op jit(solution)/shard_map/pallas_call | solution.py:205
  (46 shorter events, 0.1 us)
Async XLA Ops:
  7.2 110.4 %all-gather.2.cloned.1.call-start = ((), (), s32[]{:S(2)}) async-start(), calls=%async_computation.4 | async-start | bytes 8519680 | tf_op jit(solution)/shard_map/all_gather | solution.py:244
  8.8 25.5 %copy-start.18 = (s32[12]{0:T(128)}, s32[12]{0:T(128)S(1)}, u32[]{:S(2)}) copy-start(s32[12]{0:T(128)S(1)} %reshape.52.sel_ref) | copy-start | bytes 148
  34.2 5.0 %copy-start.2 = (bf16[64,4096]{1,0:T(8,128)(2,1)S(1)}, bf16[64,4096]{1,0:T(8,128)(2,1)}, u32[]{:S(2)}) copy-start(bf16[64,4096]{1,0:T(8,128)(2,1)} %param.11) | copy-start | bytes 1572868
  34.2 96.0 %all-to-all-start.1 = ((bf16[64,128,128]{2,1,0:T(8,128)(2,1)}), bf16[64,128,128]{2,1,0:T(8,128)(2,1)S(1)}, u32[]{:S(2)}, u32[]{:S(2)}) async-start(bf16[64,128,128]{2,1,0:T(8,128)(2,1)} %shard_map.127), calls=%async_computation.1 | async-start | bytes 4194304 | tf_op jit(solution)/shard_map/all_to_all | solution.py:267
  39.9 25.2 %collective-permute-start.6 = (bf16[64,512]{1,0:T(8,128)(2,1)S(1)}, bf16[64,512]{1,0:T(8,128)(2,1)S(1)}, u32[]{:S(2)}, u32[]{:S(2)}) collective-permute-start(bf16[64,512]{1,0:T(8,128)(2,1)S(1)} %get-tuple-element.30), channel_id=1, source_target_pairs={{0,7},{1,0},{2,1},{3,2},{4,3},{5,4},{6,5},{7,6},{8,15},{9,8},{10,9... | collective-permute-start | bytes 196616 | tf_op jit(solution)/shard_map/ppermute | solution.py:221
  50.6 17.6 %collective-permute-start.4 = (bf16[64,512]{1,0:T(8,128)(2,1)S(1)}, bf16[64,512]{1,0:T(8,128)(2,1)S(1)}, u32[]{:S(2)}, u32[]{:S(2)}) collective-permute-start(bf16[64,512]{1,0:T(8,128)(2,1)S(1)} %get-tuple-element.31), channel_id=1, source_target_pairs={{0,5},{1,6},{2,7},{3,0},{4,1},{5,2},{6,3},{7,4},{8,13},{9,14},{10,... | collective-permute-start | bytes 196616 | tf_op jit(solution)/shard_map/ppermute | solution.py:221
  52.8 19.5 %collective-permute-start.3 = (bf16[64,512]{1,0:T(8,128)(2,1)S(1)}, bf16[64,512]{1,0:T(8,128)(2,1)S(1)}, u32[]{:S(2)}, u32[]{:S(2)}) collective-permute-start(bf16[64,512]{1,0:T(8,128)(2,1)S(1)} %get-tuple-element.32), channel_id=1, source_target_pairs={{0,4},{1,5},{2,6},{3,7},{4,0},{5,1},{6,2},{7,3},{8,12},{9,13},{10,... | collective-permute-start | bytes 196616 | tf_op jit(solution)/shard_map/ppermute | solution.py:221
  54.7 17.5 %collective-permute-start.2 = (bf16[64,512]{1,0:T(8,128)(2,1)S(1)}, bf16[64,512]{1,0:T(8,128)(2,1)S(1)}, u32[]{:S(2)}, u32[]{:S(2)}) collective-permute-start(bf16[64,512]{1,0:T(8,128)(2,1)S(1)} %get-tuple-element.33), channel_id=1, source_target_pairs={{0,3},{1,4},{2,5},{3,6},{4,7},{5,0},{6,1},{7,2},{8,11},{9,12},{10,... | collective-permute-start | bytes 196616 | tf_op jit(solution)/shard_map/ppermute | solution.py:221
  59.6 12.6 %collective-permute-start.1 = (bf16[64,512]{1,0:T(8,128)(2,1)S(1)}, bf16[64,512]{1,0:T(8,128)(2,1)S(1)}, u32[]{:S(2)}, u32[]{:S(2)}) collective-permute-start(bf16[64,512]{1,0:T(8,128)(2,1)S(1)} %get-tuple-element.34), channel_id=1, source_target_pairs={{0,2},{1,3},{2,4},{3,5},{4,6},{5,7},{6,0},{7,1},{8,10},{9,11},{10,... | collective-permute-start | bytes 196616 | tf_op jit(solution)/shard_map/ppermute | solution.py:221
  65.1 52.5 %copy-start.4 = (bf16[64,512]{1,0:T(8,128)(2,1)}, bf16[64,512]{1,0:T(8,128)(2,1)S(1)}, u32[]{:S(2)}) copy-start(bf16[64,512]{1,0:T(8,128)(2,1)S(1)} %collective-permute-done.6.refs_7_) | copy-start | bytes 196612
  65.1 7.2 %collective-permute-start = (bf16[64,512]{1,0:T(8,128)(2,1)S(1)}, bf16[64,512]{1,0:T(8,128)(2,1)S(1)}, u32[]{:S(2)}, u32[]{:S(2)}) collective-permute-start(bf16[64,512]{1,0:T(8,128)(2,1)S(1)} %get-tuple-element.35), channel_id=1, source_target_pairs={{0,1},{1,2},{2,3},{3,4},{4,5},{5,6},{6,7},{7,0},{8,9},{9,10},{10,1... | collective-permute-start | bytes 196616 | tf_op jit(solution)/shard_map/ppermute | solution.py:221
  68.2 49.4 %copy-start.5 = (bf16[64,512]{1,0:T(8,128)(2,1)}, bf16[64,512]{1,0:T(8,128)(2,1)S(1)}, u32[]{:S(2)}) copy-start(bf16[64,512]{1,0:T(8,128)(2,1)S(1)} %collective-permute-done.4.refs_5_) | copy-start | bytes 196612
  68.2 6.2 %collective-permute-start.5 = (bf16[64,512]{1,0:T(8,128)(2,1)S(1)}, bf16[64,512]{1,0:T(8,128)(2,1)S(1)}, u32[]{:S(2)}, u32[]{:S(2)}) collective-permute-start(bf16[64,512]{1,0:T(8,128)(2,1)S(1)} %get-tuple-element.37), channel_id=1, source_target_pairs={{0,6},{1,7},{2,0},{3,1},{4,2},{5,3},{6,4},{7,5},{8,14},{9,15},{10,... | collective-permute-start | bytes 196616 | tf_op jit(solution)/shard_map/ppermute | solution.py:221
  72.2 45.4 %copy-start.6 = (bf16[64,512]{1,0:T(8,128)(2,1)}, bf16[64,512]{1,0:T(8,128)(2,1)S(1)}, u32[]{:S(2)}) copy-start(bf16[64,512]{1,0:T(8,128)(2,1)S(1)} %collective-permute-done.3.refs_4_) | copy-start | bytes 196612
  72.2 45.3 %copy-start.7 = (bf16[64,512]{1,0:T(8,128)(2,1)}, bf16[64,512]{1,0:T(8,128)(2,1)S(1)}, u32[]{:S(2)}) copy-start(bf16[64,512]{1,0:T(8,128)(2,1)S(1)} %collective-permute-done.2.refs_3_) | copy-start | bytes 196612
  72.3 45.3 %copy-start.8 = (bf16[64,512]{1,0:T(8,128)(2,1)}, bf16[64,512]{1,0:T(8,128)(2,1)S(1)}, u32[]{:S(2)}) copy-start(bf16[64,512]{1,0:T(8,128)(2,1)S(1)} %collective-permute-done.1.refs_2_) | copy-start | bytes 196612
  72.3 45.3 %copy-start.9 = (bf16[64,512]{1,0:T(8,128)(2,1)}, bf16[64,512]{1,0:T(8,128)(2,1)S(1)}, u32[]{:S(2)}) copy-start(bf16[64,512]{1,0:T(8,128)(2,1)S(1)} %collective-permute-done.refs_1_) | copy-start | bytes 196612
  74.4 43.2 %copy-start.10 = (bf16[64,512]{1,0:T(8,128)(2,1)}, bf16[64,512]{1,0:T(8,128)(2,1)S(1)}, u32[]{:S(2)}) copy-start(bf16[64,512]{1,0:T(8,128)(2,1)S(1)} %collective-permute-done.5.refs_6_) | copy-start | bytes 196612
  130.3 1.3 copy-start
  131.6 58.4 %all-to-all-start.2 = ((bf16[64,128,128]{2,1,0:T(8,128)(2,1)}), bf16[64,128,128]{2,1,0:T(8,128)(2,1)}, u32[]{:S(2)}, u32[]{:S(2)}) async-start(bf16[64,128,128]{2,1,0:T(8,128)(2,1)} %bitcast.12), calls=%async_computation.2 | async-start | bytes 4194304 | tf_op jit(solution)/shard_map/all_to_all | solution.py:267
  190.0 6.0 %copy-start.3 = (bf16[512,512]{1,0:T(8,128)(2,1)S(1)}, bf16[512,512]{1,0:T(8,128)(2,1)}, u32[]{:S(2)}) copy-start(bf16[512,512]{1,0:T(8,128)(2,1)} %get-tuple-element.16) | copy-start | bytes 1572868
  190.0 57.2 %all-to-all-start.3 = ((bf16[64,128,128]{2,1,0:T(8,128)(2,1)}), bf16[64,128,128]{2,1,0:T(8,128)(2,1)S(1)}, u32[]{:S(2)}, u32[]{:S(2)}) async-start(bf16[64,128,128]{2,1,0:T(8,128)(2,1)} %shard_map.131), calls=%async_computation.3 | async-start | bytes 4194304 | tf_op jit(solution)/shard_map/all_to_all | solution.py:267
  196.7 23.0 %collective-permute-start.13 = (bf16[64,512]{1,0:T(8,128)(2,1)S(1)}, bf16[64,512]{1,0:T(8,128)(2,1)S(1)}, u32[]{:S(2)}, u32[]{:S(2)}) collective-permute-start(bf16[64,512]{1,0:T(8,128)(2,1)S(1)} %get-tuple-element.22), channel_id=1, source_target_pairs={{0,7},{1,0},{2,1},{3,2},{4,3},{5,4},{6,5},{7,6},{8,15},{9,8},{10,9... | collective-permute-start | bytes 196616 | tf_op jit(solution)/shard_map/ppermute | solution.py:221
  205.7 17.4 %collective-permute-start.12 = (bf16[64,512]{1,0:T(8,128)(2,1)S(1)}, bf16[64,512]{1,0:T(8,128)(2,1)S(1)}, u32[]{:S(2)}, u32[]{:S(2)}) collective-permute-start(bf16[64,512]{1,0:T(8,128)(2,1)S(1)} %get-tuple-element.23), channel_id=1, source_target_pairs={{0,6},{1,7},{2,0},{3,1},{4,2},{5,3},{6,4},{7,5},{8,14},{9,15},{10,... | collective-permute-start | bytes 196616 | tf_op jit(solution)/shard_map/ppermute | solution.py:221
  208.6 17.9 %collective-permute-start.11 = (bf16[64,512]{1,0:T(8,128)(2,1)S(1)}, bf16[64,512]{1,0:T(8,128)(2,1)S(1)}, u32[]{:S(2)}, u32[]{:S(2)}) collective-permute-start(bf16[64,512]{1,0:T(8,128)(2,1)S(1)} %get-tuple-element.24), channel_id=1, source_target_pairs={{0,5},{1,6},{2,7},{3,0},{4,1},{5,2},{6,3},{7,4},{8,13},{9,14},{10,... | collective-permute-start | bytes 196616 | tf_op jit(solution)/shard_map/ppermute | solution.py:221
  210.8 15.7 %collective-permute-start.10 = (bf16[64,512]{1,0:T(8,128)(2,1)S(1)}, bf16[64,512]{1,0:T(8,128)(2,1)S(1)}, u32[]{:S(2)}, u32[]{:S(2)}) collective-permute-start(bf16[64,512]{1,0:T(8,128)(2,1)S(1)} %get-tuple-element.25), channel_id=1, source_target_pairs={{0,4},{1,5},{2,6},{3,7},{4,0},{5,1},{6,2},{7,3},{8,12},{9,13},{10,... | collective-permute-start | bytes 196616 | tf_op jit(solution)/shard_map/ppermute | solution.py:221
  217.8 8.7 %collective-permute-start.9 = (bf16[64,512]{1,0:T(8,128)(2,1)S(1)}, bf16[64,512]{1,0:T(8,128)(2,1)S(1)}, u32[]{:S(2)}, u32[]{:S(2)}) collective-permute-start(bf16[64,512]{1,0:T(8,128)(2,1)S(1)} %get-tuple-element.26), channel_id=1, source_target_pairs={{0,3},{1,4},{2,5},{3,6},{4,7},{5,0},{6,1},{7,2},{8,11},{9,12},{10,... | collective-permute-start | bytes 196616 | tf_op jit(solution)/shard_map/ppermute | solution.py:221
  219.7 11.5 %copy-start.11 = (bf16[64,512]{1,0:T(8,128)(2,1)}, bf16[64,512]{1,0:T(8,128)(2,1)S(1)}, u32[]{:S(2)}) copy-start(bf16[64,512]{1,0:T(8,128)(2,1)S(1)} %collective-permute-done.13.refs_7_) | copy-start | bytes 196612
  219.7 9.4 %collective-permute-start.8 = (bf16[64,512]{1,0:T(8,128)(2,1)S(1)}, bf16[64,512]{1,0:T(8,128)(2,1)S(1)}, u32[]{:S(2)}, u32[]{:S(2)}) collective-permute-start(bf16[64,512]{1,0:T(8,128)(2,1)S(1)} %get-tuple-element.27), channel_id=1, source_target_pairs={{0,2},{1,3},{2,4},{3,5},{4,6},{5,7},{6,0},{7,1},{8,10},{9,11},{10,... | collective-permute-start | bytes 196616 | tf_op jit(solution)/shard_map/ppermute | solution.py:221
  223.1 8.1 %copy-start.12 = (bf16[64,512]{1,0:T(8,128)(2,1)}, bf16[64,512]{1,0:T(8,128)(2,1)S(1)}, u32[]{:S(2)}) copy-start(bf16[64,512]{1,0:T(8,128)(2,1)S(1)} %collective-permute-done.12.refs_6_) | copy-start | bytes 196612
  223.1 8.1 %collective-permute-start.7 = (bf16[64,512]{1,0:T(8,128)(2,1)S(1)}, bf16[64,512]{1,0:T(8,128)(2,1)S(1)}, u32[]{:S(2)}, u32[]{:S(2)}) collective-permute-start(bf16[64,512]{1,0:T(8,128)(2,1)S(1)} %get-tuple-element.28), channel_id=1, source_target_pairs={{0,1},{1,2},{2,3},{3,4},{4,5},{5,6},{6,7},{7,0},{8,9},{9,10},{10,1... | collective-permute-start | bytes 196616 | tf_op jit(solution)/shard_map/ppermute | solution.py:221
  226.5 4.7 %copy-start.13 = (bf16[64,512]{1,0:T(8,128)(2,1)}, bf16[64,512]{1,0:T(8,128)(2,1)S(1)}, u32[]{:S(2)}) copy-start(bf16[64,512]{1,0:T(8,128)(2,1)S(1)} %collective-permute-done.11.refs_5_) | copy-start | bytes 196612
  226.5 4.7 %copy-start.14 = (bf16[64,512]{1,0:T(8,128)(2,1)}, bf16[64,512]{1,0:T(8,128)(2,1)S(1)}, u32[]{:S(2)}) copy-start(bf16[64,512]{1,0:T(8,128)(2,1)S(1)} %collective-permute-done.10.refs_4_) | copy-start | bytes 196612
  226.5 4.7 %copy-start.15 = (bf16[64,512]{1,0:T(8,128)(2,1)}, bf16[64,512]{1,0:T(8,128)(2,1)S(1)}, u32[]{:S(2)}) copy-start(bf16[64,512]{1,0:T(8,128)(2,1)S(1)} %collective-permute-done.9.refs_3_) | copy-start | bytes 196612
  229.1 2.1 copy-start.16
  231.2 0.6 copy-start.17
  247.2 1.4 copy-start.1
Sparse Core Ops, SparseCore 0:
  11.4 106.1 all-gather.1

commit v3 on v2

--- a/solution.py
+++ b/solution.py
@@ -3,10 +3,13 @@
 from jax import lax
 from jax.experimental import pallas as pl
 from jax.experimental.pallas import tpu as pltpu
+from jax.sharding import Mesh
 from jax.sharding import PartitionSpec as P
 
 NT = (((1,), (1,)), ((), ()))
 NN = (((1,), (0,)), ((), ()))
+SIZE_X, SIZE_Y, CORES = 4, 8, 2
+CTX = ("x", "y", "core")
 VMEM_BYTES = 56 * 1024 * 1024
 
 
@@ -34,16 +37,15 @@
     return jnp.where((key_at <= query_at) & (key_at >= start), scores, -jnp.inf)
 
 
-def pack_kernel(codes_ref, context_ref, out_ref):
-    count, _, width = out_ref.shape
+def pack_kernel(codes_ref, context_ref, *refs):
+    out_ref = refs[-1]
+    count, rows, width = out_ref.shape
     first = pl.program_id(0) * count
-
-    def step(d, carry):
-        column = pl.multiple_of(jnp.maximum(codes_ref[first + d], 0) * width, width)
-        out_ref[d] = context_ref[:, pl.ds(column, width)]
-        return carry
-
-    lax.fori_loop(0, count, step, 0, unroll=4)
+    groups = context_ref.shape[0] // rows
+    for j in range(count):
+        column = pl.multiple_of(jnp.maximum(codes_ref[first + j], 0) * width, width)
+        start = (j % groups) * rows
+        out_ref[j] = context_ref[start : start + rows, pl.ds(column, width)]
 
 
 def in_token_order(me, shares, out_ref):
@@ -52,6 +54,13 @@
     for distance, share in enumerate(shares):
         source = lax.rem(me + count - distance, count)
         out_ref[pl.ds(pl.multiple_of(source * rows, rows), rows), :] = share[...]
+
+
+def tile_of(parts):
+    rows = parts[0].shape[-2] // CORES
+    return jnp.concatenate(
+        [part[0, 0, p * rows : (p + 1) * rows] for p in range(CORES) for part in parts], axis=0
+    )
 
 
 def assemble_kernel(me_ref, *refs):
@@ -86,7 +95,7 @@
     scores_ref[0] = near
     top = jnp.max(near, axis=0, keepdims=True)
     for j in range(picks):
-        far = dot(far_k[j][...], q, NT)
+        far = dot(far_k[j][0], q, NT)
         scores_ref[j + 1] = far
         top = jnp.maximum(top, jnp.max(far, axis=0, keepdims=True))
     total = jnp.zeros((1, rows), jnp.float32)
@@ -110,10 +119,11 @@
 
 def other_grads_kernel(
     sel_ref, lens_ref, base_ref, q_ref, k_ref, v_ref,
-    k1_ref, k2_ref, k3_ref, v1_ref, v2_ref, v3_ref, top_ref, inverse_ref, *refs,
+    k1_ref, k2_ref, k3_ref, *refs,
 ):
-    *shares, attended_ref, query_ref, near_ref, far_ref, start_ref, weights_ref, g_ref = refs
-    far_k, far_v = (k1_ref, k2_ref, k3_ref), (v1_ref, v2_ref, v3_ref)
+    *far_v, top_ref, inverse_ref = refs[:8]
+    *shares, attended_ref, query_ref, near_ref, far_ref, start_ref, weights_ref, g_ref = refs[8:]
+    far_k = (k1_ref, k2_ref, k3_ref)
     head = pl.program_id(0)
     rows, width = q_ref.shape
     picks = weights_ref.shape[0] - 1
@@ -124,10 +134,10 @@
         start_ref[...] = document_starts(lens_ref, base_ref, rows)
 
     def keys_of(j):
-        return k_ref[...] if j == 0 else far_k[j - 1][...]
+        return k_ref[...] if j == 0 else far_k[j - 1][0]
 
     def values_of(j):
-        return v_ref[...] if j == 0 else far_v[j - 1][0]
+        return v_ref[...] if j == 0 else tile_of(far_v[2 * j - 2 : 2 * j])
 
     in_token_order(base_ref[1], shares, g_ref)
     q = q_ref[...]
@@ -183,17 +193,18 @@
             out_ref[:, h * width : (h + 1) * width] = total_ref[h].astype(out_ref.dtype)
 
 
-def pack(codes, context, owners, width):
-    rows = context.shape[0]
+def pack(codes, context, groups, width):
+    slots = codes.shape[0]
+    rows = context.shape[0] // groups
     steps = 4
     return pl.pallas_call(
         pack_kernel,
-        out_shape=jax.ShapeDtypeStruct((owners, rows, width), context.dtype),
+        out_shape=jax.ShapeDtypeStruct((slots, rows, width), context.dtype),
         grid_spec=pltpu.PrefetchScalarGridSpec(
             num_scalar_prefetch=1,
             grid=(steps,),
             in_specs=[pl.BlockSpec(context.shape, lambda i, *_: (0, 0))],
-            out_specs=pl.BlockSpec((owners // steps, rows, width), lambda i, *_: (i, 0, 0)),
+            out_specs=pl.BlockSpec((slots // steps, rows, width), lambda i, *_: (i, 0, 0)),
         ),
         compiler_params=pltpu.CompilerParams(vmem_limit_bytes=VMEM_BYTES),
     )(codes, context)
@@ -239,9 +250,11 @@
     width = queries.shape[1] // heads
     piece_rows = context_keys.shape[0]
     pieces = rows // piece_rows
-    owners = lax.axis_size("ctx")
+    owners = lax.axis_size(CTX)
     blocks = owners // pieces
-    gathered_keys = lax.all_gather(context_keys, "ctx", axis=0, tiled=True)
+    my_x, my_y = lax.axis_index("x"), lax.axis_index("y")
+    my_piece = lax.axis_index(CTX).astype(jnp.int32)
+    column_values = lax.all_gather(context_values, "y", axis=0, tiled=True)
     count = lax.axis_size("head")
     me = lax.axis_index("head").astype(jnp.int32)
     share_rows = rows // count
@@ -254,30 +267,54 @@
         ],
         count,
     )
-    base = jnp.stack([lax.axis_index("ctx").astype(jnp.int32) * rows, me])
     flat = selected.reshape(-1)
 
     head_of = jnp.arange(heads * picks, dtype=jnp.int32) // picks
     hits = flat[None, :] == jnp.arange(blocks, dtype=jnp.int32)[:, None]
     wanted = jnp.max(jnp.where(hits, head_of[None, :], -1), axis=1)
-    wanted = jnp.broadcast_to(wanted[:, None, None], (blocks, pieces, 128)).reshape(owners, 128)
-    codes = lax.all_to_all(wanted, "ctx", split_axis=0, concat_axis=0, tiled=True)[:, 0]
-
-    def exchange(tiles):
-        return lax.all_to_all(tiles, "ctx", split_axis=0, concat_axis=0, tiled=True)
-
-    far_values = exchange(pack(codes, context_values, owners, width)).reshape(blocks, rows, width)
+    wanted = jnp.broadcast_to(jnp.pad(wanted, (0, 128 - blocks)), (owners, 128))
+    codes = lax.all_to_all(wanted, CTX, split_axis=0, concat_axis=0, tiled=True)
+    piece_codes = lax.dynamic_slice_in_dim(codes, my_piece // pieces, 1, 1)[:, 0]
+    own_x = blocks // SIZE_X
+    peers = SIZE_X * CORES
+    me_row = (my_x * CORES + lax.axis_index("core")).astype(jnp.int32)
+    base = jnp.stack([my_piece * rows, me, me_row])
+    row_codes = lax.dynamic_slice(
+        codes.reshape(SIZE_X, SIZE_Y, CORES, 128),
+        (0, my_y, 0, my_x * own_x),
+        (SIZE_X, 1, CORES, own_x),
+    ).reshape(peers, own_x)
+    row_codes = jnp.concatenate([row_codes, row_codes])
+    row_codes = lax.dynamic_slice_in_dim(row_codes, me_row, peers, 0).reshape(-1)
+
+    def to_holders(tiles):
+        tiles = tiles.reshape(owners, piece_rows, width)
+        return lax.all_to_all(tiles, CTX, split_axis=0, concat_axis=0, tiled=True)
+
+    far_keys = to_holders(pack(piece_codes, context_keys, 1, width)).reshape(blocks, rows, width)
+    sent = pack(row_codes, column_values, own_x, width).reshape(peers, own_x, rows // CORES, width)
+    far_values = [sent[0]] + [
+        lax.ppermute(sent[d], ("x", "core"), [(i, (i + d) % peers) for i in range(peers)])
+        for d in range(1, peers)
+    ]
+    far_values = jnp.stack(far_values)
 
     by_head = pl.BlockSpec((rows, width), lambda h, *_: (0, h))
     all_far = pl.BlockSpec((blocks, rows, width), lambda h, *_: (0, 0, 0))
     far_key = [
-        pl.BlockSpec((rows, width), lambda h, sel, *_, j=j: (sel[h * picks + j], h))
-        for j in range(picks)
-    ]
-    far_value = [
         pl.BlockSpec((1, rows, width), lambda h, sel, *_, j=j: (sel[h * picks + j], 0, 0))
         for j in range(picks)
     ]
+
+    def value_at(j, c):
+        def index(h, sel, lens, base):
+            block = sel[h * picks + j]
+            source = (block // own_x) * CORES + c
+            return (lax.rem(base[2] + peers - source, peers), lax.rem(block, own_x), 0, 0)
+
+        return pl.BlockSpec((1, 1, rows // CORES, width), index)
+
+    far_value = [value_at(j, c) for j in range(picks) for c in range(CORES)]
     shares = [pl.BlockSpec((share_rows, width), lambda h, *_: (0, h))] * count
     by_stat = pl.BlockSpec((1, 1, rows), lambda h, *_: (h, 0, 0))
     near_shape = jax.ShapeDtypeStruct(queries.shape, jnp.bfloat16)
@@ -303,8 +340,8 @@
         cost_estimate=pl.CostEstimate(
             flops=2 * tile_flops, bytes_accessed=8 << 20, transcendentals=heads * 4 * rows * rows
         ),
-    )(flat, doc_lengths, base, queries, keys, *[gathered_keys] * picks, *grads)
-    value_terms = exchange(far_value_grads.reshape(owners, piece_rows, width))
+    )(flat, doc_lengths, base, queries, keys, *[far_keys] * picks, *grads)
+    value_terms = to_holders(far_value_grads)
 
     attended, query_grad, key_grad, far_key_grads = pl.pallas_call(
         other_grads_kernel,
@@ -322,9 +359,9 @@
         ),
     )(
         flat, doc_lengths, base, queries, keys, values,
-        *[gathered_keys] * picks, *[far_values] * picks, top, inverse, *grads,
-    )
-    key_terms = exchange(gate(far_key_grads.reshape(owners, piece_rows, width), value_terms))
+        *[far_keys] * picks, *[far_values] * len(far_value), top, inverse, *grads,
+    )
+    key_terms = to_holders(gate(far_key_grads, value_terms))
 
     output_parts = shifted(
         [
@@ -340,18 +377,19 @@
         + [pl.BlockSpec(memory_space=pltpu.VMEM)] * count,
         out_specs=pl.BlockSpec(memory_space=pltpu.VMEM),
     )(me.reshape(1), *output_parts)
-    context_value_grad = collect(codes, value_terms, heads)
-    context_key_grad = collect(codes, key_terms, heads)
+    context_value_grad = collect(piece_codes, value_terms, heads)
+    context_key_grad = collect(piece_codes, key_terms, heads)
     return output_rows, query_grad, key_grad, value_grad, context_key_grad, context_value_grad
 
 
 def solution(mesh):
-    split = P("ctx", "head")
-    rows = P(("ctx", "head"), None)
+    devices = mesh.devices.reshape(SIZE_X, SIZE_Y, CORES, -1)
+    split = P(CTX, "head")
+    rows = P((*CTX, "head"), None)
     return jax.shard_map(
         on_device,
-        mesh=mesh,
-        in_specs=(split, split, split, rows, split, split, P("head", "ctx", None), P()),
+        mesh=Mesh(devices, (*CTX, "head")),
+        in_specs=(split, split, split, rows, split, split, P("head", CTX, None), P()),
         out_specs=(rows, split, split, split, split, split),
         check_vma=False,
     )

time: 261 us -> 270 us (1.034)
  starting transfers between devices: 79.4 us -> 127 us
  waiting for transfers between devices: 94.1 us -> 64 us
  blocking collectives: 20.7 us -> 0 us
  local copies, waits for them, and re-layouts: 6.48 us -> 14.5 us
  Pallas kernels: 43.5 us -> 47.8 us
    all_gather x1, waiting for transfers between devices: 43.1 us -> 0.01 us  [on_device(): column_values = lax.all_gather(context_values, 'y', axis=0, tiled=True)]
    ppermute x0 -> x7, starting transfers between devices: none -> 30 us  [on_device(): lax.ppermute(sent[d], ('x', 'core'), [(i, (i + d) % peers) for i in range...]
    all_to_all x1 -> x0, blocking collectives: 20.7 us -> none  [on_device(): lax.all_to_all(wanted, 'ctx', split_axis=0, concat_axis=0, tiled=True)[:, 0]]
    all_to_all x3 -> x4, starting transfers between devices: 18.1 us -> 34.3 us  [the longest x3 22.6 us: to_holders(): return lax.all_to_all(tiles, CTX, split_axis=0, concat_axis=0, tiled=True)]
    ppermute x0 -> x7, waiting for transfers between devices: none -> 13.9 us  [on_device(): lax.ppermute(sent[d], ('x', 'core'), [(i, (i + d) % peers) for i in range...]
    unnamed x39 -> x50, local copies, waits for them, and re-layouts: 4.09 us -> 7.95 us
    pallas_call x1 -> x2, Pallas kernels: 3.68 us -> 7.49 us  [pack(): pl.pallas_call(pack_kernel, out_shape=jax.ShapeDtypeStruct((slots, rows,...]
    all_to_all x3 -> x4, waiting for transfers between devices: 43.5 us -> 41.9 us  [the longest x3 32.7 us: to_holders(): return lax.all_to_all(tiles, CTX, split_axis=0, concat_axis=0, tiled=True)]
  transfers between devices with their start and end apart: 18 -> 26, of which waited for: 6 -> 9; matrix products, arithmetic and copies ran while one was open for 2% -> 2% of each run, Pallas kernels for 15% -> 15%
where the time goes in v3:
time: 270 us; the launch traced here: 268 us
  starting transfers between devices  127 us (47%)
  waiting for transfers between devices  64 us (24%)
  Pallas kernels  47.8 us (18%)
  between operations  14.8 us (5%)
  local copies, waits for them, and re-layouts  14.5 us (5%)
    ppermute x14, starting transfers between devices, shifted(): lax.ppermute(parts[d], 'head', [(i, (i + d) % count) for i in range(count)])  62.2 us
    all_to_all x3, waiting for transfers between devices, to_holders(): return lax.all_to_all(tiles, CTX, split_axis=0, concat_axis=0, tiled=True)  32.7 us
    ppermute x7, starting transfers between devices, on_device(): lax.ppermute(sent[d], ('x', 'core'), [(i, (i + d) % peers) for i in range...  30 us
    all_to_all x3, starting transfers between devices, to_holders(): return lax.all_to_all(tiles, CTX, split_axis=0, concat_axis=0, tiled=True)  22.6 us
    pallas_call x1, Pallas kernels, on_device(): pl.pallas_call(other_grads_kernel, out_shape=(near_shape, near_shape, nea...  17.6 us
    ppermute x7, waiting for transfers between devices, on_device(): lax.ppermute(sent[d], ('x', 'core'), [(i, (i + d) % peers) for i in range...  13.9 us
    pallas_call x1, Pallas kernels, on_device(): pl.pallas_call(value_grad_kernel, out_shape=(near_shape, far_shape, stat_...  12.5 us
    all_to_all x1, starting transfers between devices, on_device(): codes = lax.all_to_all(wanted, CTX, split_axis=0, concat_axis=0, tiled=True)  11.6 us
  transfers between devices with their start and end apart: 26, of which 9 were waited for; matrix products, arithmetic and copies ran while one was open for 2% of the time, Pallas kernels for 15%

profile of v3, /device:TPU:1, one launch (start us, length us, event | category | flops | bytes accessed | tf_op | source)
XLA Modules:
  0.0 268.3 jit_solution(11359194061430775798)
XLA Ops:
  7.2 0.8 copy.22
  8.8 11.6 %all-to-all-start = ((s32[64,1,128]{2,1,0:T(1,128)}), s32[64,1,128]{2,1,0:T(1,128)S(1)}, u32[]{:S(2)}, u32[]{:S(2)}) async-start(s32[64,1,128]{2,1,0:T(1,128)} %broadcast_in_dim.19), calls=%async_computation | async-start | bytes 65536 | tf_op jit(solution)/shard_map/all_to_all | solution.py:276
  20.5 9.2 %all-to-all-done = s32[64,1,128]{2,1,0:T(1,128)S(1)} async-done(((s32[64,1,128]{2,1,0:T(1,128)}), s32[64,1,128]{2,1,0:T(1,128)S(1)}, u32[]{:S(2)}, u32[]{:S(2)}) %all-to-all-start) | async-done | bytes 32800 | tf_op jit(solution)/shard_map/all_to_all | solution.py:276
  29.6 1.9 dynamic-slice_reduce_fusion.codes_ref
  31.5 3.6 %shard_map.127 = bf16[64,128,128]{2,1,0:T(8,128)(2,1)} custom-call(s32[64]{0:T(128)} %dynamic-slice_reduce_fusion.codes_ref, bf16[128,512]{1,0:T(8,128)(2,1)} %context_ref.1), custom_call_target="tpu_custom_call" | custom-call | tf_op jit(solution)/shard_map/pallas_call | solution.py:200
  35.1 4.9 %all-to-all-start.1 = ((bf16[64,128,128]{2,1,0:T(8,128)(2,1)}), bf16[64,128,128]{2,1,0:T(8,128)(2,1)S(1)}, u32[]{:S(2)}, u32[]{:S(2)}) async-start(bf16[64,128,128]{2,1,0:T(8,128)(2,1)} %shard_map.127), calls=%async_computation.1 | async-start | bytes 4194304 | tf_op jit(solution)/shard_map/all_to_all | solution.py:292
  41.5 10.7 %collective-permute-start.13 = (bf16[64,512]{1,0:T(8,128)(2,1)S(1)}, bf16[64,512]{1,0:T(8,128)(2,1)S(1)}, u32[]{:S(2)}, u32[]{:S(2)}) collective-permute-start(bf16[64,512]{1,0:T(8,128)(2,1)S(1)} %get-tuple-element.37), channel_id=1, source_target_pairs={{0,7},{1,0},{2,1},{3,2},{4,3},{5,4},{6,5},{7,6},{8,15},{9,8},{10,9... | collective-permute-start | bytes 196616 | tf_op jit(solution)/shard_map/ppermute | solution.py:232
  52.2 2.2 collective-permute-start.11
  54.3 1.9 collective-permute-start.10
  56.3 4.9 %collective-permute-start.9 = (bf16[64,512]{1,0:T(8,128)(2,1)S(1)}, bf16[64,512]{1,0:T(8,128)(2,1)S(1)}, u32[]{:S(2)}, u32[]{:S(2)}) collective-permute-start(bf16[64,512]{1,0:T(8,128)(2,1)S(1)} %get-tuple-element.40), channel_id=1, source_target_pairs={{0,3},{1,4},{2,5},{3,6},{4,7},{5,0},{6,1},{7,2},{8,11},{9,12},{10,... | collective-permute-start | bytes 196616 | tf_op jit(solution)/shard_map/ppermute | solution.py:232
  61.2 5.5 %collective-permute-start.8 = (bf16[64,512]{1,0:T(8,128)(2,1)S(1)}, bf16[64,512]{1,0:T(8,128)(2,1)S(1)}, u32[]{:S(2)}, u32[]{:S(2)}) collective-permute-start(bf16[64,512]{1,0:T(8,128)(2,1)S(1)} %get-tuple-element.41), channel_id=1, source_target_pairs={{0,2},{1,3},{2,4},{3,5},{4,6},{5,7},{6,0},{7,1},{8,10},{9,11},{10,... | collective-permute-start | bytes 196616 | tf_op jit(solution)/shard_map/ppermute | solution.py:232
  66.7 3.1 %collective-permute-start.7 = (bf16[64,512]{1,0:T(8,128)(2,1)S(1)}, bf16[64,512]{1,0:T(8,128)(2,1)S(1)}, u32[]{:S(2)}, u32[]{:S(2)}) collective-permute-start(bf16[64,512]{1,0:T(8,128)(2,1)S(1)} %get-tuple-element.42), channel_id=1, source_target_pairs={{0,1},{1,2},{2,3},{3,4},{4,5},{5,6},{6,7},{7,0},{8,9},{9,10},{10,1... | collective-permute-start | bytes 196616 | tf_op jit(solution)/shard_map/ppermute | solution.py:232
  69.8 3.4 %collective-permute-start.12 = (bf16[64,512]{1,0:T(8,128)(2,1)S(1)}, bf16[64,512]{1,0:T(8,128)(2,1)S(1)}, u32[]{:S(2)}, u32[]{:S(2)}) collective-permute-start(bf16[64,512]{1,0:T(8,128)(2,1)S(1)} %get-tuple-element.44), channel_id=1, source_target_pairs={{0,6},{1,7},{2,0},{3,1},{4,2},{5,3},{6,4},{7,5},{8,14},{9,15},{10,... | collective-permute-start | bytes 196616 | tf_op jit(solution)/shard_map/ppermute | solution.py:232
  73.8 2.3 collective-permute-done.12.refs_6_.refs_14_
  76.1 24.8 %all-to-all-done.1 = bf16[64,128,128]{2,1,0:T(8,128)(2,1)S(1)} async-done(((bf16[64,128,128]{2,1,0:T(8,128)(2,1)}), bf16[64,128,128]{2,1,0:T(8,128)(2,1)S(1)}, u32[]{:S(2)}, u32[]{:S(2)}) %all-to-all-start.1) | async-done | bytes 2097184 | tf_op jit(solution)/shard_map/all_to_all | solution.py:292
  101.0 1.3 copy-done.1
  102.3 12.5 %shard_map.129 = (bf16[512,512]{1,0:T(8,128)(2,1)}, bf16[16,512,128]{2,1,0:T(8,128)(2,1)}, f32[4,1,512]{2,1,0:T(1,128)}, f32[4,1,512]{2,1,0:T(1,128)}) custom-call(s32[12]{0:T(128)} %copy-done.20, s32[64]{0:T(128)} %lens_ref.3, s32[3]{0:T(128)} %pad_add_fusion.1.base_ref, bf16[512,512]{1,0:T(8,128)(2,1)} %q_ref.3, bf16[512,512]{1,0:T(8,128)(2,1)} %k_ref.3, ...), custom_call_target="tpu_custom_call" | custom-call | flops 2147483648 | bytes 8388608 | tf_op jit(solution)/shard_map/pallas_call | solution.py:329
  114.9 5.8 %all-to-all-start.2 = ((bf16[64,128,128]{2,1,0:T(8,128)(2,1)}), bf16[64,128,128]{2,1,0:T(8,128)(2,1)S(1)}, u32[]{:S(2)}, u32[]{:S(2)}) async-start(bf16[64,128,128]{2,1,0:T(8,128)(2,1)} %bitcast.35), calls=%async_computation.2 | async-start | bytes 4194304 | tf_op jit(solution)/shard_map/all_to_all | solution.py:292
  121.7 3.9 %shard_map.128 = bf16[32,256,128]{2,1,0:T(8,128)(2,1)} custom-call(s32[32]{0:T(128)} %reshape.78.codes_ref, bf16[1024,512]{1,0:T(8,128)(2,1)} %all-gather.2.cloned.1.call-done.context_ref), custom_call_target="tpu_custom_call" | custom-call | tf_op jit(solution)/shard_map/pallas_call | solution.py:200
  125.6 1.6 fusion.1
  127.2 1.6 collective-permute-start
  128.8 3.2 %collective-permute-start.1 = (bf16[4,256,128]{2,1,0:T(8,128)(2,1)S(1)}, bf16[4,256,128]{2,1,0:T(8,128)(2,1)S(1)}, u32[]{:S(2)}, u32[]{:S(2)}) collective-permute-start(bf16[4,256,128]{2,1,0:T(8,128)(2,1)S(1)} %get-tuple-element.27), channel_id=1, source_target_pairs={{0,128},{8,136},{128,256},{136,264},{256,384},{264,392},{384,0},{3... | collective-permute-start | bytes 786440 | tf_op jit(solution)/shard_map/ppermute | solution.py:297
  132.0 1.0 fusion
  133.0 3.3 %collective-permute-start.5 = (bf16[4,256,128]{2,1,0:T(8,128)(2,1)S(1)}, bf16[4,256,128]{2,1,0:T(8,128)(2,1)S(1)}, u32[]{:S(2)}, u32[]{:S(2)}) collective-permute-start(bf16[4,256,128]{2,1,0:T(8,128)(2,1)S(1)} %get-tuple-element.23), channel_id=1, source_target_pairs={{0,384},{8,392},{128,0},{136,8},{256,128},{264,136},{384,256},{392... | collective-permute-start | bytes 786440 | tf_op jit(solution)/shard_map/ppermute | solution.py:297
  136.3 4.1 %collective-permute-start.4 = (bf16[4,256,128]{2,1,0:T(8,128)(2,1)S(1)}, bf16[4,256,128]{2,1,0:T(8,128)(2,1)S(1)}, u32[]{:S(2)}, u32[]{:S(2)}) collective-permute-start(bf16[4,256,128]{2,1,0:T(8,128)(2,1)S(1)} %get-tuple-element.24), channel_id=1, source_target_pairs={{0,264},{8,384},{128,392},{136,0},{256,8},{264,128},{384,136},{392... | collective-permute-start | bytes 786440 | tf_op jit(solution)/shard_map/ppermute | solution.py:297
  140.5 3.0 %collective-permute-start.2 = (bf16[4,256,128]{2,1,0:T(8,128)(2,1)S(1)}, bf16[4,256,128]{2,1,0:T(8,128)(2,1)S(1)}, u32[]{:S(2)}, u32[]{:S(2)}) collective-permute-start(bf16[4,256,128]{2,1,0:T(8,128)(2,1)S(1)} %get-tuple-element.26), channel_id=1, source_target_pairs={{0,136},{8,256},{128,264},{136,384},{256,392},{264,0},{384,8},{392... | collective-permute-start | bytes 786440 | tf_op jit(solution)/shard_map/ppermute | solution.py:297
  143.5 3.2 %collective-permute-done.1 = bf16[4,256,128]{2,1,0:T(8,128)(2,1)S(1)} collective-permute-done((bf16[4,256,128]{2,1,0:T(8,128)(2,1)S(1)}, bf16[4,256,128]{2,1,0:T(8,128)(2,1)S(1)}, u32[]{:S(2)}, u32[]{:S(2)}) %collective-permute-start.1) | collective-permute-done | bytes 262176 | tf_op jit(solution)/shard_map/ppermute | solution.py:297
  146.7 14.8 %collective-permute-start.3 = (bf16[4,256,128]{2,1,0:T(8,128)(2,1)S(1)}, bf16[4,256,128]{2,1,0:T(8,128)(2,1)S(1)}, u32[]{:S(2)}, u32[]{:S(2)}) collective-permute-start(bf16[4,256,128]{2,1,0:T(8,128)(2,1)S(1)} %get-tuple-element.25), channel_id=1, source_target_pairs={{0,256},{8,264},{128,384},{136,392},{256,0},{264,8},{384,128},{392... | collective-permute-start | bytes 786440 | tf_op jit(solution)/shard_map/ppermute | solution.py:297
  161.5 1.1 collective-permute-done.2
  162.6 9.6 %collective-permute-done.3 = bf16[4,256,128]{2,1,0:T(8,128)(2,1)S(1)} collective-permute-done((bf16[4,256,128]{2,1,0:T(8,128)(2,1)S(1)}, bf16[4,256,128]{2,1,0:T(8,128)(2,1)S(1)}, u32[]{:S(2)}, u32[]{:S(2)}) %collective-permute-start.3) | collective-permute-done | bytes 262176 | tf_op jit(solution)/shard_map/ppermute | solution.py:297
  172.5 1.4 copy-done
  173.9 17.6 %shard_map.130 = (bf16[512,512]{1,0:T(8,128)(2,1)}, bf16[512,512]{1,0:T(8,128)(2,1)}, bf16[512,512]{1,0:T(8,128)(2,1)}, bf16[16,512,128]{2,1,0:T(8,128)(2,1)}) custom-call(s32[12]{0:T(128)} %copy-done.20, s32[64]{0:T(128)} %lens_ref.3, s32[3]{0:T(128)} %pad_add_fusion.1.base_ref, bf16[512,512]{1,0:T(8,128)(2,1)} %q_ref.3, bf16[512,512]{1,0:T(8,128)(2,1)} %k_ref.3, ...), custom_call_target="tpu_custom_call" | custom-call | flops 5368709120 | bytes 8388608 | tf_op jit(solution)/shard_map/pallas_call | solution.py:346
  191.5 1.3 copy-done.2
  192.8 11.9 %all-to-all-start.3 = ((bf16[64,128,128]{2,1,0:T(8,128)(2,1)}), bf16[64,128,128]{2,1,0:T(8,128)(2,1)S(1)}, u32[]{:S(2)}, u32[]{:S(2)}) async-start(bf16[64,128,128]{2,1,0:T(8,128)(2,1)} %bitcast.34), calls=%async_computation.3 | async-start | bytes 4194304 | tf_op jit(solution)/shard_map/all_to_all | solution.py:292
  205.5 10.9 %collective-permute-start.20 = (bf16[64,512]{1,0:T(8,128)(2,1)S(1)}, bf16[64,512]{1,0:T(8,128)(2,1)S(1)}, u32[]{:S(2)}, u32[]{:S(2)}) collective-permute-start(bf16[64,512]{1,0:T(8,128)(2,1)S(1)} %get-tuple-element.29), channel_id=1, source_target_pairs={{0,7},{1,0},{2,1},{3,2},{4,3},{5,4},{6,5},{7,6},{8,15},{9,8},{10,9... | collective-permute-start | bytes 196616 | tf_op jit(solution)/shard_map/ppermute | solution.py:232
  216.4 2.2 collective-permute-start.19
  218.6 1.9 collective-permute-start.18
  220.5 7.3 %collective-permute-start.17 = (bf16[64,512]{1,0:T(8,128)(2,1)S(1)}, bf16[64,512]{1,0:T(8,128)(2,1)S(1)}, u32[]{:S(2)}, u32[]{:S(2)}) collective-permute-start(bf16[64,512]{1,0:T(8,128)(2,1)S(1)} %get-tuple-element.32), channel_id=1, source_target_pairs={{0,4},{1,5},{2,6},{3,7},{4,0},{5,1},{6,2},{7,3},{8,12},{9,13},{10,... | collective-permute-start | bytes 196616 | tf_op jit(solution)/shard_map/ppermute | solution.py:232
  227.8 1.9 collective-permute-start.16
  229.8 3.1 %collective-permute-start.15 = (bf16[64,512]{1,0:T(8,128)(2,1)S(1)}, bf16[64,512]{1,0:T(8,128)(2,1)S(1)}, u32[]{:S(2)}, u32[]{:S(2)}) collective-permute-start(bf16[64,512]{1,0:T(8,128)(2,1)S(1)} %get-tuple-element.34), channel_id=1, source_target_pairs={{0,2},{1,3},{2,4},{3,5},{4,6},{5,7},{6,0},{7,1},{8,10},{9,11},{10,... | collective-permute-start | bytes 196616 | tf_op jit(solution)/shard_map/ppermute | solution.py:232
  232.9 3.3 %collective-permute-start.14 = (bf16[64,512]{1,0:T(8,128)(2,1)S(1)}, bf16[64,512]{1,0:T(8,128)(2,1)S(1)}, u32[]{:S(2)}, u32[]{:S(2)}) collective-permute-start(bf16[64,512]{1,0:T(8,128)(2,1)S(1)} %get-tuple-element.35), channel_id=1, source_target_pairs={{0,1},{1,2},{2,3},{3,4},{4,5},{5,6},{6,7},{7,0},{8,9},{9,10},{10,1... | collective-permute-start | bytes 196616 | tf_op jit(solution)/shard_map/ppermute | solution.py:232
  236.3 3.6 %collective-permute-done.15.refs_2_ = bf16[64,512]{1,0:T(8,128)(2,1)S(1)} collective-permute-done((bf16[64,512]{1,0:T(8,128)(2,1)S(1)}, bf16[64,512]{1,0:T(8,128)(2,1)S(1)}, u32[]{:S(2)}, u32[]{:S(2)}) %collective-permute-start.15) | collective-permute-done | bytes 65568 | tf_op jit(solution)/shard_map/ppermute | solution.py:232
  239.9 1.6 collective-permute-done.14.refs_1_
  242.1 1.9 shard_map.131
  244.0 4.1 %shard_map.134 = bf16[128,512]{1,0:T(8,128)(2,1)} custom-call(s32[64]{0:T(128)} %dynamic-slice_reduce_fusion.codes_ref, bf16[64,128,128]{2,1,0:T(8,128)(2,1)} %copy-done.2), custom_call_target="tpu_custom_call" | custom-call | tf_op jit(solution)/shard_map/pallas_call | solution.py:216
  248.1 7.9 %all-to-all-done.3.terms_ref = bf16[64,128,128]{2,1,0:T(8,128)(2,1)S(1)} async-done(((bf16[64,128,128]{2,1,0:T(8,128)(2,1)}), bf16[64,128,128]{2,1,0:T(8,128)(2,1)S(1)}, u32[]{:S(2)}, u32[]{:S(2)}) %all-to-all-start.3) | async-done | bytes 2097184 | tf_op jit(solution)/shard_map/all_to_all | solution.py:292
  256.0 1.3 copy-done.3
  257.3 4.1 %shard_map.133 = bf16[128,512]{1,0:T(8,128)(2,1)} custom-call(s32[64]{0:T(128)} %dynamic-slice_reduce_fusion.codes_ref, bf16[64,128,128]{2,1,0:T(8,128)(2,1)} %copy-done.3), custom_call_target="tpu_custom_call" | custom-call | tf_op jit(solution)/shard_map/pallas_call | solution.py:216
  (80 shorter events, 5.5 us)
Async XLA Ops:
  8.0 27.1 %copy-start.20 = (s32[12]{0:T(128)}, s32[12]{0:T(128)S(1)}, u32[]{:S(2)}) copy-start(s32[12]{0:T(128)S(1)} %reshape.74.sel_ref) | copy-start | bytes 148
  8.8 20.8 %all-to-all-start = ((s32[64,1,128]{2,1,0:T(1,128)}), s32[64,1,128]{2,1,0:T(1,128)S(1)}, u32[]{:S(2)}, u32[]{:S(2)}) async-start(s32[64,1,128]{2,1,0:T(1,128)} %broadcast_in_dim.19), calls=%async_computation | async-start | bytes 65536 | tf_op jit(solution)/shard_map/all_to_all | solution.py:276
  35.1 5.7 %copy-start.4 = (bf16[64,4096]{1,0:T(8,128)(2,1)S(1)}, bf16[64,4096]{1,0:T(8,128)(2,1)}, u32[]{:S(2)}) copy-start(bf16[64,4096]{1,0:T(8,128)(2,1)} %param.11) | copy-start | bytes 1572868
  35.1 65.9 %all-to-all-start.1 = ((bf16[64,128,128]{2,1,0:T(8,128)(2,1)}), bf16[64,128,128]{2,1,0:T(8,128)(2,1)S(1)}, u32[]{:S(2)}, u32[]{:S(2)}) async-start(bf16[64,128,128]{2,1,0:T(8,128)(2,1)} %shard_map.127), calls=%async_computation.1 | async-start | bytes 4194304 | tf_op jit(solution)/shard_map/all_to_all | solution.py:292
  40.0 81.7 %all-gather.2.cloned.1.call-start = ((), (), s32[]{:S(2)}) async-start(), calls=%async_computation.4 | async-start | bytes 1179648 | tf_op jit(solution)/shard_map/all_gather | solution.py:257
  41.5 25.2 %collective-permute-start.13 = (bf16[64,512]{1,0:T(8,128)(2,1)S(1)}, bf16[64,512]{1,0:T(8,128)(2,1)S(1)}, u32[]{:S(2)}, u32[]{:S(2)}) collective-permute-start(bf16[64,512]{1,0:T(8,128)(2,1)S(1)} %get-tuple-element.37), channel_id=1, source_target_pairs={{0,7},{1,0},{2,1},{3,2},{4,3},{5,4},{6,5},{7,6},{8,15},{9,8},{10,9... | collective-permute-start | bytes 196616 | tf_op jit(solution)/shard_map/ppermute | solution.py:232
  52.2 17.6 %collective-permute-start.11 = (bf16[64,512]{1,0:T(8,128)(2,1)S(1)}, bf16[64,512]{1,0:T(8,128)(2,1)S(1)}, u32[]{:S(2)}, u32[]{:S(2)}) collective-permute-start(bf16[64,512]{1,0:T(8,128)(2,1)S(1)} %get-tuple-element.38), channel_id=1, source_target_pairs={{0,5},{1,6},{2,7},{3,0},{4,1},{5,2},{6,3},{7,4},{8,13},{9,14},{10,... | collective-permute-start | bytes 196616 | tf_op jit(solution)/shard_map/ppermute | solution.py:232
  54.3 19.4 %collective-permute-start.10 = (bf16[64,512]{1,0:T(8,128)(2,1)S(1)}, bf16[64,512]{1,0:T(8,128)(2,1)S(1)}, u32[]{:S(2)}, u32[]{:S(2)}) collective-permute-start(bf16[64,512]{1,0:T(8,128)(2,1)S(1)} %get-tuple-element.39), channel_id=1, source_target_pairs={{0,4},{1,5},{2,6},{3,7},{4,0},{5,1},{6,2},{7,3},{8,12},{9,13},{10,... | collective-permute-start | bytes 196616 | tf_op jit(solution)/shard_map/ppermute | solution.py:232
  56.3 17.5 %collective-permute-start.9 = (bf16[64,512]{1,0:T(8,128)(2,1)S(1)}, bf16[64,512]{1,0:T(8,128)(2,1)S(1)}, u32[]{:S(2)}, u32[]{:S(2)}) collective-permute-start(bf16[64,512]{1,0:T(8,128)(2,1)S(1)} %get-tuple-element.40), channel_id=1, source_target_pairs={{0,3},{1,4},{2,5},{3,6},{4,7},{5,0},{6,1},{7,2},{8,11},{9,12},{10,... | collective-permute-start | bytes 196616 | tf_op jit(solution)/shard_map/ppermute | solution.py:232
  61.2 12.6 %collective-permute-start.8 = (bf16[64,512]{1,0:T(8,128)(2,1)S(1)}, bf16[64,512]{1,0:T(8,128)(2,1)S(1)}, u32[]{:S(2)}, u32[]{:S(2)}) collective-permute-start(bf16[64,512]{1,0:T(8,128)(2,1)S(1)} %get-tuple-element.41), channel_id=1, source_target_pairs={{0,2},{1,3},{2,4},{3,5},{4,6},{5,7},{6,0},{7,1},{8,10},{9,11},{10,... | collective-permute-start | bytes 196616 | tf_op jit(solution)/shard_map/ppermute | solution.py:232
  66.7 34.3 %copy-start.6 = (bf16[64,512]{1,0:T(8,128)(2,1)}, bf16[64,512]{1,0:T(8,128)(2,1)S(1)}, u32[]{:S(2)}) copy-start(bf16[64,512]{1,0:T(8,128)(2,1)S(1)} %collective-permute-done.13.refs_7_.refs_15_) | copy-start | bytes 196612
  66.7 7.1 %collective-permute-start.7 = (bf16[64,512]{1,0:T(8,128)(2,1)S(1)}, bf16[64,512]{1,0:T(8,128)(2,1)S(1)}, u32[]{:S(2)}, u32[]{:S(2)}) collective-permute-start(bf16[64,512]{1,0:T(8,128)(2,1)S(1)} %get-tuple-element.42), channel_id=1, source_target_pairs={{0,1},{1,2},{2,3},{3,4},{4,5},{5,6},{6,7},{7,0},{8,9},{9,10},{10,1... | collective-permute-start | bytes 196616 | tf_op jit(solution)/shard_map/ppermute | solution.py:232
  69.8 31.2 %copy-start.7 = (bf16[64,512]{1,0:T(8,128)(2,1)}, bf16[64,512]{1,0:T(8,128)(2,1)S(1)}, u32[]{:S(2)}) copy-start(bf16[64,512]{1,0:T(8,128)(2,1)S(1)} %collective-permute-done.11.refs_5_.refs_13_) | copy-start | bytes 196612
  69.8 6.3 %collective-permute-start.12 = (bf16[64,512]{1,0:T(8,128)(2,1)S(1)}, bf16[64,512]{1,0:T(8,128)(2,1)S(1)}, u32[]{:S(2)}, u32[]{:S(2)}) collective-permute-start(bf16[64,512]{1,0:T(8,128)(2,1)S(1)} %get-tuple-element.44), channel_id=1, source_target_pairs={{0,6},{1,7},{2,0},{3,1},{4,2},{5,3},{6,4},{7,5},{8,14},{9,15},{10,... | collective-permute-start | bytes 196616 | tf_op jit(solution)/shard_map/ppermute | solution.py:232
  73.8 27.2 %copy-start.8 = (bf16[64,512]{1,0:T(8,128)(2,1)}, bf16[64,512]{1,0:T(8,128)(2,1)S(1)}, u32[]{:S(2)}) copy-start(bf16[64,512]{1,0:T(8,128)(2,1)S(1)} %collective-permute-done.10.refs_4_.refs_12_) | copy-start | bytes 196612
  73.8 27.2 %copy-start.9 = (bf16[64,512]{1,0:T(8,128)(2,1)}, bf16[64,512]{1,0:T(8,128)(2,1)S(1)}, u32[]{:S(2)}) copy-start(bf16[64,512]{1,0:T(8,128)(2,1)S(1)} %collective-permute-done.9.refs_3_.refs_11_) | copy-start | bytes 196612
  73.8 27.2 %copy-start.10 = (bf16[64,512]{1,0:T(8,128)(2,1)}, bf16[64,512]{1,0:T(8,128)(2,1)S(1)}, u32[]{:S(2)}) copy-start(bf16[64,512]{1,0:T(8,128)(2,1)S(1)} %collective-permute-done.8.refs_2_.refs_10_) | copy-start | bytes 196612
  73.8 27.2 %copy-start.11 = (bf16[64,512]{1,0:T(8,128)(2,1)}, bf16[64,512]{1,0:T(8,128)(2,1)S(1)}, u32[]{:S(2)}) copy-start(bf16[64,512]{1,0:T(8,128)(2,1)S(1)} %collective-permute-done.7.refs_1_.refs_9_) | copy-start | bytes 196612
  76.1 24.9 %copy-start.12 = (bf16[64,512]{1,0:T(8,128)(2,1)}, bf16[64,512]{1,0:T(8,128)(2,1)S(1)}, u32[]{:S(2)}) copy-start(bf16[64,512]{1,0:T(8,128)(2,1)S(1)} %collective-permute-done.12.refs_6_.refs_14_) | copy-start | bytes 196612
  101.0 1.3 copy-start.1
  114.9 76.6 %all-to-all-start.2 = ((bf16[64,128,128]{2,1,0:T(8,128)(2,1)}), bf16[64,128,128]{2,1,0:T(8,128)(2,1)S(1)}, u32[]{:S(2)}, u32[]{:S(2)}) async-start(bf16[64,128,128]{2,1,0:T(8,128)(2,1)} %bitcast.35), calls=%async_computation.2 | async-start | bytes 4194304 | tf_op jit(solution)/shard_map/all_to_all | solution.py:292
  127.2 13.3 %collective-permute-start = (bf16[4,256,128]{2,1,0:T(8,128)(2,1)S(1)}, bf16[4,256,128]{2,1,0:T(8,128)(2,1)S(1)}, u32[]{:S(2)}, u32[]{:S(2)}) collective-permute-start(bf16[4,256,128]{2,1,0:T(8,128)(2,1)S(1)} %get-tuple-element.28), channel_id=1, source_target_pairs={{0,8},{8,128},{128,136},{136,256},{256,264},{264,384},{384,392},{3... | collective-permute-start | bytes 786440 | tf_op jit(solution)/shard_map/ppermute | solution.py:297
  128.8 17.8 %collective-permute-start.1 = (bf16[4,256,128]{2,1,0:T(8,128)(2,1)S(1)}, bf16[4,256,128]{2,1,0:T(8,128)(2,1)S(1)}, u32[]{:S(2)}, u32[]{:S(2)}) collective-permute-start(bf16[4,256,128]{2,1,0:T(8,128)(2,1)S(1)} %get-tuple-element.27), channel_id=1, source_target_pairs={{0,128},{8,136},{128,256},{136,264},{256,384},{264,392},{384,0},{3... | collective-permute-start | bytes 786440 | tf_op jit(solution)/shard_map/ppermute | solution.py:297
  133.0 39.4 %collective-permute-start.6 = (bf16[4,256,128]{2,1,0:T(8,128)(2,1)S(1)}, bf16[4,256,128]{2,1,0:T(8,128)(2,1)S(1)}, u32[]{:S(2)}, u32[]{:S(2)}) collective-permute-start(bf16[4,256,128]{2,1,0:T(8,128)(2,1)S(1)} %get-tuple-element.22), channel_id=1, source_target_pairs={{0,392},{8,0},{128,8},{136,128},{256,136},{264,256},{384,264},{392... | collective-permute-start | bytes 786440 | tf_op jit(solution)/shard_map/ppermute | solution.py:297
  133.0 39.4 %collective-permute-start.5 = (bf16[4,256,128]{2,1,0:T(8,128)(2,1)S(1)}, bf16[4,256,128]{2,1,0:T(8,128)(2,1)S(1)}, u32[]{:S(2)}, u32[]{:S(2)}) collective-permute-start(bf16[4,256,128]{2,1,0:T(8,128)(2,1)S(1)} %get-tuple-element.23), channel_id=1, source_target_pairs={{0,384},{8,392},{128,0},{136,8},{256,128},{264,136},{384,256},{392... | collective-permute-start | bytes 786440 | tf_op jit(solution)/shard_map/ppermute | solution.py:297
  136.3 36.0 %collective-permute-start.4 = (bf16[4,256,128]{2,1,0:T(8,128)(2,1)S(1)}, bf16[4,256,128]{2,1,0:T(8,128)(2,1)S(1)}, u32[]{:S(2)}, u32[]{:S(2)}) collective-permute-start(bf16[4,256,128]{2,1,0:T(8,128)(2,1)S(1)} %get-tuple-element.24), channel_id=1, source_target_pairs={{0,264},{8,384},{128,392},{136,0},{256,8},{264,128},{384,136},{392... | collective-permute-start | bytes 786440 | tf_op jit(solution)/shard_map/ppermute | solution.py:297
  140.5 22.1 %collective-permute-start.2 = (bf16[4,256,128]{2,1,0:T(8,128)(2,1)S(1)}, bf16[4,256,128]{2,1,0:T(8,128)(2,1)S(1)}, u32[]{:S(2)}, u32[]{:S(2)}) collective-permute-start(bf16[4,256,128]{2,1,0:T(8,128)(2,1)S(1)} %get-tuple-element.26), channel_id=1, source_target_pairs={{0,136},{8,256},{128,264},{136,384},{256,392},{264,0},{384,8},{392... | collective-permute-start | bytes 786440 | tf_op jit(solution)/shard_map/ppermute | solution.py:297
  146.7 25.6 %collective-permute-start.3 = (bf16[4,256,128]{2,1,0:T(8,128)(2,1)S(1)}, bf16[4,256,128]{2,1,0:T(8,128)(2,1)S(1)}, u32[]{:S(2)}, u32[]{:S(2)}) collective-permute-start(bf16[4,256,128]{2,1,0:T(8,128)(2,1)S(1)} %get-tuple-element.25), channel_id=1, source_target_pairs={{0,256},{8,264},{128,384},{136,392},{256,0},{264,8},{384,128},{392... | collective-permute-start | bytes 786440 | tf_op jit(solution)/shard_map/ppermute | solution.py:297
  172.5 1.4 copy-start
  191.5 1.3 copy-start.2
  192.8 12.0 %copy-start.5 = (bf16[512,512]{1,0:T(8,128)(2,1)S(1)}, bf16[512,512]{1,0:T(8,128)(2,1)}, u32[]{:S(2)}) copy-start(bf16[512,512]{1,0:T(8,128)(2,1)} %get-tuple-element.16) | copy-start | bytes 1572868
  192.8 63.2 %all-to-all-start.3 = ((bf16[64,128,128]{2,1,0:T(8,128)(2,1)}), bf16[64,128,128]{2,1,0:T(8,128)(2,1)S(1)}, u32[]{:S(2)}, u32[]{:S(2)}) async-start(bf16[64,128,128]{2,1,0:T(8,128)(2,1)} %bitcast.34), calls=%async_computation.3 | async-start | bytes 4194304 | tf_op jit(solution)/shard_map/all_to_all | solution.py:292
  205.5 24.2 %collective-permute-start.20 = (bf16[64,512]{1,0:T(8,128)(2,1)S(1)}, bf16[64,512]{1,0:T(8,128)(2,1)S(1)}, u32[]{:S(2)}, u32[]{:S(2)}) collective-permute-start(bf16[64,512]{1,0:T(8,128)(2,1)S(1)} %get-tuple-element.29), channel_id=1, source_target_pairs={{0,7},{1,0},{2,1},{3,2},{4,3},{5,4},{6,5},{7,6},{8,15},{9,8},{10,9... | collective-permute-start | bytes 196616 | tf_op jit(solution)/shard_map/ppermute | solution.py:232
  216.4 16.5 %collective-permute-start.19 = (bf16[64,512]{1,0:T(8,128)(2,1)S(1)}, bf16[64,512]{1,0:T(8,128)(2,1)S(1)}, u32[]{:S(2)}, u32[]{:S(2)}) collective-permute-start(bf16[64,512]{1,0:T(8,128)(2,1)S(1)} %get-tuple-element.30), channel_id=1, source_target_pairs={{0,6},{1,7},{2,0},{3,1},{4,2},{5,3},{6,4},{7,5},{8,14},{9,15},{10,... | collective-permute-start | bytes 196616 | tf_op jit(solution)/shard_map/ppermute | solution.py:232
  218.6 17.6 %collective-permute-start.18 = (bf16[64,512]{1,0:T(8,128)(2,1)S(1)}, bf16[64,512]{1,0:T(8,128)(2,1)S(1)}, u32[]{:S(2)}, u32[]{:S(2)}) collective-permute-start(bf16[64,512]{1,0:T(8,128)(2,1)S(1)} %get-tuple-element.31), channel_id=1, source_target_pairs={{0,5},{1,6},{2,7},{3,0},{4,1},{5,2},{6,3},{7,4},{8,13},{9,14},{10,... | collective-permute-start | bytes 196616 | tf_op jit(solution)/shard_map/ppermute | solution.py:232
  220.5 15.7 %collective-permute-start.17 = (bf16[64,512]{1,0:T(8,128)(2,1)S(1)}, bf16[64,512]{1,0:T(8,128)(2,1)S(1)}, u32[]{:S(2)}, u32[]{:S(2)}) collective-permute-start(bf16[64,512]{1,0:T(8,128)(2,1)S(1)} %get-tuple-element.32), channel_id=1, source_target_pairs={{0,4},{1,5},{2,6},{3,7},{4,0},{5,1},{6,2},{7,3},{8,12},{9,13},{10,... | collective-permute-start | bytes 196616 | tf_op jit(solution)/shard_map/ppermute | solution.py:232
  227.8 8.5 %collective-permute-start.16 = (bf16[64,512]{1,0:T(8,128)(2,1)S(1)}, bf16[64,512]{1,0:T(8,128)(2,1)S(1)}, u32[]{:S(2)}, u32[]{:S(2)}) collective-permute-start(bf16[64,512]{1,0:T(8,128)(2,1)S(1)} %get-tuple-element.33), channel_id=1, source_target_pairs={{0,3},{1,4},{2,5},{3,6},{4,7},{5,0},{6,1},{7,2},{8,11},{9,12},{10,... | collective-permute-start | bytes 196616 | tf_op jit(solution)/shard_map/ppermute | solution.py:232
  229.7 11.7 %copy-start.13 = (bf16[64,512]{1,0:T(8,128)(2,1)}, bf16[64,512]{1,0:T(8,128)(2,1)S(1)}, u32[]{:S(2)}) copy-start(bf16[64,512]{1,0:T(8,128)(2,1)S(1)} %collective-permute-done.20.refs_7_) | copy-start | bytes 196612
  229.8 10.1 %collective-permute-start.15 = (bf16[64,512]{1,0:T(8,128)(2,1)S(1)}, bf16[64,512]{1,0:T(8,128)(2,1)S(1)}, u32[]{:S(2)}, u32[]{:S(2)}) collective-permute-start(bf16[64,512]{1,0:T(8,128)(2,1)S(1)} %get-tuple-element.34), channel_id=1, source_target_pairs={{0,2},{1,3},{2,4},{3,5},{4,6},{5,7},{6,0},{7,1},{8,10},{9,11},{10,... | collective-permute-start | bytes 196616 | tf_op jit(solution)/shard_map/ppermute | solution.py:232
  232.9 8.6 %copy-start.14 = (bf16[64,512]{1,0:T(8,128)(2,1)}, bf16[64,512]{1,0:T(8,128)(2,1)S(1)}, u32[]{:S(2)}) copy-start(bf16[64,512]{1,0:T(8,128)(2,1)S(1)} %collective-permute-done.19.refs_6_) | copy-start | bytes 196612
  232.9 8.6 %collective-permute-start.14 = (bf16[64,512]{1,0:T(8,128)(2,1)S(1)}, bf16[64,512]{1,0:T(8,128)(2,1)S(1)}, u32[]{:S(2)}, u32[]{:S(2)}) collective-permute-start(bf16[64,512]{1,0:T(8,128)(2,1)S(1)} %get-tuple-element.35), channel_id=1, source_target_pairs={{0,1},{1,2},{2,3},{3,4},{4,5},{5,6},{6,7},{7,0},{8,9},{9,10},{10,1... | collective-permute-start | bytes 196616 | tf_op jit(solution)/shard_map/ppermute | solution.py:232
  236.2 5.2 %copy-start.15 = (bf16[64,512]{1,0:T(8,128)(2,1)}, bf16[64,512]{1,0:T(8,128)(2,1)S(1)}, u32[]{:S(2)}) copy-start(bf16[64,512]{1,0:T(8,128)(2,1)S(1)} %collective-permute-done.18.refs_5_) | copy-start | bytes 196612
  236.3 5.2 %copy-start.16 = (bf16[64,512]{1,0:T(8,128)(2,1)}, bf16[64,512]{1,0:T(8,128)(2,1)S(1)}, u32[]{:S(2)}) copy-start(bf16[64,512]{1,0:T(8,128)(2,1)S(1)} %collective-permute-done.17.refs_4_) | copy-start | bytes 196612
  236.3 5.2 %copy-start.17 = (bf16[64,512]{1,0:T(8,128)(2,1)}, bf16[64,512]{1,0:T(8,128)(2,1)S(1)}, u32[]{:S(2)}) copy-start(bf16[64,512]{1,0:T(8,128)(2,1)S(1)} %collective-permute-done.16.refs_3_) | copy-start | bytes 196612
  239.9 1.6 copy-start.18
  241.5 0.6 copy-start.19
  256.0 1.3 copy-start.3
Sparse Core Ops, SparseCore 0:
  42.9 55.3 all-gather.1

commit v4 on v3

--- a/solution.py
+++ b/solution.py
@@ -56,11 +56,16 @@
         out_ref[pl.ds(pl.multiple_of(source * rows, rows), rows), :] = share[...]
 
 
-def tile_of(parts):
-    rows = parts[0].shape[-2] // CORES
-    return jnp.concatenate(
-        [part[0, 0, p * rows : (p + 1) * rows] for p in range(CORES) for part in parts], axis=0
-    )
+def tile_of(ref):
+    return ref[...].reshape(-1, ref.shape[-1])
+
+
+def store_pieces(out_ref, block, part):
+    count, rows = out_ref.shape[1:3]
+    for c in range(CORES):
+        for p in range(count // CORES):
+            at = (c * (count // CORES) + p) * rows
+            out_ref[block, p * CORES + c] = part[at : at + rows]
 
 
 def assemble_kernel(me_ref, *refs):
@@ -95,7 +100,7 @@
     scores_ref[0] = near
     top = jnp.max(near, axis=0, keepdims=True)
     for j in range(picks):
-        far = dot(far_k[j][0], q, NT)
+        far = dot(tile_of(far_k[j]), q, NT)
         scores_ref[j + 1] = far
         top = jnp.maximum(top, jnp.max(far, axis=0, keepdims=True))
     total = jnp.zeros((1, rows), jnp.float32)
@@ -114,16 +119,20 @@
         if j == 0:
             near_ref[...] = part
         else:
-            far_ref[sel_ref[head * picks + j - 1]] = part
+            block = sel_ref[head * picks + j - 1]
+            own_x, rows_core = far_ref.shape[2:4]
+            for c in range(CORES):
+                far_ref[block // own_x, c, lax.rem(block, own_x)] = part[
+                    c * rows_core : (c + 1) * rows_core
+                ]
 
 
 def other_grads_kernel(
     sel_ref, lens_ref, base_ref, q_ref, k_ref, v_ref,
-    k1_ref, k2_ref, k3_ref, *refs,
+    k1_ref, k2_ref, k3_ref, v1_ref, v2_ref, v3_ref, top_ref, inverse_ref, *refs,
 ):
-    *far_v, top_ref, inverse_ref = refs[:8]
-    *shares, attended_ref, query_ref, near_ref, far_ref, start_ref, weights_ref, g_ref = refs[8:]
-    far_k = (k1_ref, k2_ref, k3_ref)
+    *shares, attended_ref, query_ref, near_ref, far_ref, start_ref, weights_ref, g_ref = refs
+    far_k, far_v = (k1_ref, k2_ref, k3_ref), (v1_ref, v2_ref, v3_ref)
     head = pl.program_id(0)
     rows, width = q_ref.shape
     picks = weights_ref.shape[0] - 1
@@ -134,10 +143,10 @@
         start_ref[...] = document_starts(lens_ref, base_ref, rows)
 
     def keys_of(j):
-        return k_ref[...] if j == 0 else far_k[j - 1][0]
+        return k_ref[...] if j == 0 else tile_of(far_k[j - 1])
 
     def values_of(j):
-        return v_ref[...] if j == 0 else tile_of(far_v[2 * j - 2 : 2 * j])
+        return v_ref[...] if j == 0 else tile_of(far_v[j - 1])
 
     in_token_order(base_ref[1], shares, g_ref)
     q = q_ref[...]
@@ -165,7 +174,7 @@
         if j == 0:
             near_ref[...] = part
         else:
-            far_ref[sel_ref[head * picks + j - 1]] = part
+            store_pieces(far_ref, sel_ref[head * picks + j - 1], part)
         query_grad = query_grad + dot(keys_of(j).T, score_grads, NN)
     query_ref[...] = query_grad.astype(jnp.bfloat16).T
 
@@ -193,21 +202,55 @@
             out_ref[:, h * width : (h + 1) * width] = total_ref[h].astype(out_ref.dtype)
 
 
-def pack(codes, context, groups, width):
+def pack(codes, context, half, groups, width, *after):
     slots = codes.shape[0]
-    rows = context.shape[0] // groups
+    rows, columns = context.shape[0], context.shape[1] // 2
     steps = 4
     return pl.pallas_call(
         pack_kernel,
-        out_shape=jax.ShapeDtypeStruct((slots, rows, width), context.dtype),
+        out_shape=jax.ShapeDtypeStruct((slots, rows // groups, width), context.dtype),
         grid_spec=pltpu.PrefetchScalarGridSpec(
             num_scalar_prefetch=1,
             grid=(steps,),
-            in_specs=[pl.BlockSpec(context.shape, lambda i, *_: (0, 0))],
-            out_specs=pl.BlockSpec((slots // steps, rows, width), lambda i, *_: (i, 0, 0)),
+            in_specs=[pl.BlockSpec((rows, columns), lambda i, *_: (0, half))]
+            + [pl.BlockSpec(memory_space=pl.ANY)] * len(after),
+            out_specs=pl.BlockSpec((slots // steps, rows // groups, width), lambda i, *_: (i, 0, 0)),
         ),
         compiler_params=pltpu.CompilerParams(vmem_limit_bytes=VMEM_BYTES),
-    )(codes, context)
+    )(codes, context, *after)
+
+
+def row_sum_kernel(codes_ref, terms_ref, out_ref, total_ref):
+    block = pl.program_id(0)
+    sources, _, rows, width = terms_ref.shape
+    heads = total_ref.shape[0] - 1
+    total_ref[...] = jnp.zeros_like(total_ref)
+
+    def step(s, carry):
+        code = codes_ref[s * pl.num_programs(0) + block]
+        slot = jnp.where(code >= 0, code, heads)
+        total_ref[slot] += terms_ref[s, 0].astype(jnp.float32)
+        return carry
+
+    lax.fori_loop(0, sources, step, 0)
+    for h in range(heads):
+        out_ref[:, h * width : (h + 1) * width] = total_ref[h].astype(out_ref.dtype)
+
+
+def row_sum(codes, terms, heads):
+    sources, blocks, rows, width = terms.shape
+    return pl.pallas_call(
+        row_sum_kernel,
+        out_shape=jax.ShapeDtypeStruct((blocks * rows, heads * width), terms.dtype),
+        grid_spec=pltpu.PrefetchScalarGridSpec(
+            num_scalar_prefetch=1,
+            grid=(blocks,),
+            in_specs=[pl.BlockSpec((sources, 1, rows, width), lambda i, *_: (0, i, 0, 0))],
+            out_specs=pl.BlockSpec((rows, heads * width), lambda i, *_: (i, 0)),
+            scratch_shapes=[pltpu.VMEM((heads + 1, rows, width), jnp.float32)],
+        ),
+        compiler_params=pltpu.CompilerParams(vmem_limit_bytes=VMEM_BYTES),
+    )(codes, terms)
 
 
 def collect(codes, terms, heads):
@@ -254,7 +297,9 @@
     blocks = owners // pieces
     my_x, my_y = lax.axis_index("x"), lax.axis_index("y")
     my_piece = lax.axis_index(CTX).astype(jnp.int32)
-    column_values = lax.all_gather(context_values, "y", axis=0, tiled=True)
+    column = lax.all_gather(
+        jnp.concatenate([context_keys, context_values], axis=1), "y", axis=0, tiled=True
+    )
     count = lax.axis_size("head")
     me = lax.axis_index("head").astype(jnp.int32)
     share_rows = rows // count
@@ -267,6 +312,7 @@
         ],
         count,
     )
+    base = jnp.stack([my_piece * rows, me])
     flat = selected.reshape(-1)
 
     head_of = jnp.arange(heads * picks, dtype=jnp.int32) // picks
@@ -276,49 +322,42 @@
     codes = lax.all_to_all(wanted, CTX, split_axis=0, concat_axis=0, tiled=True)
     piece_codes = lax.dynamic_slice_in_dim(codes, my_piece // pieces, 1, 1)[:, 0]
     own_x = blocks // SIZE_X
-    peers = SIZE_X * CORES
-    me_row = (my_x * CORES + lax.axis_index("core")).astype(jnp.int32)
-    base = jnp.stack([my_piece * rows, me, me_row])
     row_codes = lax.dynamic_slice(
         codes.reshape(SIZE_X, SIZE_Y, CORES, 128),
         (0, my_y, 0, my_x * own_x),
         (SIZE_X, 1, CORES, own_x),
-    ).reshape(peers, own_x)
-    row_codes = jnp.concatenate([row_codes, row_codes])
-    row_codes = lax.dynamic_slice_in_dim(row_codes, me_row, peers, 0).reshape(-1)
+    ).reshape(-1)
+    peers = SIZE_X * CORES
+
+    row_shape = (SIZE_X, CORES, own_x, rows // CORES, width)
+
+    def along_row(tiles):
+        tiles = tiles.reshape(peers, own_x, rows // CORES, width)
+        received = lax.all_to_all(tiles, ("x", "core"), split_axis=0, concat_axis=0, tiled=True)
+        return received.reshape(row_shape)
 
     def to_holders(tiles):
         tiles = tiles.reshape(owners, piece_rows, width)
         return lax.all_to_all(tiles, CTX, split_axis=0, concat_axis=0, tiled=True)
 
-    far_keys = to_holders(pack(piece_codes, context_keys, 1, width)).reshape(blocks, rows, width)
-    sent = pack(row_codes, column_values, own_x, width).reshape(peers, own_x, rows // CORES, width)
-    far_values = [sent[0]] + [
-        lax.ppermute(sent[d], ("x", "core"), [(i, (i + d) % peers) for i in range(peers)])
-        for d in range(1, peers)
-    ]
-    far_values = jnp.stack(far_values)
+    early = count - 1
+    far_keys = along_row(pack(row_codes, column, 0, own_x, width, *grads[1:early]))
+    far_values = along_row(pack(row_codes, column, 1, own_x, width, *grads[early:]))
 
     by_head = pl.BlockSpec((rows, width), lambda h, *_: (0, h))
-    all_far = pl.BlockSpec((blocks, rows, width), lambda h, *_: (0, 0, 0))
-    far_key = [
-        pl.BlockSpec((1, rows, width), lambda h, sel, *_, j=j: (sel[h * picks + j], 0, 0))
+    all_rows = pl.BlockSpec(row_shape, lambda h, *_: (0, 0, 0, 0, 0))
+    all_far = pl.BlockSpec((blocks, pieces, piece_rows, width), lambda h, *_: (0, 0, 0, 0))
+    far = [
+        pl.BlockSpec(
+            (1, CORES, 1, rows // CORES, width),
+            lambda h, sel, *_, j=j: (sel[h * picks + j] // own_x, 0, sel[h * picks + j] % own_x, 0, 0),
+        )
         for j in range(picks)
     ]
-
-    def value_at(j, c):
-        def index(h, sel, lens, base):
-            block = sel[h * picks + j]
-            source = (block // own_x) * CORES + c
-            return (lax.rem(base[2] + peers - source, peers), lax.rem(block, own_x), 0, 0)
-
-        return pl.BlockSpec((1, 1, rows // CORES, width), index)
-
-    far_value = [value_at(j, c) for j in range(picks) for c in range(CORES)]
     shares = [pl.BlockSpec((share_rows, width), lambda h, *_: (0, h))] * count
     by_stat = pl.BlockSpec((1, 1, rows), lambda h, *_: (h, 0, 0))
     near_shape = jax.ShapeDtypeStruct(queries.shape, jnp.bfloat16)
-    far_shape = jax.ShapeDtypeStruct((blocks, rows, width), jnp.bfloat16)
+    far_shape = jax.ShapeDtypeStruct((blocks, pieces, piece_rows, width), jnp.bfloat16)
     stat_shape = jax.ShapeDtypeStruct((heads, 1, rows), jnp.float32)
     scratch = [
         pltpu.VMEM((1, rows), jnp.int32),
@@ -328,12 +367,17 @@
     tile_flops = 2 * rows * rows * width * (picks + 1) * heads
     value_grad, far_value_grads, top, inverse = pl.pallas_call(
         value_grad_kernel,
-        out_shape=(near_shape, far_shape, stat_shape, stat_shape),
+        out_shape=(
+            near_shape,
+            jax.ShapeDtypeStruct(row_shape, jnp.bfloat16),
+            stat_shape,
+            stat_shape,
+        ),
         grid_spec=pltpu.PrefetchScalarGridSpec(
             num_scalar_prefetch=3,
             grid=(heads,),
-            in_specs=[by_head, by_head, *far_key, *shares],
-            out_specs=[by_head, all_far, by_stat, by_stat],
+            in_specs=[by_head, by_head, *far, *shares],
+            out_specs=[by_head, all_rows, by_stat, by_stat],
             scratch_shapes=scratch,
         ),
         compiler_params=pltpu.CompilerParams(vmem_limit_bytes=VMEM_BYTES),
@@ -341,7 +385,9 @@
             flops=2 * tile_flops, bytes_accessed=8 << 20, transcendentals=heads * 4 * rows * rows
         ),
     )(flat, doc_lengths, base, queries, keys, *[far_keys] * picks, *grads)
-    value_terms = to_holders(far_value_grads)
+    value_terms = along_row(gate(far_value_grads, far_values))
+    value_sums = row_sum(row_codes, value_terms.reshape(peers, *row_shape[2:]), heads)
+    context_value_grad = lax.psum_scatter(value_sums, "y", scatter_dimension=0, tiled=True)
 
     attended, query_grad, key_grad, far_key_grads = pl.pallas_call(
         other_grads_kernel,
@@ -349,7 +395,7 @@
         grid_spec=pltpu.PrefetchScalarGridSpec(
             num_scalar_prefetch=3,
             grid=(heads,),
-            in_specs=[by_head, by_head, by_head, *far_key, *far_value, by_stat, by_stat, *shares],
+            in_specs=[by_head, by_head, by_head, *far, *far, by_stat, by_stat, *shares],
             out_specs=[by_head, by_head, by_head, all_far],
             scratch_shapes=scratch,
         ),
@@ -359,7 +405,7 @@
         ),
     )(
         flat, doc_lengths, base, queries, keys, values,
-        *[far_keys] * picks, *[far_values] * len(far_value), top, inverse, *grads,
+        *[far_keys] * picks, *[far_values] * picks, top, inverse, *grads,
     )
     key_terms = to_holders(gate(far_key_grads, value_terms))
 
@@ -377,7 +423,6 @@
         + [pl.BlockSpec(memory_space=pltpu.VMEM)] * count,
         out_specs=pl.BlockSpec(memory_space=pltpu.VMEM),
     )(me.reshape(1), *output_parts)
-    context_value_grad = collect(piece_codes, value_terms, heads)
     context_key_grad = collect(piece_codes, key_terms, heads)
     return output_rows, query_grad, key_grad, value_grad, context_key_grad, context_value_grad
 

time: 270 us -> 242 us (0.90)
  starting transfers between devices: 127 us -> 96.2 us
    all_to_all x0 -> x3, waiting for transfers between devices: none -> 36.6 us  [along_row(): lax.all_to_all(tiles, ('x', 'core'), split_axis=0, concat_axis=0, tiled=T...]
    ppermute x7 -> x0, starting transfers between devices: 30 us -> none  [on_device(): lax.ppermute(sent[d], ('x', 'core'), [(i, (i + d) % peers) for i in range...]
    all_to_all x0 -> x3, starting transfers between devices: none -> 16.3 us  [along_row(): lax.all_to_all(tiles, ('x', 'core'), split_axis=0, concat_axis=0, tiled=T...]
    all_to_all x3 -> x1, starting transfers between devices: 22.6 us -> 7.45 us  [to_holders(): return lax.all_to_all(tiles, CTX, split_axis=0, concat_axis=0, tiled=True)]
    ppermute x7 -> x0, waiting for transfers between devices: 13.9 us -> none  [on_device(): lax.ppermute(sent[d], ('x', 'core'), [(i, (i + d) % peers) for i in range...]
    all_to_all x3 -> x1, waiting for transfers between devices: 32.7 us -> 21.6 us  [to_holders(): return lax.all_to_all(tiles, CTX, split_axis=0, concat_axis=0, tiled=True)]
    all_to_all x1, waiting for transfers between devices: 9.18 us -> 0.01 us  [on_device(): codes = lax.all_to_all(wanted, CTX, split_axis=0, concat_axis=0, tiled=True)]
    pallas_call x3 -> x4, Pallas kernels: 20 us -> 25.3 us  [the longest x1 12.7 us: on_device(): pl.pallas_call(value_grad_kernel, out_shape=(near_shape, jax.ShapeDtypeSt...]
  transfers between devices with their start and end apart: 26 -> 21, of which waited for: 9 -> 10; matrix products, arithmetic and copies ran while one was open for 2% -> 3% of each run, Pallas kernels for 15% -> 19%
where the time goes in v4:
time: 242 us; the launch traced here: 241 us
  starting transfers between devices  96.2 us (40%)
  waiting for transfers between devices  65.7 us (27%)
  Pallas kernels  48.7 us (20%)
  between operations  14.5 us (6%)
  local copies, waits for them, and re-layouts  13.7 us (6%)
    ppermute x14, starting transfers between devices, shifted(): lax.ppermute(parts[d], 'head', [(i, (i + d) % count) for i in range(count)])  61.3 us
    all_to_all x3, waiting for transfers between devices, along_row(): lax.all_to_all(tiles, ('x', 'core'), split_axis=0, concat_axis=0, tiled=T...  36.6 us
    all_to_all x1, waiting for transfers between devices, to_holders(): return lax.all_to_all(tiles, CTX, split_axis=0, concat_axis=0, tiled=True)  21.6 us
    pallas_call x1, Pallas kernels, on_device(): pl.pallas_call(other_grads_kernel, out_shape=(near_shape, near_shape, nea...  17.4 us
    all_to_all x3, starting transfers between devices, along_row(): lax.all_to_all(tiles, ('x', 'core'), split_axis=0, concat_axis=0, tiled=T...  16.3 us
    pallas_call x1, Pallas kernels, on_device(): pl.pallas_call(value_grad_kernel, out_shape=(near_shape, jax.ShapeDtypeSt...  12.7 us
    all_to_all x1, starting transfers between devices, on_device(): codes = lax.all_to_all(wanted, CTX, split_axis=0, concat_axis=0, tiled=True)  11.1 us
    unnamed x41, local copies, waits for them, and re-layouts  7.93 us
  transfers between devices with their start and end apart: 21, of which 10 were waited for; matrix products, arithmetic and copies ran while one was open for 3% of the time, Pallas kernels for 19%

profile of v4, /device:TPU:1, one launch (start us, length us, event | category | flops | bytes accessed | tf_op | source)
XLA Modules:
  0.0 241.2 jit_solution(14436664801288756207)
XLA Ops:
  7.2 1.7 pad_maximum_fusion
  9.0 1.8 constant_dynamic-slice_fusion.8
  10.8 11.5 %collective-permute-start.5 = (bf16[64,512]{1,0:T(8,128)(2,1)S(1)}, bf16[64,512]{1,0:T(8,128)(2,1)S(1)}, u32[]{:S(2)}, u32[]{:S(2)}) collective-permute-start(bf16[64,512]{1,0:T(8,128)(2,1)S(1)} %get-tuple-element.31), channel_id=1, source_target_pairs={{0,6},{1,7},{2,0},{3,1},{4,2},{5,3},{6,4},{7,5},{8,14},{9,15},{10,... | collective-permute-start | bytes 196616 | tf_op jit(solution)/shard_map/ppermute | solution.py:275
  22.2 0.8 copy.21
  23.2 0.6 broadcast_in_dim.19
  23.9 11.1 %all-to-all-start = ((s32[64,1,128]{2,1,0:T(1,128)}), s32[64,1,128]{2,1,0:T(1,128)S(1)}, u32[]{:S(2)}, u32[]{:S(2)}) async-start(s32[64,1,128]{2,1,0:T(1,128)} %broadcast_in_dim.19), calls=%async_computation | async-start | bytes 65536 | tf_op jit(solution)/shard_map/all_to_all | solution.py:322
  35.0 1.9 collective-permute-start.4
  36.9 7.3 %collective-permute-start.3 = (bf16[64,512]{1,0:T(8,128)(2,1)S(1)}, bf16[64,512]{1,0:T(8,128)(2,1)S(1)}, u32[]{:S(2)}, u32[]{:S(2)}) collective-permute-start(bf16[64,512]{1,0:T(8,128)(2,1)S(1)} %get-tuple-element.33), channel_id=1, source_target_pairs={{0,4},{1,5},{2,6},{3,7},{4,0},{5,1},{6,2},{7,3},{8,12},{9,13},{10,... | collective-permute-start | bytes 196616 | tf_op jit(solution)/shard_map/ppermute | solution.py:275
  44.2 1.9 collective-permute-start.2
  46.1 3.3 %collective-permute-start.1 = (bf16[64,512]{1,0:T(8,128)(2,1)S(1)}, bf16[64,512]{1,0:T(8,128)(2,1)S(1)}, u32[]{:S(2)}, u32[]{:S(2)}) collective-permute-start(bf16[64,512]{1,0:T(8,128)(2,1)S(1)} %get-tuple-element.35), channel_id=1, source_target_pairs={{0,2},{1,3},{2,4},{3,5},{4,6},{5,7},{6,0},{7,1},{8,10},{9,11},{10,... | collective-permute-start | bytes 196616 | tf_op jit(solution)/shard_map/ppermute | solution.py:275
  49.5 3.1 %collective-permute-start = (bf16[64,512]{1,0:T(8,128)(2,1)S(1)}, bf16[64,512]{1,0:T(8,128)(2,1)S(1)}, u32[]{:S(2)}, u32[]{:S(2)}) collective-permute-start(bf16[64,512]{1,0:T(8,128)(2,1)S(1)} %get-tuple-element.36), channel_id=1, source_target_pairs={{0,1},{1,2},{2,3},{3,4},{4,5},{5,6},{6,7},{7,0},{8,9},{9,10},{10,1... | collective-permute-start | bytes 196616 | tf_op jit(solution)/shard_map/ppermute | solution.py:275
  52.7 0.7 reshape.69.codes_ref
  53.3 2.0 collective-permute-done.2.refs_2_.refs_3_
  55.3 1.3 collective-permute-done.refs_0_.refs_1_
  57.2 3.9 %shard_map.127 = bf16[32,256,128]{2,1,0:T(8,128)(2,1)} custom-call(s32[32]{0:T(128)} %reshape.69.codes_ref, bf16[1024,1024]{1,0:T(8,128)(2,1)} %all-gather.2.cloned.1.call-done.context_ref, bf16[64,512]{1,0:T(8,128)(2,1)} %copy-done.10, bf16[64,512]{1,0:T(8,128)(2,1)} %copy-done.9, bf16[64,512]{1,0:T(8,128)(2,1)} %copy-done.8, bf16[64,512]{1,0:T(8,128)(2,1)} %copy-done.7, ...), custom_call_target="tpu_custom_call" | custom-call | tf_op jit(solution)/shard_map/pallas_call | solution.py:209
  61.1 7.5 %all-to-all-start.1 = ((bf16[8,4,256,128]{3,2,1,0:T(8,128)(2,1)}), bf16[8,4,256,128]{3,2,1,0:T(8,128)(2,1)S(1)}, u32[]{:S(2)}, u32[]{:S(2)}) async-start(bf16[8,4,256,128]{3,2,1,0:T(8,128)(2,1)} %bitcast.19), calls=%async_computation.1 | async-start | bytes 4194304 | tf_op jit(solution)/shard_map/all_to_all | solution.py:336
  68.7 5.7 %collective-permute-start.6 = (bf16[64,512]{1,0:T(8,128)(2,1)S(1)}, bf16[64,512]{1,0:T(8,128)(2,1)S(1)}, u32[]{:S(2)}, u32[]{:S(2)}) collective-permute-start(bf16[64,512]{1,0:T(8,128)(2,1)S(1)} %get-tuple-element.37), channel_id=1, source_target_pairs={{0,7},{1,0},{2,1},{3,2},{4,3},{5,4},{6,5},{7,6},{8,15},{9,8},{10,9... | collective-permute-start | bytes 196616 | tf_op jit(solution)/shard_map/ppermute | solution.py:275
  74.4 1.5 collective-permute-done.6.refs_0_.refs_7_
  75.9 0.6 copy-done.11
  76.5 3.9 %shard_map.128 = bf16[32,256,128]{2,1,0:T(8,128)(2,1)} custom-call(s32[32]{0:T(128)} %reshape.69.codes_ref, bf16[1024,1024]{1,0:T(8,128)(2,1)} %all-gather.2.cloned.1.call-done.context_ref, bf16[64,512]{1,0:T(8,128)(2,1)} %copy-done.11), custom_call_target="tpu_custom_call" | custom-call | tf_op jit(solution)/shard_map/pallas_call | solution.py:209
  80.3 14.6 %all-to-all-done.1 = bf16[8,4,256,128]{3,2,1,0:T(8,128)(2,1)S(1)} async-done(((bf16[8,4,256,128]{3,2,1,0:T(8,128)(2,1)}), bf16[8,4,256,128]{3,2,1,0:T(8,128)(2,1)S(1)}, u32[]{:S(2)}, u32[]{:S(2)}) %all-to-all-start.1) | async-done | bytes 2097184 | tf_op jit(solution)/shard_map/all_to_all | solution.py:336
  95.0 1.4 copy-done.3
  96.3 4.4 %all-to-all-start.2 = ((bf16[8,4,256,128]{3,2,1,0:T(8,128)(2,1)}), bf16[8,4,256,128]{3,2,1,0:T(8,128)(2,1)S(1)}, u32[]{:S(2)}, u32[]{:S(2)}) async-start(bf16[8,4,256,128]{3,2,1,0:T(8,128)(2,1)} %bitcast.20), calls=%async_computation.2 | async-start | bytes 4194304 | tf_op jit(solution)/shard_map/all_to_all | solution.py:336
  101.3 12.7 %shard_map.129 = (bf16[512,512]{1,0:T(8,128)(2,1)}, bf16[4,2,4,256,128]{4,3,2,1,0:T(8,128)(2,1)}, f32[4,1,512]{2,1,0:T(1,128)}, f32[4,1,512]{2,1,0:T(1,128)}) custom-call(s32[12]{0:T(128)} %copy-done.19, s32[64]{0:T(128)} %lens_ref.3, s32[2]{0:T(128)} %pad_add_fusion.base_ref, bf16[512,512]{1,0:T(8,128)(2,1)} %q_ref.3, bf16[512,512]{1,0:T(8,128)(2,1)} %k_ref.3, ...), custom_call_target="tpu_custom_call" | custom-call | flops 2147483648 | bytes 8388608 | tf_op jit(solution)/shard_map/pallas_call | solution.py:368
  114.0 13.0 %all-to-all-done.2 = bf16[8,4,256,128]{3,2,1,0:T(8,128)(2,1)S(1)} async-done(((bf16[8,4,256,128]{3,2,1,0:T(8,128)(2,1)}), bf16[8,4,256,128]{3,2,1,0:T(8,128)(2,1)S(1)}, u32[]{:S(2)}, u32[]{:S(2)}) %all-to-all-start.2) | async-done | bytes 2097184 | tf_op jit(solution)/shard_map/all_to_all | solution.py:336
  127.1 1.4 copy-done.1
  128.4 4.4 %all-to-all-start.3 = ((bf16[8,4,256,128]{3,2,1,0:T(8,128)(2,1)}), bf16[8,4,256,128]{3,2,1,0:T(8,128)(2,1)S(1)}, u32[]{:S(2)}, u32[]{:S(2)}) async-start(bf16[8,4,256,128]{3,2,1,0:T(8,128)(2,1)} %bitcast.18), calls=%async_computation.3 | async-start | bytes 4194304 | tf_op jit(solution)/shard_map/all_to_all | solution.py:336
  132.8 17.4 %shard_map.130 = (bf16[512,512]{1,0:T(8,128)(2,1)}, bf16[512,512]{1,0:T(8,128)(2,1)}, bf16[512,512]{1,0:T(8,128)(2,1)}, bf16[16,4,128,128]{3,2,1,0:T(8,128)(2,1)}) custom-call(s32[12]{0:T(128)} %copy-done.19, s32[64]{0:T(128)} %lens_ref.3, s32[2]{0:T(128)} %pad_add_fusion.base_ref, bf16[512,512]{1,0:T(8,128)(2,1)} %q_ref.3, bf16[512,512]{1,0:T(8,128)(2,1)} %k_ref.3, ...), custom_call_target="tpu_custom_call" | custom-call | flops 5368709120 | bytes 8388608 | tf_op jit(solution)/shard_map/pallas_call | solution.py:392
  150.2 9.0 %all-to-all-done.3.terms_ref = bf16[8,4,256,128]{3,2,1,0:T(8,128)(2,1)S(1)} async-done(((bf16[8,4,256,128]{3,2,1,0:T(8,128)(2,1)}), bf16[8,4,256,128]{3,2,1,0:T(8,128)(2,1)S(1)}, u32[]{:S(2)}, u32[]{:S(2)}) %all-to-all-start.3) | async-done | bytes 2097184 | tf_op jit(solution)/shard_map/all_to_all | solution.py:336
  159.2 1.4 copy-done
  160.5 7.4 %all-to-all-start.4 = ((bf16[64,128,128]{2,1,0:T(8,128)(2,1)}), bf16[64,128,128]{2,1,0:T(8,128)(2,1)S(1)}, u32[]{:S(2)}, u32[]{:S(2)}) async-start(bf16[64,128,128]{2,1,0:T(8,128)(2,1)} %bitcast.17), calls=%async_computation.4 | async-start | bytes 4194304 | tf_op jit(solution)/shard_map/all_to_all | solution.py:341
  168.0 4.8 %shard_map.135 = bf16[1024,512]{1,0:T(8,128)(2,1)} custom-call(s32[32]{0:T(128)} %reshape.69.codes_ref, bf16[8,4,256,128]{3,2,1,0:T(8,128)(2,1)} %copy-done), custom_call_target="tpu_custom_call" | custom-call | tf_op jit(solution)/shard_map/pallas_call | solution.py:242
  172.9 0.7 constant_dynamic-slice_fusion
  173.6 5.0 %collective-permute-start.13 = (bf16[64,512]{1,0:T(8,128)(2,1)S(1)}, bf16[64,512]{1,0:T(8,128)(2,1)S(1)}, u32[]{:S(2)}, u32[]{:S(2)}) collective-permute-start(bf16[64,512]{1,0:T(8,128)(2,1)S(1)} %get-tuple-element.22), channel_id=1, source_target_pairs={{0,7},{1,0},{2,1},{3,2},{4,3},{5,4},{6,5},{7,6},{8,15},{9,8},{10,9... | collective-permute-start | bytes 196616 | tf_op jit(solution)/shard_map/ppermute | solution.py:275
  178.6 3.7 %collective-permute-start.12 = (bf16[64,512]{1,0:T(8,128)(2,1)S(1)}, bf16[64,512]{1,0:T(8,128)(2,1)S(1)}, u32[]{:S(2)}, u32[]{:S(2)}) collective-permute-start(bf16[64,512]{1,0:T(8,128)(2,1)S(1)} %get-tuple-element.23), channel_id=1, source_target_pairs={{0,6},{1,7},{2,0},{3,1},{4,2},{5,3},{6,4},{7,5},{8,14},{9,15},{10,... | collective-permute-start | bytes 196616 | tf_op jit(solution)/shard_map/ppermute | solution.py:275
  182.3 2.5 %collective-permute-start.11 = (bf16[64,512]{1,0:T(8,128)(2,1)S(1)}, bf16[64,512]{1,0:T(8,128)(2,1)S(1)}, u32[]{:S(2)}, u32[]{:S(2)}) collective-permute-start(bf16[64,512]{1,0:T(8,128)(2,1)S(1)} %get-tuple-element.24), channel_id=1, source_target_pairs={{0,5},{1,6},{2,7},{3,0},{4,1},{5,2},{6,3},{7,4},{8,13},{9,14},{10,... | collective-permute-start | bytes 196616 | tf_op jit(solution)/shard_map/ppermute | solution.py:275
  184.8 5.9 %collective-permute-start.10 = (bf16[64,512]{1,0:T(8,128)(2,1)S(1)}, bf16[64,512]{1,0:T(8,128)(2,1)S(1)}, u32[]{:S(2)}, u32[]{:S(2)}) collective-permute-start(bf16[64,512]{1,0:T(8,128)(2,1)S(1)} %get-tuple-element.25), channel_id=1, source_target_pairs={{0,4},{1,5},{2,6},{3,7},{4,0},{5,1},{6,2},{7,3},{8,12},{9,13},{10,... | collective-permute-start | bytes 196616 | tf_op jit(solution)/shard_map/ppermute | solution.py:275
  190.7 1.9 collective-permute-start.9
  192.7 4.7 %collective-permute-start.8 = (bf16[64,512]{1,0:T(8,128)(2,1)S(1)}, bf16[64,512]{1,0:T(8,128)(2,1)S(1)}, u32[]{:S(2)}, u32[]{:S(2)}) collective-permute-start(bf16[64,512]{1,0:T(8,128)(2,1)S(1)} %get-tuple-element.27), channel_id=1, source_target_pairs={{0,2},{1,3},{2,4},{3,5},{4,6},{5,7},{6,0},{7,1},{8,10},{9,11},{10,... | collective-permute-start | bytes 196616 | tf_op jit(solution)/shard_map/ppermute | solution.py:275
  197.4 2.9 %collective-permute-start.7 = (bf16[64,512]{1,0:T(8,128)(2,1)S(1)}, bf16[64,512]{1,0:T(8,128)(2,1)S(1)}, u32[]{:S(2)}, u32[]{:S(2)}) collective-permute-start(bf16[64,512]{1,0:T(8,128)(2,1)S(1)} %get-tuple-element.28), channel_id=1, source_target_pairs={{0,1},{1,2},{2,3},{3,4},{4,5},{5,6},{6,7},{7,0},{8,9},{9,10},{10,1... | collective-permute-start | bytes 196616 | tf_op jit(solution)/shard_map/ppermute | solution.py:275
  200.3 1.8 dynamic-slice_reduce_fusion.codes_ref
  202.2 1.0 collective-permute-done.8.refs_2_
  203.2 1.6 collective-permute-done.7.refs_1_
  204.8 0.6 copy-done.18
  205.4 1.9 shard_map.131
  207.3 21.6 %all-to-all-done.4.terms_ref = bf16[64,128,128]{2,1,0:T(8,128)(2,1)S(1)} async-done(((bf16[64,128,128]{2,1,0:T(8,128)(2,1)}), bf16[64,128,128]{2,1,0:T(8,128)(2,1)S(1)}, u32[]{:S(2)}, u32[]{:S(2)}) %all-to-all-start.4) | async-done | bytes 2097184 | tf_op jit(solution)/shard_map/all_to_all | solution.py:341
  228.8 1.4 copy-done.2
  230.2 4.1 %shard_map.134 = bf16[128,512]{1,0:T(8,128)(2,1)} custom-call(s32[64]{0:T(128)} %dynamic-slice_reduce_fusion.codes_ref, bf16[64,128,128]{2,1,0:T(8,128)(2,1)} %copy-done.2), custom_call_target="tpu_custom_call" | custom-call | tf_op jit(solution)/shard_map/pallas_call | solution.py:259
  (58 shorter events, 1.7 us)
Async XLA Ops:
  7.2 49.6 %all-gather.2.cloned.1.call-start = ((), (), s32[]{:S(2)}) async-start(), calls=%async_computation.6 | async-start | bytes 2359296 | tf_op jit(solution)/shard_map/all_gather | solution.py:300
  10.8 38.7 %collective-permute-start.5 = (bf16[64,512]{1,0:T(8,128)(2,1)S(1)}, bf16[64,512]{1,0:T(8,128)(2,1)S(1)}, u32[]{:S(2)}, u32[]{:S(2)}) collective-permute-start(bf16[64,512]{1,0:T(8,128)(2,1)S(1)} %get-tuple-element.31), channel_id=1, source_target_pairs={{0,6},{1,7},{2,0},{3,1},{4,2},{5,3},{6,4},{7,5},{8,14},{9,15},{10,... | collective-permute-start | bytes 196616 | tf_op jit(solution)/shard_map/ppermute | solution.py:275
  23.1 38.0 %copy-start.19 = (s32[12]{0:T(128)}, s32[12]{0:T(128)S(1)}, u32[]{:S(2)}) copy-start(s32[12]{0:T(128)S(1)} %reshape.67.sel_ref) | copy-start | bytes 148
  23.9 28.7 %all-to-all-start = ((s32[64,1,128]{2,1,0:T(1,128)}), s32[64,1,128]{2,1,0:T(1,128)S(1)}, u32[]{:S(2)}, u32[]{:S(2)}) async-start(s32[64,1,128]{2,1,0:T(1,128)} %broadcast_in_dim.19), calls=%async_computation | async-start | bytes 65536 | tf_op jit(solution)/shard_map/all_to_all | solution.py:322
  35.0 18.4 %collective-permute-start.4 = (bf16[64,512]{1,0:T(8,128)(2,1)S(1)}, bf16[64,512]{1,0:T(8,128)(2,1)S(1)}, u32[]{:S(2)}, u32[]{:S(2)}) collective-permute-start(bf16[64,512]{1,0:T(8,128)(2,1)S(1)} %get-tuple-element.32), channel_id=1, source_target_pairs={{0,5},{1,6},{2,7},{3,0},{4,1},{5,2},{6,3},{7,4},{8,13},{9,14},{10,... | collective-permute-start | bytes 196616 | tf_op jit(solution)/shard_map/ppermute | solution.py:275
  36.9 16.4 %collective-permute-start.3 = (bf16[64,512]{1,0:T(8,128)(2,1)S(1)}, bf16[64,512]{1,0:T(8,128)(2,1)S(1)}, u32[]{:S(2)}, u32[]{:S(2)}) collective-permute-start(bf16[64,512]{1,0:T(8,128)(2,1)S(1)} %get-tuple-element.33), channel_id=1, source_target_pairs={{0,4},{1,5},{2,6},{3,7},{4,0},{5,1},{6,2},{7,3},{8,12},{9,13},{10,... | collective-permute-start | bytes 196616 | tf_op jit(solution)/shard_map/ppermute | solution.py:275
  44.2 11.1 %collective-permute-start.2 = (bf16[64,512]{1,0:T(8,128)(2,1)S(1)}, bf16[64,512]{1,0:T(8,128)(2,1)S(1)}, u32[]{:S(2)}, u32[]{:S(2)}) collective-permute-start(bf16[64,512]{1,0:T(8,128)(2,1)S(1)} %get-tuple-element.34), channel_id=1, source_target_pairs={{0,3},{1,4},{2,5},{3,6},{4,7},{5,0},{6,1},{7,2},{8,11},{9,12},{10,... | collective-permute-start | bytes 196616 | tf_op jit(solution)/shard_map/ppermute | solution.py:275
  46.1 9.2 %collective-permute-start.1 = (bf16[64,512]{1,0:T(8,128)(2,1)S(1)}, bf16[64,512]{1,0:T(8,128)(2,1)S(1)}, u32[]{:S(2)}, u32[]{:S(2)}) collective-permute-start(bf16[64,512]{1,0:T(8,128)(2,1)S(1)} %get-tuple-element.35), channel_id=1, source_target_pairs={{0,2},{1,3},{2,4},{3,5},{4,6},{5,7},{6,0},{7,1},{8,10},{9,11},{10,... | collective-permute-start | bytes 196616 | tf_op jit(solution)/shard_map/ppermute | solution.py:275
  49.5 7.3 %copy-start.5 = (bf16[64,512]{1,0:T(8,128)(2,1)}, bf16[64,512]{1,0:T(8,128)(2,1)S(1)}, u32[]{:S(2)}) copy-start(bf16[64,512]{1,0:T(8,128)(2,1)S(1)} %collective-permute-done.5.refs_5_.refs_6_) | copy-start | bytes 196612
  49.5 7.2 %collective-permute-start = (bf16[64,512]{1,0:T(8,128)(2,1)S(1)}, bf16[64,512]{1,0:T(8,128)(2,1)S(1)}, u32[]{:S(2)}, u32[]{:S(2)}) collective-permute-start(bf16[64,512]{1,0:T(8,128)(2,1)S(1)} %get-tuple-element.36), channel_id=1, source_target_pairs={{0,1},{1,2},{2,3},{3,4},{4,5},{5,6},{6,7},{7,0},{8,9},{9,10},{10,1... | collective-permute-start | bytes 196616 | tf_op jit(solution)/shard_map/ppermute | solution.py:275
  53.3 3.4 %copy-start.6 = (bf16[64,512]{1,0:T(8,128)(2,1)}, bf16[64,512]{1,0:T(8,128)(2,1)S(1)}, u32[]{:S(2)}) copy-start(bf16[64,512]{1,0:T(8,128)(2,1)S(1)} %collective-permute-done.4.refs_4_.refs_5_) | copy-start | bytes 196612
  53.3 3.4 %copy-start.7 = (bf16[64,512]{1,0:T(8,128)(2,1)}, bf16[64,512]{1,0:T(8,128)(2,1)S(1)}, u32[]{:S(2)}) copy-start(bf16[64,512]{1,0:T(8,128)(2,1)S(1)} %collective-permute-done.3.refs_3_.refs_4_) | copy-start | bytes 196612
  55.3 1.5 copy-start.8
  55.3 1.5 copy-start.9
  56.6 0.6 copy-start.10
  61.1 33.8 %all-to-all-start.1 = ((bf16[8,4,256,128]{3,2,1,0:T(8,128)(2,1)}), bf16[8,4,256,128]{3,2,1,0:T(8,128)(2,1)S(1)}, u32[]{:S(2)}, u32[]{:S(2)}) async-start(bf16[8,4,256,128]{3,2,1,0:T(8,128)(2,1)} %bitcast.19), calls=%async_computation.1 | async-start | bytes 4194304 | tf_op jit(solution)/shard_map/all_to_all | solution.py:336
  68.7 7.2 %collective-permute-start.6 = (bf16[64,512]{1,0:T(8,128)(2,1)S(1)}, bf16[64,512]{1,0:T(8,128)(2,1)S(1)}, u32[]{:S(2)}, u32[]{:S(2)}) collective-permute-start(bf16[64,512]{1,0:T(8,128)(2,1)S(1)} %get-tuple-element.37), channel_id=1, source_target_pairs={{0,7},{1,0},{2,1},{3,2},{4,3},{5,4},{6,5},{7,6},{8,15},{9,8},{10,9... | collective-permute-start | bytes 196616 | tf_op jit(solution)/shard_map/ppermute | solution.py:275
  75.9 0.6 copy-start.11
  95.0 1.4 copy-start.3
  96.3 30.7 %all-to-all-start.2 = ((bf16[8,4,256,128]{3,2,1,0:T(8,128)(2,1)}), bf16[8,4,256,128]{3,2,1,0:T(8,128)(2,1)S(1)}, u32[]{:S(2)}, u32[]{:S(2)}) async-start(bf16[8,4,256,128]{3,2,1,0:T(8,128)(2,1)} %bitcast.20), calls=%async_computation.2 | async-start | bytes 4194304 | tf_op jit(solution)/shard_map/all_to_all | solution.py:336
  127.1 1.4 copy-start.1
  128.4 30.7 %all-to-all-start.3 = ((bf16[8,4,256,128]{3,2,1,0:T(8,128)(2,1)}), bf16[8,4,256,128]{3,2,1,0:T(8,128)(2,1)S(1)}, u32[]{:S(2)}, u32[]{:S(2)}) async-start(bf16[8,4,256,128]{3,2,1,0:T(8,128)(2,1)} %bitcast.18), calls=%async_computation.3 | async-start | bytes 4194304 | tf_op jit(solution)/shard_map/all_to_all | solution.py:336
  159.2 1.4 copy-start
  160.5 68.3 %all-to-all-start.4 = ((bf16[64,128,128]{2,1,0:T(8,128)(2,1)}), bf16[64,128,128]{2,1,0:T(8,128)(2,1)S(1)}, u32[]{:S(2)}, u32[]{:S(2)}) async-start(bf16[64,128,128]{2,1,0:T(8,128)(2,1)} %bitcast.17), calls=%async_computation.4 | async-start | bytes 4194304 | tf_op jit(solution)/shard_map/all_to_all | solution.py:341
  168.0 4.9 %copy-start.4 = (bf16[512,512]{1,0:T(8,128)(2,1)S(1)}, bf16[512,512]{1,0:T(8,128)(2,1)}, u32[]{:S(2)}) copy-start(bf16[512,512]{1,0:T(8,128)(2,1)} %get-tuple-element.16) | copy-start | bytes 1572868
  168.0 66.3 %reduce-scatter.2.cloned.1.call-start = ((), (), s32[]{:S(2)}) async-start(), calls=%async_computation.7 | async-start | bytes 1179648 | tf_op jit(solution)/shard_map/reduce_scatter | solution.py:390
  173.6 19.0 %collective-permute-start.13 = (bf16[64,512]{1,0:T(8,128)(2,1)S(1)}, bf16[64,512]{1,0:T(8,128)(2,1)S(1)}, u32[]{:S(2)}, u32[]{:S(2)}) collective-permute-start(bf16[64,512]{1,0:T(8,128)(2,1)S(1)} %get-tuple-element.22), channel_id=1, source_target_pairs={{0,7},{1,0},{2,1},{3,2},{4,3},{5,4},{6,5},{7,6},{8,15},{9,8},{10,9... | collective-permute-start | bytes 196616 | tf_op jit(solution)/shard_map/ppermute | solution.py:275
  178.6 18.8 %collective-permute-start.12 = (bf16[64,512]{1,0:T(8,128)(2,1)S(1)}, bf16[64,512]{1,0:T(8,128)(2,1)S(1)}, u32[]{:S(2)}, u32[]{:S(2)}) collective-permute-start(bf16[64,512]{1,0:T(8,128)(2,1)S(1)} %get-tuple-element.23), channel_id=1, source_target_pairs={{0,6},{1,7},{2,0},{3,1},{4,2},{5,3},{6,4},{7,5},{8,14},{9,15},{10,... | collective-permute-start | bytes 196616 | tf_op jit(solution)/shard_map/ppermute | solution.py:275
  182.3 19.9 %collective-permute-start.11 = (bf16[64,512]{1,0:T(8,128)(2,1)S(1)}, bf16[64,512]{1,0:T(8,128)(2,1)S(1)}, u32[]{:S(2)}, u32[]{:S(2)}) collective-permute-start(bf16[64,512]{1,0:T(8,128)(2,1)S(1)} %get-tuple-element.24), channel_id=1, source_target_pairs={{0,5},{1,6},{2,7},{3,0},{4,1},{5,2},{6,3},{7,4},{8,13},{9,14},{10,... | collective-permute-start | bytes 196616 | tf_op jit(solution)/shard_map/ppermute | solution.py:275
  184.8 17.4 %collective-permute-start.10 = (bf16[64,512]{1,0:T(8,128)(2,1)S(1)}, bf16[64,512]{1,0:T(8,128)(2,1)S(1)}, u32[]{:S(2)}, u32[]{:S(2)}) collective-permute-start(bf16[64,512]{1,0:T(8,128)(2,1)S(1)} %get-tuple-element.25), channel_id=1, source_target_pairs={{0,4},{1,5},{2,6},{3,7},{4,0},{5,1},{6,2},{7,3},{8,12},{9,13},{10,... | collective-permute-start | bytes 196616 | tf_op jit(solution)/shard_map/ppermute | solution.py:275
  190.7 11.4 %collective-permute-start.9 = (bf16[64,512]{1,0:T(8,128)(2,1)S(1)}, bf16[64,512]{1,0:T(8,128)(2,1)S(1)}, u32[]{:S(2)}, u32[]{:S(2)}) collective-permute-start(bf16[64,512]{1,0:T(8,128)(2,1)S(1)} %get-tuple-element.26), channel_id=1, source_target_pairs={{0,3},{1,4},{2,5},{3,6},{4,7},{5,0},{6,1},{7,2},{8,11},{9,12},{10,... | collective-permute-start | bytes 196616 | tf_op jit(solution)/shard_map/ppermute | solution.py:275
  192.7 12.1 %copy-start.12 = (bf16[64,512]{1,0:T(8,128)(2,1)}, bf16[64,512]{1,0:T(8,128)(2,1)S(1)}, u32[]{:S(2)}) copy-start(bf16[64,512]{1,0:T(8,128)(2,1)S(1)} %collective-permute-done.13.refs_7_) | copy-start | bytes 196612
  192.7 10.5 %collective-permute-start.8 = (bf16[64,512]{1,0:T(8,128)(2,1)S(1)}, bf16[64,512]{1,0:T(8,128)(2,1)S(1)}, u32[]{:S(2)}, u32[]{:S(2)}) collective-permute-start(bf16[64,512]{1,0:T(8,128)(2,1)S(1)} %get-tuple-element.27), channel_id=1, source_target_pairs={{0,2},{1,3},{2,4},{3,5},{4,6},{5,7},{6,0},{7,1},{8,10},{9,11},{10,... | collective-permute-start | bytes 196616 | tf_op jit(solution)/shard_map/ppermute | solution.py:275
  197.4 7.4 %copy-start.13 = (bf16[64,512]{1,0:T(8,128)(2,1)}, bf16[64,512]{1,0:T(8,128)(2,1)S(1)}, u32[]{:S(2)}) copy-start(bf16[64,512]{1,0:T(8,128)(2,1)S(1)} %collective-permute-done.12.refs_6_) | copy-start | bytes 196612
  197.4 7.4 %collective-permute-start.7 = (bf16[64,512]{1,0:T(8,128)(2,1)S(1)}, bf16[64,512]{1,0:T(8,128)(2,1)S(1)}, u32[]{:S(2)}, u32[]{:S(2)}) collective-permute-start(bf16[64,512]{1,0:T(8,128)(2,1)S(1)} %get-tuple-element.28), channel_id=1, source_target_pairs={{0,1},{1,2},{2,3},{3,4},{4,5},{5,6},{6,7},{7,0},{8,9},{9,10},{10,1... | collective-permute-start | bytes 196616 | tf_op jit(solution)/shard_map/ppermute | solution.py:275
  202.2 2.6 %copy-start.14 = (bf16[64,512]{1,0:T(8,128)(2,1)}, bf16[64,512]{1,0:T(8,128)(2,1)S(1)}, u32[]{:S(2)}) copy-start(bf16[64,512]{1,0:T(8,128)(2,1)S(1)} %collective-permute-done.11.refs_5_) | copy-start | bytes 196612
  202.2 2.6 %copy-start.15 = (bf16[64,512]{1,0:T(8,128)(2,1)}, bf16[64,512]{1,0:T(8,128)(2,1)S(1)}, u32[]{:S(2)}) copy-start(bf16[64,512]{1,0:T(8,128)(2,1)S(1)} %collective-permute-done.10.refs_4_) | copy-start | bytes 196612
  202.2 2.6 %copy-start.16 = (bf16[64,512]{1,0:T(8,128)(2,1)}, bf16[64,512]{1,0:T(8,128)(2,1)S(1)}, u32[]{:S(2)}) copy-start(bf16[64,512]{1,0:T(8,128)(2,1)S(1)} %collective-permute-done.9.refs_3_) | copy-start | bytes 196612
  203.2 1.6 copy-start.17
  204.8 0.6 copy-start.18
  228.8 1.4 copy-start.2
Sparse Core Ops, SparseCore 0:
  10.7 46.0 all-gather.1
  173.0 53.1 reduce-scatter.1

commit v5 on v4

--- a/solution.py
+++ b/solution.py
@@ -10,7 +10,7 @@
 NN = (((1,), (0,)), ((), ()))
 SIZE_X, SIZE_Y, CORES = 4, 8, 2
 CTX = ("x", "y", "core")
-VMEM_BYTES = 56 * 1024 * 1024
+MIB = 1024 * 1024
 
 
 def dot(a, b, dims):
@@ -60,12 +60,10 @@
     return ref[...].reshape(-1, ref.shape[-1])
 
 
-def store_pieces(out_ref, block, part):
-    count, rows = out_ref.shape[1:3]
+def store_halves(out_ref, block, part):
+    own_x, rows = out_ref.shape[2:4]
     for c in range(CORES):
-        for p in range(count // CORES):
-            at = (c * (count // CORES) + p) * rows
-            out_ref[block, p * CORES + c] = part[at : at + rows]
+        out_ref[block // own_x, c, lax.rem(block, own_x)] = part[c * rows : (c + 1) * rows]
 
 
 def assemble_kernel(me_ref, *refs):
@@ -119,12 +117,7 @@
         if j == 0:
             near_ref[...] = part
         else:
-            block = sel_ref[head * picks + j - 1]
-            own_x, rows_core = far_ref.shape[2:4]
-            for c in range(CORES):
-                far_ref[block // own_x, c, lax.rem(block, own_x)] = part[
-                    c * rows_core : (c + 1) * rows_core
-                ]
+            store_halves(far_ref, sel_ref[head * picks + j - 1], part)
 
 
 def other_grads_kernel(
@@ -174,32 +167,9 @@
         if j == 0:
             near_ref[...] = part
         else:
-            store_pieces(far_ref, sel_ref[head * picks + j - 1], part)
+            store_halves(far_ref, sel_ref[head * picks + j - 1], part)
         query_grad = query_grad + dot(keys_of(j).T, score_grads, NN)
     query_ref[...] = query_grad.astype(jnp.bfloat16).T
-
-
-def collect_kernel(codes_ref, terms_ref, out_ref, total_ref):
-    step_at = pl.program_id(0)
-    sources, rows, width = terms_ref.shape
-    heads = total_ref.shape[0] - 1
-
-    @pl.when(step_at == 0)
-    def _():
-        total_ref[...] = jnp.zeros_like(total_ref)
-
-    def step(s, carry):
-        code = codes_ref[step_at * sources + s]
-        slot = jnp.where(code >= 0, code, heads)
-        total_ref[slot] += terms_ref[s].astype(jnp.float32)
-        return carry
-
-    lax.fori_loop(0, sources, step, 0)
-
-    @pl.when(step_at == pl.num_programs(0) - 1)
-    def _():
-        for h in range(heads):
-            out_ref[:, h * width : (h + 1) * width] = total_ref[h].astype(out_ref.dtype)
 
 
 def pack(codes, context, half, groups, width, *after):
@@ -216,11 +186,12 @@
             + [pl.BlockSpec(memory_space=pl.ANY)] * len(after),
             out_specs=pl.BlockSpec((slots // steps, rows // groups, width), lambda i, *_: (i, 0, 0)),
         ),
-        compiler_params=pltpu.CompilerParams(vmem_limit_bytes=VMEM_BYTES),
+        compiler_params=pltpu.CompilerParams(vmem_limit_bytes=60 * MIB),
     )(codes, context, *after)
 
 
-def row_sum_kernel(codes_ref, terms_ref, out_ref, total_ref):
+def row_sum_kernel(codes_ref, terms_ref, *refs):
+    out_ref, total_ref = refs[-2:]
     block = pl.program_id(0)
     sources, _, rows, width = terms_ref.shape
     heads = total_ref.shape[0] - 1
@@ -237,7 +208,7 @@
         out_ref[:, h * width : (h + 1) * width] = total_ref[h].astype(out_ref.dtype)
 
 
-def row_sum(codes, terms, heads):
+def row_sum(codes, terms, heads, *after):
     sources, blocks, rows, width = terms.shape
     return pl.pallas_call(
         row_sum_kernel,
@@ -245,29 +216,13 @@
         grid_spec=pltpu.PrefetchScalarGridSpec(
             num_scalar_prefetch=1,
             grid=(blocks,),
-            in_specs=[pl.BlockSpec((sources, 1, rows, width), lambda i, *_: (0, i, 0, 0))],
+            in_specs=[pl.BlockSpec((sources, 1, rows, width), lambda i, *_: (0, i, 0, 0))]
+            + [pl.BlockSpec(memory_space=pl.ANY)] * len(after),
             out_specs=pl.BlockSpec((rows, heads * width), lambda i, *_: (i, 0)),
             scratch_shapes=[pltpu.VMEM((heads + 1, rows, width), jnp.float32)],
         ),
-        compiler_params=pltpu.CompilerParams(vmem_limit_bytes=VMEM_BYTES),
-    )(codes, terms)
-
-
-def collect(codes, terms, heads):
-    owners, rows, width = terms.shape
-    steps = 4
-    return pl.pallas_call(
-        collect_kernel,
-        out_shape=jax.ShapeDtypeStruct((rows, heads * width), terms.dtype),
-        grid_spec=pltpu.PrefetchScalarGridSpec(
-            num_scalar_prefetch=1,
-            grid=(steps,),
-            in_specs=[pl.BlockSpec((owners // steps, rows, width), lambda i, *_: (i, 0, 0))],
-            out_specs=pl.BlockSpec((rows, heads * width), lambda i, *_: (0, 0)),
-            scratch_shapes=[pltpu.VMEM((heads + 1, rows, width), jnp.float32)],
-        ),
-        compiler_params=pltpu.CompilerParams(vmem_limit_bytes=VMEM_BYTES),
-    )(codes, terms)
+        compiler_params=pltpu.CompilerParams(vmem_limit_bytes=6 * MIB),
+    )(codes, terms, *after)
 
 
 def shifted(parts, count):
@@ -320,7 +275,6 @@
     wanted = jnp.max(jnp.where(hits, head_of[None, :], -1), axis=1)
     wanted = jnp.broadcast_to(jnp.pad(wanted, (0, 128 - blocks)), (owners, 128))
     codes = lax.all_to_all(wanted, CTX, split_axis=0, concat_axis=0, tiled=True)
-    piece_codes = lax.dynamic_slice_in_dim(codes, my_piece // pieces, 1, 1)[:, 0]
     own_x = blocks // SIZE_X
     row_codes = lax.dynamic_slice(
         codes.reshape(SIZE_X, SIZE_Y, CORES, 128),
@@ -336,17 +290,13 @@
         received = lax.all_to_all(tiles, ("x", "core"), split_axis=0, concat_axis=0, tiled=True)
         return received.reshape(row_shape)
 
-    def to_holders(tiles):
-        tiles = tiles.reshape(owners, piece_rows, width)
-        return lax.all_to_all(tiles, CTX, split_axis=0, concat_axis=0, tiled=True)
-
     early = count - 1
     far_keys = along_row(pack(row_codes, column, 0, own_x, width, *grads[1:early]))
-    far_values = along_row(pack(row_codes, column, 1, own_x, width, *grads[early:]))
+    packed_values = pack(row_codes, column, 1, own_x, width, *grads[early:])
+    far_values = along_row(gate(packed_values, far_keys[0, 0, 0, :16]))
 
     by_head = pl.BlockSpec((rows, width), lambda h, *_: (0, h))
-    all_rows = pl.BlockSpec(row_shape, lambda h, *_: (0, 0, 0, 0, 0))
-    all_far = pl.BlockSpec((blocks, pieces, piece_rows, width), lambda h, *_: (0, 0, 0, 0))
+    all_far = pl.BlockSpec(row_shape, lambda h, *_: (0, 0, 0, 0, 0))
     far = [
         pl.BlockSpec(
             (1, CORES, 1, rows // CORES, width),
@@ -357,7 +307,7 @@
     shares = [pl.BlockSpec((share_rows, width), lambda h, *_: (0, h))] * count
     by_stat = pl.BlockSpec((1, 1, rows), lambda h, *_: (h, 0, 0))
     near_shape = jax.ShapeDtypeStruct(queries.shape, jnp.bfloat16)
-    far_shape = jax.ShapeDtypeStruct((blocks, pieces, piece_rows, width), jnp.bfloat16)
+    far_shape = jax.ShapeDtypeStruct(row_shape, jnp.bfloat16)
     stat_shape = jax.ShapeDtypeStruct((heads, 1, rows), jnp.float32)
     scratch = [
         pltpu.VMEM((1, rows), jnp.int32),
@@ -367,25 +317,20 @@
     tile_flops = 2 * rows * rows * width * (picks + 1) * heads
     value_grad, far_value_grads, top, inverse = pl.pallas_call(
         value_grad_kernel,
-        out_shape=(
-            near_shape,
-            jax.ShapeDtypeStruct(row_shape, jnp.bfloat16),
-            stat_shape,
-            stat_shape,
-        ),
+        out_shape=(near_shape, far_shape, stat_shape, stat_shape),
         grid_spec=pltpu.PrefetchScalarGridSpec(
             num_scalar_prefetch=3,
             grid=(heads,),
             in_specs=[by_head, by_head, *far, *shares],
-            out_specs=[by_head, all_rows, by_stat, by_stat],
+            out_specs=[by_head, all_far, by_stat, by_stat],
             scratch_shapes=scratch,
         ),
-        compiler_params=pltpu.CompilerParams(vmem_limit_bytes=VMEM_BYTES),
+        compiler_params=pltpu.CompilerParams(vmem_limit_bytes=58 * MIB),
         cost_estimate=pl.CostEstimate(
             flops=2 * tile_flops, bytes_accessed=8 << 20, transcendentals=heads * 4 * rows * rows
         ),
     )(flat, doc_lengths, base, queries, keys, *[far_keys] * picks, *grads)
-    value_terms = along_row(gate(far_value_grads, far_values))
+    value_terms = along_row(gate(far_value_grads, far_values[0, 0, 0, :16]))
     value_sums = row_sum(row_codes, value_terms.reshape(peers, *row_shape[2:]), heads)
     context_value_grad = lax.psum_scatter(value_sums, "y", scatter_dimension=0, tiled=True)
 
@@ -399,7 +344,7 @@
             out_specs=[by_head, by_head, by_head, all_far],
             scratch_shapes=scratch,
         ),
-        compiler_params=pltpu.CompilerParams(vmem_limit_bytes=VMEM_BYTES),
+        compiler_params=pltpu.CompilerParams(vmem_limit_bytes=58 * MIB),
         cost_estimate=pl.CostEstimate(
             flops=5 * tile_flops, bytes_accessed=8 << 20, transcendentals=heads * 4 * rows * rows
         ),
@@ -407,8 +352,6 @@
         flat, doc_lengths, base, queries, keys, values,
         *[far_keys] * picks, *[far_values] * picks, top, inverse, *grads,
     )
-    key_terms = to_holders(gate(far_key_grads, value_terms))
-
     output_parts = shifted(
         [
             lax.dynamic_slice_in_dim(attended, lax.rem(me + d, count) * share_rows, share_rows, 0)
@@ -416,6 +359,12 @@
         ],
         count,
     )
+    key_terms = along_row(gate(far_key_grads, value_terms[0, 0, 0, :16]))
+    key_sums = row_sum(row_codes, key_terms.reshape(peers, *row_shape[2:]), heads, *output_parts[1:6])
+    key_sums = lax.all_to_all(key_sums, "y", split_axis=0, concat_axis=0, tiled=True)
+    key_sums = key_sums.reshape(SIZE_Y, piece_rows, heads * width).astype(jnp.float32)
+    context_key_grad = jnp.sum(key_sums, axis=0).astype(jnp.bfloat16)
+
     output_rows = pl.pallas_call(
         assemble_kernel,
         out_shape=jax.ShapeDtypeStruct((share_rows, count * heads * width), jnp.bfloat16),
@@ -423,7 +372,6 @@
         + [pl.BlockSpec(memory_space=pltpu.VMEM)] * count,
         out_specs=pl.BlockSpec(memory_space=pltpu.VMEM),
     )(me.reshape(1), *output_parts)
-    context_key_grad = collect(piece_codes, key_terms, heads)
     return output_rows, query_grad, key_grad, value_grad, context_key_grad, context_value_grad
 
 

time: 242 us -> 241 us (level)
  starting transfers between devices: 96.2 us -> 102 us
  local copies, waits for them, and re-layouts: 13.7 us -> 9.77 us
  waiting for transfers between devices: 65.7 us -> 62 us
    all_to_all x1, waiting for transfers between devices: 21.6 us -> 12.7 us  [on_device(): lax.all_to_all(key_sums, 'y', split_axis=0, concat_axis=0, tiled=True)]
    ppermute x14, waiting for transfers between devices: 7.38 us -> 12.3 us  [shifted(): lax.ppermute(parts[d], 'head', [(i, (i + d) % count) for i in range(count)])]
    pallas_call x2 -> x1, Pallas kernels: 16.9 us -> 12.7 us  [on_device(): pl.pallas_call(value_grad_kernel, out_shape=(near_shape, far_shape, stat_...]
    ppermute x14, starting transfers between devices: 61.3 us -> 65.2 us  [shifted(): lax.ppermute(parts[d], 'head', [(i, (i + d) % count) for i in range(count)])]
    unnamed x41 -> x39, local copies, waits for them, and re-layouts: 7.93 us -> 4.08 us
    all_to_all x3 -> x4, starting transfers between devices: 16.3 us -> 20 us  [along_row(): lax.all_to_all(tiles, ('x', 'core'), split_axis=0, concat_axis=0, tiled=T...]
    pallas_call x1 -> x2, Pallas kernels: 4.78 us -> 7.32 us  [row_sum(): pl.pallas_call(row_sum_kernel, out_shape=jax.ShapeDtypeStruct((blocks * r...]
    all_to_all x3 -> x4, waiting for transfers between devices: 36.6 us -> 37 us  [along_row(): lax.all_to_all(tiles, ('x', 'core'), split_axis=0, concat_axis=0, tiled=T...]
  transfers between devices with their start and end apart: 21 -> 22, of which waited for: 10 -> 10; matrix products, arithmetic and copies ran while one was open for 3% -> 3% of each run, Pallas kernels for 19% -> 18%
where the time goes in v5:
time: 241 us; the launch traced here: 238 us
  starting transfers between devices  102 us (42%)
  waiting for transfers between devices  62 us (26%)
  Pallas kernels  47.1 us (20%)
  between operations  14.5 us (6%)
  local copies, waits for them, and re-layouts  9.77 us (4%)
  other arithmetic  3.29 us (1%)
    ppermute x14, starting transfers between devices, shifted(): lax.ppermute(parts[d], 'head', [(i, (i + d) % count) for i in range(count)])  65.2 us
    all_to_all x4, waiting for transfers between devices, along_row(): lax.all_to_all(tiles, ('x', 'core'), split_axis=0, concat_axis=0, tiled=T...  37 us
    all_to_all x4, starting transfers between devices, along_row(): lax.all_to_all(tiles, ('x', 'core'), split_axis=0, concat_axis=0, tiled=T...  20 us
    pallas_call x1, Pallas kernels, on_device(): pl.pallas_call(other_grads_kernel, out_shape=(near_shape, near_shape, nea...  17.4 us
    pallas_call x1, Pallas kernels, on_device(): pl.pallas_call(value_grad_kernel, out_shape=(near_shape, far_shape, stat_...  12.7 us
    all_to_all x1, waiting for transfers between devices, on_device(): lax.all_to_all(key_sums, 'y', split_axis=0, concat_axis=0, tiled=True)  12.7 us
    ppermute x14, waiting for transfers between devices, shifted(): lax.ppermute(parts[d], 'head', [(i, (i + d) % count) for i in range(count)])  12.3 us
    all_to_all x1, starting transfers between devices, on_device(): codes = lax.all_to_all(wanted, CTX, split_axis=0, concat_axis=0, tiled=True)  11.1 us
  transfers between devices with their start and end apart: 22, of which 10 were waited for; matrix products, arithmetic and copies ran while one was open for 3% of the time, Pallas kernels for 18%

profile of v5, /device:TPU:1, one launch (start us, length us, event | category | flops | bytes accessed | tf_op | source)
XLA Modules:
  0.0 238.3 jit_solution(11977966590654048749)
XLA Ops:
  7.2 1.7 pad_maximum_fusion
  9.0 1.7 constant_dynamic-slice_fusion.8
  10.7 4.8 %collective-permute-start = (bf16[64,512]{1,0:T(8,128)(2,1)S(1)}, bf16[64,512]{1,0:T(8,128)(2,1)S(1)}, u32[]{:S(2)}, u32[]{:S(2)}) collective-permute-start(bf16[64,512]{1,0:T(8,128)(2,1)S(1)} %get-tuple-element.36), channel_id=1, source_target_pairs={{0,1},{1,2},{2,3},{3,4},{4,5},{5,6},{6,7},{7,0},{8,9},{9,10},{10,1... | collective-permute-start | bytes 196616 | tf_op jit(solution)/shard_map/ppermute | solution.py:230
  15.6 0.8 copy.20
  16.6 0.6 broadcast_in_dim.19
  17.2 11.1 %all-to-all-start = ((s32[64,1,128]{2,1,0:T(1,128)}), s32[64,1,128]{2,1,0:T(1,128)S(1)}, u32[]{:S(2)}, u32[]{:S(2)}) async-start(s32[64,1,128]{2,1,0:T(1,128)} %broadcast_in_dim.19), calls=%async_computation | async-start | bytes 65536 | tf_op jit(solution)/shard_map/all_to_all | solution.py:277
  28.3 5.8 %collective-permute-start.1 = (bf16[64,512]{1,0:T(8,128)(2,1)S(1)}, bf16[64,512]{1,0:T(8,128)(2,1)S(1)}, u32[]{:S(2)}, u32[]{:S(2)}) collective-permute-start(bf16[64,512]{1,0:T(8,128)(2,1)S(1)} %get-tuple-element.35), channel_id=1, source_target_pairs={{0,2},{1,3},{2,4},{3,5},{4,6},{5,7},{6,0},{7,1},{8,10},{9,11},{10,... | collective-permute-start | bytes 196616 | tf_op jit(solution)/shard_map/ppermute | solution.py:230
  34.1 7.0 %collective-permute-start.2 = (bf16[64,512]{1,0:T(8,128)(2,1)S(1)}, bf16[64,512]{1,0:T(8,128)(2,1)S(1)}, u32[]{:S(2)}, u32[]{:S(2)}) collective-permute-start(bf16[64,512]{1,0:T(8,128)(2,1)S(1)} %get-tuple-element.34), channel_id=1, source_target_pairs={{0,3},{1,4},{2,5},{3,6},{4,7},{5,0},{6,1},{7,2},{8,11},{9,12},{10,... | collective-permute-start | bytes 196616 | tf_op jit(solution)/shard_map/ppermute | solution.py:230
  41.1 2.8 %collective-permute-start.3 = (bf16[64,512]{1,0:T(8,128)(2,1)S(1)}, bf16[64,512]{1,0:T(8,128)(2,1)S(1)}, u32[]{:S(2)}, u32[]{:S(2)}) collective-permute-start(bf16[64,512]{1,0:T(8,128)(2,1)S(1)} %get-tuple-element.33), channel_id=1, source_target_pairs={{0,4},{1,5},{2,6},{3,7},{4,0},{5,1},{6,2},{7,3},{8,12},{9,13},{10,... | collective-permute-start | bytes 196616 | tf_op jit(solution)/shard_map/ppermute | solution.py:230
  44.0 6.4 %collective-permute-start.4 = (bf16[64,512]{1,0:T(8,128)(2,1)S(1)}, bf16[64,512]{1,0:T(8,128)(2,1)S(1)}, u32[]{:S(2)}, u32[]{:S(2)}) collective-permute-start(bf16[64,512]{1,0:T(8,128)(2,1)S(1)} %get-tuple-element.32), channel_id=1, source_target_pairs={{0,5},{1,6},{2,7},{3,0},{4,1},{5,2},{6,3},{7,4},{8,13},{9,14},{10,... | collective-permute-start | bytes 196616 | tf_op jit(solution)/shard_map/ppermute | solution.py:230
  50.4 3.4 %collective-permute-start.5 = (bf16[64,512]{1,0:T(8,128)(2,1)S(1)}, bf16[64,512]{1,0:T(8,128)(2,1)S(1)}, u32[]{:S(2)}, u32[]{:S(2)}) collective-permute-start(bf16[64,512]{1,0:T(8,128)(2,1)S(1)} %get-tuple-element.31), channel_id=1, source_target_pairs={{0,6},{1,7},{2,0},{3,1},{4,2},{5,3},{6,4},{7,5},{8,14},{9,15},{10,... | collective-permute-start | bytes 196616 | tf_op jit(solution)/shard_map/ppermute | solution.py:230
  54.5 0.9 collective-permute-done.4.refs_4_.refs_5_
  55.5 3.1 %collective-permute-done.5.refs_5_.refs_6_ = bf16[64,512]{1,0:T(8,128)(2,1)S(1)} collective-permute-done((bf16[64,512]{1,0:T(8,128)(2,1)S(1)}, bf16[64,512]{1,0:T(8,128)(2,1)S(1)}, u32[]{:S(2)}, u32[]{:S(2)}) %collective-permute-start.5) | collective-permute-done | bytes 65568 | tf_op jit(solution)/shard_map/ppermute | solution.py:230
  59.2 3.9 %shard_map.127 = bf16[32,256,128]{2,1,0:T(8,128)(2,1)} custom-call(s32[32]{0:T(128)} %reshape.71.codes_ref, bf16[1024,1024]{1,0:T(8,128)(2,1)} %all-gather.2.cloned.1.call-done.context_ref, bf16[64,512]{1,0:T(8,128)(2,1)} %copy-done.9, bf16[64,512]{1,0:T(8,128)(2,1)} %copy-done.10, bf16[64,512]{1,0:T(8,128)(2,1)} %copy-done.11, bf16[64,512]{1,0:T(8,128)(2,1)} %copy-done.12, ...), custom_call_target="tpu_custom_call" | custom-call | tf_op jit(solution)/shard_map/pallas_call | solution.py:179
  63.1 6.0 %all-to-all-start.1 = ((bf16[8,4,256,128]{3,2,1,0:T(8,128)(2,1)}), bf16[8,4,256,128]{3,2,1,0:T(8,128)(2,1)S(1)}, u32[]{:S(2)}, u32[]{:S(2)}) async-start(bf16[8,4,256,128]{3,2,1,0:T(8,128)(2,1)} %bitcast.22), calls=%async_computation.1 | async-start | bytes 4194304 | tf_op jit(solution)/shard_map/all_to_all | solution.py:290
  69.1 5.2 %collective-permute-start.6 = (bf16[64,512]{1,0:T(8,128)(2,1)S(1)}, bf16[64,512]{1,0:T(8,128)(2,1)S(1)}, u32[]{:S(2)}, u32[]{:S(2)}) collective-permute-start(bf16[64,512]{1,0:T(8,128)(2,1)S(1)} %get-tuple-element.37), channel_id=1, source_target_pairs={{0,7},{1,0},{2,1},{3,2},{4,3},{5,4},{6,5},{7,6},{8,15},{9,8},{10,9... | collective-permute-start | bytes 196616 | tf_op jit(solution)/shard_map/ppermute | solution.py:230
  74.4 1.5 collective-permute-done.6.refs_0_.refs_7_
  76.5 3.9 %shard_map.128.kept_ref = bf16[32,256,128]{2,1,0:T(8,128)(2,1)} custom-call(s32[32]{0:T(128)} %reshape.71.codes_ref, bf16[1024,1024]{1,0:T(8,128)(2,1)} %all-gather.2.cloned.1.call-done.context_ref, bf16[64,512]{1,0:T(8,128)(2,1)} %copy-done.15), custom_call_target="tpu_custom_call" | custom-call | tf_op jit(solution)/shard_map/pallas_call | solution.py:179
  80.4 15.1 %all-to-all-done.1 = bf16[8,4,256,128]{3,2,1,0:T(8,128)(2,1)S(1)} async-done(((bf16[8,4,256,128]{3,2,1,0:T(8,128)(2,1)}), bf16[8,4,256,128]{3,2,1,0:T(8,128)(2,1)S(1)}, u32[]{:S(2)}, u32[]{:S(2)}) %all-to-all-start.1) | async-done | bytes 2097184 | tf_op jit(solution)/shard_map/all_to_all | solution.py:290
  95.4 0.6 slice_bitcast_fusion.2.after_ref
  96.1 0.7 copy-done.6
  96.8 4.4 %all-to-all-start.2 = ((bf16[8,4,256,128]{3,2,1,0:T(8,128)(2,1)}), bf16[8,4,256,128]{3,2,1,0:T(8,128)(2,1)S(1)}, u32[]{:S(2)}, u32[]{:S(2)}) async-start(bf16[8,4,256,128]{3,2,1,0:T(8,128)(2,1)} %bitcast.20), calls=%async_computation.2 | async-start | bytes 4194304 | tf_op jit(solution)/shard_map/all_to_all | solution.py:290
  101.2 0.7 pad_add_fusion.base_ref
  101.8 12.7 %shard_map.130 = (bf16[512,512]{1,0:T(8,128)(2,1)}, bf16[4,2,4,256,128]{4,3,2,1,0:T(8,128)(2,1)}, f32[4,1,512]{2,1,0:T(1,128)}, f32[4,1,512]{2,1,0:T(1,128)}) custom-call(s32[12]{0:T(128)} %copy-done.18, s32[64]{0:T(128)} %lens_ref.3, s32[2]{0:T(128)} %pad_add_fusion.base_ref, bf16[512,512]{1,0:T(8,128)(2,1)} %q_ref.3, bf16[512,512]{1,0:T(8,128)(2,1)} %k_ref.3, ...), custom_call_target="tpu_custom_call" | custom-call | flops 2147483648 | bytes 8388608 | tf_op jit(solution)/shard_map/pallas_call | solution.py:318
  114.6 13.0 %all-to-all-done.2 = bf16[8,4,256,128]{3,2,1,0:T(8,128)(2,1)S(1)} async-done(((bf16[8,4,256,128]{3,2,1,0:T(8,128)(2,1)}), bf16[8,4,256,128]{3,2,1,0:T(8,128)(2,1)S(1)}, u32[]{:S(2)}, u32[]{:S(2)}) %all-to-all-start.2) | async-done | bytes 2097184 | tf_op jit(solution)/shard_map/all_to_all | solution.py:290
  128.1 0.7 copy-done.7
  128.9 4.4 %all-to-all-start.3 = ((bf16[8,4,256,128]{3,2,1,0:T(8,128)(2,1)}), bf16[8,4,256,128]{3,2,1,0:T(8,128)(2,1)S(1)}, u32[]{:S(2)}, u32[]{:S(2)}) async-start(bf16[8,4,256,128]{3,2,1,0:T(8,128)(2,1)} %bitcast.23), calls=%async_computation.3 | async-start | bytes 4194304 | tf_op jit(solution)/shard_map/all_to_all | solution.py:290
  133.2 17.4 %shard_map.131 = (bf16[512,512]{1,0:T(8,128)(2,1)}, bf16[512,512]{1,0:T(8,128)(2,1)}, bf16[512,512]{1,0:T(8,128)(2,1)}, bf16[4,2,4,256,128]{4,3,2,1,0:T(8,128)(2,1)}) custom-call(s32[12]{0:T(128)} %copy-done.18, s32[64]{0:T(128)} %lens_ref.3, s32[2]{0:T(128)} %pad_add_fusion.base_ref, bf16[512,512]{1,0:T(8,128)(2,1)} %q_ref.3, bf16[512,512]{1,0:T(8,128)(2,1)} %k_ref.3, ...), custom_call_target="tpu_custom_call" | custom-call | flops 5368709120 | bytes 8388608 | tf_op jit(solution)/shard_map/pallas_call | solution.py:337
  150.6 9.0 %all-to-all-done.3.terms_ref = bf16[8,4,256,128]{3,2,1,0:T(8,128)(2,1)S(1)} async-done(((bf16[8,4,256,128]{3,2,1,0:T(8,128)(2,1)}), bf16[8,4,256,128]{3,2,1,0:T(8,128)(2,1)S(1)}, u32[]{:S(2)}, u32[]{:S(2)}) %all-to-all-start.3) | async-done | bytes 2097184 | tf_op jit(solution)/shard_map/all_to_all | solution.py:290
  160.2 5.2 %all-to-all-start.4 = ((bf16[8,4,256,128]{3,2,1,0:T(8,128)(2,1)}), bf16[8,4,256,128]{3,2,1,0:T(8,128)(2,1)}, u32[]{:S(2)}, u32[]{:S(2)}) async-start(bf16[8,4,256,128]{3,2,1,0:T(8,128)(2,1)} %bitcast.21), calls=%async_computation.4 | async-start | bytes 4194304 | tf_op jit(solution)/shard_map/all_to_all | solution.py:290
  165.4 2.8 %shard_map.136 = bf16[1024,512]{1,0:T(8,128)(2,1)} custom-call(s32[32]{0:T(128)S(1)} %copy-done.5, bf16[8,4,256,128]{3,2,1,0:T(8,128)(2,1)S(1)} %all-to-all-done.3.terms_ref), custom_call_target="tpu_custom_call" | custom-call | tf_op jit(solution)/shard_map/pallas_call | solution.py:213
  168.3 0.7 constant_dynamic-slice_fusion
  169.0 3.5 %collective-permute-start.7 = (bf16[64,512]{1,0:T(8,128)(2,1)S(1)}, bf16[64,512]{1,0:T(8,128)(2,1)S(1)}, u32[]{:S(2)}, u32[]{:S(2)}) collective-permute-start(bf16[64,512]{1,0:T(8,128)(2,1)S(1)} %get-tuple-element.28), channel_id=1, source_target_pairs={{0,1},{1,2},{2,3},{3,4},{4,5},{5,6},{6,7},{7,0},{8,9},{9,10},{10,1... | collective-permute-start | bytes 196616 | tf_op jit(solution)/shard_map/ppermute | solution.py:230
  172.5 4.1 %collective-permute-start.8 = (bf16[64,512]{1,0:T(8,128)(2,1)S(1)}, bf16[64,512]{1,0:T(8,128)(2,1)S(1)}, u32[]{:S(2)}, u32[]{:S(2)}) collective-permute-start(bf16[64,512]{1,0:T(8,128)(2,1)S(1)} %get-tuple-element.27), channel_id=1, source_target_pairs={{0,2},{1,3},{2,4},{3,5},{4,6},{5,7},{6,0},{7,1},{8,10},{9,11},{10,... | collective-permute-start | bytes 196616 | tf_op jit(solution)/shard_map/ppermute | solution.py:230
  176.6 4.9 %collective-permute-start.9 = (bf16[64,512]{1,0:T(8,128)(2,1)S(1)}, bf16[64,512]{1,0:T(8,128)(2,1)S(1)}, u32[]{:S(2)}, u32[]{:S(2)}) collective-permute-start(bf16[64,512]{1,0:T(8,128)(2,1)S(1)} %get-tuple-element.26), channel_id=1, source_target_pairs={{0,3},{1,4},{2,5},{3,6},{4,7},{5,0},{6,1},{7,2},{8,11},{9,12},{10,... | collective-permute-start | bytes 196616 | tf_op jit(solution)/shard_map/ppermute | solution.py:230
  181.5 3.7 %collective-permute-start.10 = (bf16[64,512]{1,0:T(8,128)(2,1)S(1)}, bf16[64,512]{1,0:T(8,128)(2,1)S(1)}, u32[]{:S(2)}, u32[]{:S(2)}) collective-permute-start(bf16[64,512]{1,0:T(8,128)(2,1)S(1)} %get-tuple-element.25), channel_id=1, source_target_pairs={{0,4},{1,5},{2,6},{3,7},{4,0},{5,1},{6,2},{7,3},{8,12},{9,13},{10,... | collective-permute-start | bytes 196616 | tf_op jit(solution)/shard_map/ppermute | solution.py:230
  185.2 4.4 %collective-permute-start.11 = (bf16[64,512]{1,0:T(8,128)(2,1)S(1)}, bf16[64,512]{1,0:T(8,128)(2,1)S(1)}, u32[]{:S(2)}, u32[]{:S(2)}) collective-permute-start(bf16[64,512]{1,0:T(8,128)(2,1)S(1)} %get-tuple-element.24), channel_id=1, source_target_pairs={{0,5},{1,6},{2,7},{3,0},{4,1},{5,2},{6,3},{7,4},{8,13},{9,14},{10,... | collective-permute-start | bytes 196616 | tf_op jit(solution)/shard_map/ppermute | solution.py:230
  189.7 1.2 collective-permute-done.10.refs_4_.refs_3_
  190.9 2.3 collective-permute-done.11.refs_5_.refs_4_
  193.2 4.6 %shard_map.135 = bf16[1024,512]{1,0:T(8,128)(2,1)} custom-call(s32[32]{0:T(128)S(1)} %copy-done.5, bf16[8,4,256,128]{3,2,1,0:T(8,128)(2,1)} %all-to-all-done.4.terms_ref, bf16[64,512]{1,0:T(8,128)(2,1)S(1)} %collective-permute-done.7.refs_1_.refs_0_, bf16[64,512]{1,0:T(8,128)(2,1)S(1)} %collective-permute-done.8.refs_2_.refs_1_, ...), custom_call_target="tpu_custom_call" | custom-call | tf_op jit(solution)/shard_map/pallas_call | solution.py:213
  197.8 5.2 %all-to-all-start.5 = ((bf16[8,128,512]{2,1,0:T(8,128)(2,1)}), bf16[8,128,512]{2,1,0:T(8,128)(2,1)S(1)}, u32[]{:S(2)}, u32[]{:S(2)}) async-start(bf16[8,128,512]{2,1,0:T(8,128)(2,1)} %bitcast.13), calls=%async_computation.5 | async-start | bytes 2097152 | tf_op jit(solution)/shard_map/all_to_all | solution.py:364
  203.1 4.2 %collective-permute-start.12 = (bf16[64,512]{1,0:T(8,128)(2,1)S(1)}, bf16[64,512]{1,0:T(8,128)(2,1)S(1)}, u32[]{:S(2)}, u32[]{:S(2)}) collective-permute-start(bf16[64,512]{1,0:T(8,128)(2,1)S(1)} %get-tuple-element.23), channel_id=1, source_target_pairs={{0,6},{1,7},{2,0},{3,1},{4,2},{5,3},{6,4},{7,5},{8,14},{9,15},{10,... | collective-permute-start | bytes 196616 | tf_op jit(solution)/shard_map/ppermute | solution.py:230
  207.3 4.9 %collective-permute-start.13 = (bf16[64,512]{1,0:T(8,128)(2,1)S(1)}, bf16[64,512]{1,0:T(8,128)(2,1)S(1)}, u32[]{:S(2)}, u32[]{:S(2)}) collective-permute-start(bf16[64,512]{1,0:T(8,128)(2,1)S(1)} %get-tuple-element.22), channel_id=1, source_target_pairs={{0,7},{1,0},{2,1},{3,2},{4,3},{5,4},{6,5},{7,6},{8,15},{9,8},{10,9... | collective-permute-start | bytes 196616 | tf_op jit(solution)/shard_map/ppermute | solution.py:230
  212.2 3.3 %collective-permute-done.13.refs_7_ = bf16[64,512]{1,0:T(8,128)(2,1)S(1)} collective-permute-done((bf16[64,512]{1,0:T(8,128)(2,1)S(1)}, bf16[64,512]{1,0:T(8,128)(2,1)S(1)}, u32[]{:S(2)}, u32[]{:S(2)}) %collective-permute-start.13) | collective-permute-done | bytes 65568 | tf_op jit(solution)/shard_map/ppermute | solution.py:230
  215.5 0.6 copy-done.17
  216.1 1.9 shard_map.132
  218.0 12.7 %all-to-all-done.5 = bf16[8,128,512]{2,1,0:T(8,128)(2,1)S(1)} async-done(((bf16[8,128,512]{2,1,0:T(8,128)(2,1)}), bf16[8,128,512]{2,1,0:T(8,128)(2,1)S(1)}, u32[]{:S(2)}, u32[]{:S(2)}) %all-to-all-start.5) | async-done | bytes 1048608 | tf_op jit(solution)/shard_map/all_to_all | solution.py:364
  230.6 0.8 reduce_sum.12
  (62 shorter events, 3.5 us)
Async XLA Ops:
  7.2 51.4 %all-gather.2.cloned.1.call-start = ((), (), s32[]{:S(2)}) async-start(), calls=%async_computation.7 | async-start | bytes 2359296 | tf_op jit(solution)/shard_map/all_gather | solution.py:255
  10.7 39.6 %collective-permute-start = (bf16[64,512]{1,0:T(8,128)(2,1)S(1)}, bf16[64,512]{1,0:T(8,128)(2,1)S(1)}, u32[]{:S(2)}, u32[]{:S(2)}) collective-permute-start(bf16[64,512]{1,0:T(8,128)(2,1)S(1)} %get-tuple-element.36), channel_id=1, source_target_pairs={{0,1},{1,2},{2,3},{3,4},{4,5},{5,6},{6,7},{7,0},{8,9},{9,10},{10,1... | collective-permute-start | bytes 196616 | tf_op jit(solution)/shard_map/ppermute | solution.py:230
  16.4 46.7 %copy-start.18 = (s32[12]{0:T(128)}, s32[12]{0:T(128)S(1)}, u32[]{:S(2)}) copy-start(s32[12]{0:T(128)S(1)} %reshape.69.sel_ref) | copy-start | bytes 148
  17.2 36.6 %all-to-all-start = ((s32[64,1,128]{2,1,0:T(1,128)}), s32[64,1,128]{2,1,0:T(1,128)S(1)}, u32[]{:S(2)}, u32[]{:S(2)}) async-start(s32[64,1,128]{2,1,0:T(1,128)} %broadcast_in_dim.19), calls=%async_computation | async-start | bytes 65536 | tf_op jit(solution)/shard_map/all_to_all | solution.py:277
  28.3 26.2 %collective-permute-start.1 = (bf16[64,512]{1,0:T(8,128)(2,1)S(1)}, bf16[64,512]{1,0:T(8,128)(2,1)S(1)}, u32[]{:S(2)}, u32[]{:S(2)}) collective-permute-start(bf16[64,512]{1,0:T(8,128)(2,1)S(1)} %get-tuple-element.35), channel_id=1, source_target_pairs={{0,2},{1,3},{2,4},{3,5},{4,6},{5,7},{6,0},{7,1},{8,10},{9,11},{10,... | collective-permute-start | bytes 196616 | tf_op jit(solution)/shard_map/ppermute | solution.py:230
  34.1 20.4 %collective-permute-start.2 = (bf16[64,512]{1,0:T(8,128)(2,1)S(1)}, bf16[64,512]{1,0:T(8,128)(2,1)S(1)}, u32[]{:S(2)}, u32[]{:S(2)}) collective-permute-start(bf16[64,512]{1,0:T(8,128)(2,1)S(1)} %get-tuple-element.34), channel_id=1, source_target_pairs={{0,3},{1,4},{2,5},{3,6},{4,7},{5,0},{6,1},{7,2},{8,11},{9,12},{10,... | collective-permute-start | bytes 196616 | tf_op jit(solution)/shard_map/ppermute | solution.py:230
  41.1 13.4 %collective-permute-start.3 = (bf16[64,512]{1,0:T(8,128)(2,1)S(1)}, bf16[64,512]{1,0:T(8,128)(2,1)S(1)}, u32[]{:S(2)}, u32[]{:S(2)}) collective-permute-start(bf16[64,512]{1,0:T(8,128)(2,1)S(1)} %get-tuple-element.33), channel_id=1, source_target_pairs={{0,4},{1,5},{2,6},{3,7},{4,0},{5,1},{6,2},{7,3},{8,12},{9,13},{10,... | collective-permute-start | bytes 196616 | tf_op jit(solution)/shard_map/ppermute | solution.py:230
  44.0 11.5 %collective-permute-start.4 = (bf16[64,512]{1,0:T(8,128)(2,1)S(1)}, bf16[64,512]{1,0:T(8,128)(2,1)S(1)}, u32[]{:S(2)}, u32[]{:S(2)}) collective-permute-start(bf16[64,512]{1,0:T(8,128)(2,1)S(1)} %get-tuple-element.32), channel_id=1, source_target_pairs={{0,5},{1,6},{2,7},{3,0},{4,1},{5,2},{6,3},{7,4},{8,13},{9,14},{10,... | collective-permute-start | bytes 196616 | tf_op jit(solution)/shard_map/ppermute | solution.py:230
  50.4 8.2 %copy-start.9 = (bf16[64,512]{1,0:T(8,128)(2,1)}, bf16[64,512]{1,0:T(8,128)(2,1)S(1)}, u32[]{:S(2)}) copy-start(bf16[64,512]{1,0:T(8,128)(2,1)S(1)} %collective-permute-done.refs_0_.refs_1_) | copy-start | bytes 196612
  50.4 8.2 %collective-permute-start.5 = (bf16[64,512]{1,0:T(8,128)(2,1)S(1)}, bf16[64,512]{1,0:T(8,128)(2,1)S(1)}, u32[]{:S(2)}, u32[]{:S(2)}) collective-permute-start(bf16[64,512]{1,0:T(8,128)(2,1)S(1)} %get-tuple-element.31), channel_id=1, source_target_pairs={{0,6},{1,7},{2,0},{3,1},{4,2},{5,3},{6,4},{7,5},{8,14},{9,15},{10,... | collective-permute-start | bytes 196616 | tf_op jit(solution)/shard_map/ppermute | solution.py:230
  54.5 4.1 %copy-start.10 = (bf16[64,512]{1,0:T(8,128)(2,1)}, bf16[64,512]{1,0:T(8,128)(2,1)S(1)}, u32[]{:S(2)}) copy-start(bf16[64,512]{1,0:T(8,128)(2,1)S(1)} %collective-permute-done.1.refs_1_.refs_2_) | copy-start | bytes 196612
  54.5 4.1 %copy-start.11 = (bf16[64,512]{1,0:T(8,128)(2,1)}, bf16[64,512]{1,0:T(8,128)(2,1)S(1)}, u32[]{:S(2)}) copy-start(bf16[64,512]{1,0:T(8,128)(2,1)S(1)} %collective-permute-done.2.refs_2_.refs_3_) | copy-start | bytes 196612
  54.5 4.1 %copy-start.12 = (bf16[64,512]{1,0:T(8,128)(2,1)}, bf16[64,512]{1,0:T(8,128)(2,1)S(1)}, u32[]{:S(2)}) copy-start(bf16[64,512]{1,0:T(8,128)(2,1)S(1)} %collective-permute-done.3.refs_3_.refs_4_) | copy-start | bytes 196612
  55.5 3.1 %copy-start.13 = (bf16[64,512]{1,0:T(8,128)(2,1)}, bf16[64,512]{1,0:T(8,128)(2,1)S(1)}, u32[]{:S(2)}) copy-start(bf16[64,512]{1,0:T(8,128)(2,1)S(1)} %collective-permute-done.4.refs_4_.refs_5_) | copy-start | bytes 196612
  58.5 0.6 copy-start.14
  63.1 32.4 %all-to-all-start.1 = ((bf16[8,4,256,128]{3,2,1,0:T(8,128)(2,1)}), bf16[8,4,256,128]{3,2,1,0:T(8,128)(2,1)S(1)}, u32[]{:S(2)}, u32[]{:S(2)}) async-start(bf16[8,4,256,128]{3,2,1,0:T(8,128)(2,1)} %bitcast.22), calls=%async_computation.1 | async-start | bytes 4194304 | tf_op jit(solution)/shard_map/all_to_all | solution.py:290
  69.1 6.8 %collective-permute-start.6 = (bf16[64,512]{1,0:T(8,128)(2,1)S(1)}, bf16[64,512]{1,0:T(8,128)(2,1)S(1)}, u32[]{:S(2)}, u32[]{:S(2)}) collective-permute-start(bf16[64,512]{1,0:T(8,128)(2,1)S(1)} %get-tuple-element.37), channel_id=1, source_target_pairs={{0,7},{1,0},{2,1},{3,2},{4,3},{5,4},{6,5},{7,6},{8,15},{9,8},{10,9... | collective-permute-start | bytes 196616 | tf_op jit(solution)/shard_map/ppermute | solution.py:230
  75.9 0.6 copy-start.15
  95.4 1.3 copy-start.6
  96.8 30.7 %all-to-all-start.2 = ((bf16[8,4,256,128]{3,2,1,0:T(8,128)(2,1)}), bf16[8,4,256,128]{3,2,1,0:T(8,128)(2,1)S(1)}, u32[]{:S(2)}, u32[]{:S(2)}) async-start(bf16[8,4,256,128]{3,2,1,0:T(8,128)(2,1)} %bitcast.20), calls=%async_computation.2 | async-start | bytes 4194304 | tf_op jit(solution)/shard_map/all_to_all | solution.py:290
  127.5 1.3 copy-start.7
  128.9 30.7 %all-to-all-start.3 = ((bf16[8,4,256,128]{3,2,1,0:T(8,128)(2,1)}), bf16[8,4,256,128]{3,2,1,0:T(8,128)(2,1)S(1)}, u32[]{:S(2)}, u32[]{:S(2)}) async-start(bf16[8,4,256,128]{3,2,1,0:T(8,128)(2,1)} %bitcast.23), calls=%async_computation.3 | async-start | bytes 4194304 | tf_op jit(solution)/shard_map/all_to_all | solution.py:290
  160.2 5.2 %copy-start.5 = (s32[32]{0:T(128)S(1)}, s32[32]{0:T(128)}, u32[]{:S(2)}) copy-start(s32[32]{0:T(128)} %reshape.71.codes_ref) | copy-start | bytes 388
  160.2 33.1 %all-to-all-start.4 = ((bf16[8,4,256,128]{3,2,1,0:T(8,128)(2,1)}), bf16[8,4,256,128]{3,2,1,0:T(8,128)(2,1)}, u32[]{:S(2)}, u32[]{:S(2)}) async-start(bf16[8,4,256,128]{3,2,1,0:T(8,128)(2,1)} %bitcast.21), calls=%async_computation.4 | async-start | bytes 4194304 | tf_op jit(solution)/shard_map/all_to_all | solution.py:290
  165.4 2.9 %copy-start.8 = (bf16[512,512]{1,0:T(8,128)(2,1)S(1)}, bf16[512,512]{1,0:T(8,128)(2,1)}, u32[]{:S(2)}) copy-start(bf16[512,512]{1,0:T(8,128)(2,1)} %get-tuple-element.16) | copy-start | bytes 1572868
  165.4 66.0 %reduce-scatter.2.cloned.1.call-start = ((), (), s32[]{:S(2)}) async-start(), calls=%async_computation.8 | async-start | bytes 1179648 | tf_op jit(solution)/shard_map/reduce_scatter | solution.py:335
  169.0 20.7 %collective-permute-start.7 = (bf16[64,512]{1,0:T(8,128)(2,1)S(1)}, bf16[64,512]{1,0:T(8,128)(2,1)S(1)}, u32[]{:S(2)}, u32[]{:S(2)}) collective-permute-start(bf16[64,512]{1,0:T(8,128)(2,1)S(1)} %get-tuple-element.28), channel_id=1, source_target_pairs={{0,1},{1,2},{2,3},{3,4},{4,5},{5,6},{6,7},{7,0},{8,9},{9,10},{10,1... | collective-permute-start | bytes 196616 | tf_op jit(solution)/shard_map/ppermute | solution.py:230
  172.5 17.2 %collective-permute-start.8 = (bf16[64,512]{1,0:T(8,128)(2,1)S(1)}, bf16[64,512]{1,0:T(8,128)(2,1)S(1)}, u32[]{:S(2)}, u32[]{:S(2)}) collective-permute-start(bf16[64,512]{1,0:T(8,128)(2,1)S(1)} %get-tuple-element.27), channel_id=1, source_target_pairs={{0,2},{1,3},{2,4},{3,5},{4,6},{5,7},{6,0},{7,1},{8,10},{9,11},{10,... | collective-permute-start | bytes 196616 | tf_op jit(solution)/shard_map/ppermute | solution.py:230
  176.6 13.1 %collective-permute-start.9 = (bf16[64,512]{1,0:T(8,128)(2,1)S(1)}, bf16[64,512]{1,0:T(8,128)(2,1)S(1)}, u32[]{:S(2)}, u32[]{:S(2)}) collective-permute-start(bf16[64,512]{1,0:T(8,128)(2,1)S(1)} %get-tuple-element.26), channel_id=1, source_target_pairs={{0,3},{1,4},{2,5},{3,6},{4,7},{5,0},{6,1},{7,2},{8,11},{9,12},{10,... | collective-permute-start | bytes 196616 | tf_op jit(solution)/shard_map/ppermute | solution.py:230
  181.5 9.5 %collective-permute-start.10 = (bf16[64,512]{1,0:T(8,128)(2,1)S(1)}, bf16[64,512]{1,0:T(8,128)(2,1)S(1)}, u32[]{:S(2)}, u32[]{:S(2)}) collective-permute-start(bf16[64,512]{1,0:T(8,128)(2,1)S(1)} %get-tuple-element.25), channel_id=1, source_target_pairs={{0,4},{1,5},{2,6},{3,7},{4,0},{5,1},{6,2},{7,3},{8,12},{9,13},{10,... | collective-permute-start | bytes 196616 | tf_op jit(solution)/shard_map/ppermute | solution.py:230
  185.2 8.0 %collective-permute-start.11 = (bf16[64,512]{1,0:T(8,128)(2,1)S(1)}, bf16[64,512]{1,0:T(8,128)(2,1)S(1)}, u32[]{:S(2)}, u32[]{:S(2)}) collective-permute-start(bf16[64,512]{1,0:T(8,128)(2,1)S(1)} %get-tuple-element.24), channel_id=1, source_target_pairs={{0,5},{1,6},{2,7},{3,0},{4,1},{5,2},{6,3},{7,4},{8,13},{9,14},{10,... | collective-permute-start | bytes 196616 | tf_op jit(solution)/shard_map/ppermute | solution.py:230
  189.6 8.2 %copy-start = (bf16[64,512]{1,0:T(8,128)(2,1)}, bf16[64,512]{1,0:T(8,128)(2,1)S(1)}, u32[]{:S(2)}) copy-start(bf16[64,512]{1,0:T(8,128)(2,1)S(1)} %collective-permute-done.7.refs_1_.refs_0_) | copy-start | bytes 196612
  189.7 8.1 %copy-start.1 = (bf16[64,512]{1,0:T(8,128)(2,1)}, bf16[64,512]{1,0:T(8,128)(2,1)S(1)}, u32[]{:S(2)}) copy-start(bf16[64,512]{1,0:T(8,128)(2,1)S(1)} %collective-permute-done.8.refs_2_.refs_1_) | copy-start | bytes 196612
  189.7 8.1 %copy-start.2 = (bf16[64,512]{1,0:T(8,128)(2,1)}, bf16[64,512]{1,0:T(8,128)(2,1)S(1)}, u32[]{:S(2)}) copy-start(bf16[64,512]{1,0:T(8,128)(2,1)S(1)} %collective-permute-done.9.refs_3_.refs_2_) | copy-start | bytes 196612
  190.9 6.9 %copy-start.3 = (bf16[64,512]{1,0:T(8,128)(2,1)}, bf16[64,512]{1,0:T(8,128)(2,1)S(1)}, u32[]{:S(2)}) copy-start(bf16[64,512]{1,0:T(8,128)(2,1)S(1)} %collective-permute-done.10.refs_4_.refs_3_) | copy-start | bytes 196612
  193.2 4.6 %copy-start.4 = (bf16[64,512]{1,0:T(8,128)(2,1)}, bf16[64,512]{1,0:T(8,128)(2,1)S(1)}, u32[]{:S(2)}) copy-start(bf16[64,512]{1,0:T(8,128)(2,1)S(1)} %collective-permute-done.11.refs_5_.refs_4_) | copy-start | bytes 196612
  197.8 32.8 %all-to-all-start.5 = ((bf16[8,128,512]{2,1,0:T(8,128)(2,1)}), bf16[8,128,512]{2,1,0:T(8,128)(2,1)S(1)}, u32[]{:S(2)}, u32[]{:S(2)}) async-start(bf16[8,128,512]{2,1,0:T(8,128)(2,1)} %bitcast.13), calls=%async_computation.5 | async-start | bytes 2097152 | tf_op jit(solution)/shard_map/all_to_all | solution.py:364
  203.1 9.1 %collective-permute-start.12 = (bf16[64,512]{1,0:T(8,128)(2,1)S(1)}, bf16[64,512]{1,0:T(8,128)(2,1)S(1)}, u32[]{:S(2)}, u32[]{:S(2)}) collective-permute-start(bf16[64,512]{1,0:T(8,128)(2,1)S(1)} %get-tuple-element.23), channel_id=1, source_target_pairs={{0,6},{1,7},{2,0},{3,1},{4,2},{5,3},{6,4},{7,5},{8,14},{9,15},{10,... | collective-permute-start | bytes 196616 | tf_op jit(solution)/shard_map/ppermute | solution.py:230
  207.3 8.2 %collective-permute-start.13 = (bf16[64,512]{1,0:T(8,128)(2,1)S(1)}, bf16[64,512]{1,0:T(8,128)(2,1)S(1)}, u32[]{:S(2)}, u32[]{:S(2)}) collective-permute-start(bf16[64,512]{1,0:T(8,128)(2,1)S(1)} %get-tuple-element.22), channel_id=1, source_target_pairs={{0,7},{1,0},{2,1},{3,2},{4,3},{5,4},{6,5},{7,6},{8,15},{9,8},{10,9... | collective-permute-start | bytes 196616 | tf_op jit(solution)/shard_map/ppermute | solution.py:230
  212.2 3.3 %copy-start.16 = (bf16[64,512]{1,0:T(8,128)(2,1)}, bf16[64,512]{1,0:T(8,128)(2,1)S(1)}, u32[]{:S(2)}) copy-start(bf16[64,512]{1,0:T(8,128)(2,1)S(1)} %collective-permute-done.12.refs_6_) | copy-start | bytes 196612
  215.5 0.6 copy-start.17
Sparse Core Ops, SparseCore 0:
  10.7 45.4 all-gather.1
  169.6 36.1 reduce-scatter.1

commit v6 on v5

--- a/solution.py
+++ b/solution.py
@@ -1,3 +1,5 @@
+import functools
+
 import jax
 import jax.numpy as jnp
 from jax import lax
@@ -37,15 +39,18 @@
     return jnp.where((key_at <= query_at) & (key_at >= start), scores, -jnp.inf)
 
 
-def pack_kernel(codes_ref, context_ref, *refs):
+def pack_kernel(sections, codes_ref, *refs):
     out_ref = refs[-1]
     count, rows, width = out_ref.shape
     first = pl.program_id(0) * count
-    groups = context_ref.shape[0] // rows
+    rows = rows // sections
     for j in range(count):
         column = pl.multiple_of(jnp.maximum(codes_ref[first + j], 0) * width, width)
-        start = (j % groups) * rows
-        out_ref[j] = context_ref[start : start + rows, pl.ds(column, width)]
+        for i, section in enumerate(refs[:sections]):
+            start = (j * rows) % section.shape[0]
+            out_ref[j, i * rows : (i + 1) * rows] = section[
+                start : start + rows, pl.ds(column, width)
+            ]
 
 
 def in_token_order(me, shares, out_ref):
@@ -56,14 +61,30 @@
         out_ref[pl.ds(pl.multiple_of(source * rows, rows), rows), :] = share[...]
 
 
-def tile_of(ref):
-    return ref[...].reshape(-1, ref.shape[-1])
+def key_tile(top, bottom):
+    pieces = top.shape[1]
+    order = [p * CORES + c for c in range(CORES) for p in range(pieces // CORES)]
+    return jnp.concatenate([top[0, i] for i in order] + [bottom[0, c, 0] for c in range(CORES)], axis=0)
+
+
+def value_tile(ref):
+    rows = ref.shape[3] // 2
+    return jnp.concatenate(
+        [ref[0, c, 0, i * rows : (i + 1) * rows] for i in range(2) for c in range(CORES)], axis=0
+    )
 
 
 def store_halves(out_ref, block, part):
     own_x, rows = out_ref.shape[2:4]
+    half = rows // 4
     for c in range(CORES):
-        out_ref[block // own_x, c, lax.rem(block, own_x)] = part[c * rows : (c + 1) * rows]
+        for p in range(2):
+            for i in range(2):
+                at = i * CORES * 2 * half + (c * 2 + p) * half
+                to = (p * 2 + i) * half
+                out_ref[block // own_x, c, lax.rem(block, own_x), to : to + half] = part[
+                    at : at + half
+                ]
 
 
 def assemble_kernel(me_ref, *refs):
@@ -80,10 +101,10 @@
 
 
 def value_grad_kernel(
-    sel_ref, lens_ref, base_ref, q_ref, k_ref, k1_ref, k2_ref, k3_ref, *refs,
+    sel_ref, lens_ref, base_ref, q_ref, k_ref, *refs,
 ):
+    far_k, refs = list(zip(refs[:3], refs[3:6])), refs[6:]
     *shares, near_ref, far_ref, top_ref, inverse_ref, start_ref, scores_ref, g_ref = refs
-    far_k = (k1_ref, k2_ref, k3_ref)
     head = pl.program_id(0)
     rows, width = q_ref.shape
     picks = scores_ref.shape[0] - 1
@@ -98,7 +119,7 @@
     scores_ref[0] = near
     top = jnp.max(near, axis=0, keepdims=True)
     for j in range(picks):
-        far = dot(tile_of(far_k[j]), q, NT)
+        far = dot(key_tile(*far_k[j]), q, NT)
         scores_ref[j + 1] = far
         top = jnp.maximum(top, jnp.max(far, axis=0, keepdims=True))
     total = jnp.zeros((1, rows), jnp.float32)
@@ -122,10 +143,10 @@
 
 def other_grads_kernel(
     sel_ref, lens_ref, base_ref, q_ref, k_ref, v_ref,
-    k1_ref, k2_ref, k3_ref, v1_ref, v2_ref, v3_ref, top_ref, inverse_ref, *refs,
+    *refs,
 ):
-    *shares, attended_ref, query_ref, near_ref, far_ref, start_ref, weights_ref, g_ref = refs
-    far_k, far_v = (k1_ref, k2_ref, k3_ref), (v1_ref, v2_ref, v3_ref)
+    far_k, far_v, (top_ref, inverse_ref) = list(zip(refs[:3], refs[3:6])), refs[6:9], refs[9:11]
+    *shares, attended_ref, query_ref, near_ref, far_ref, start_ref, weights_ref, g_ref = refs[11:]
     head = pl.program_id(0)
     rows, width = q_ref.shape
     picks = weights_ref.shape[0] - 1
@@ -136,10 +157,10 @@
         start_ref[...] = document_starts(lens_ref, base_ref, rows)
 
     def keys_of(j):
-        return k_ref[...] if j == 0 else tile_of(far_k[j - 1])
+        return k_ref[...] if j == 0 else key_tile(*far_k[j - 1])
 
     def values_of(j):
-        return v_ref[...] if j == 0 else tile_of(far_v[j - 1])
+        return v_ref[...] if j == 0 else value_tile(far_v[j - 1])
 
     in_token_order(base_ref[1], shares, g_ref)
     q = q_ref[...]
@@ -172,22 +193,22 @@
     query_ref[...] = query_grad.astype(jnp.bfloat16).T
 
 
-def pack(codes, context, half, groups, width, *after):
+def pack(codes, context, rows, columns, sections, groups, width, *after):
     slots = codes.shape[0]
-    rows, columns = context.shape[0], context.shape[1] // 2
     steps = 4
+    slot_rows = rows // groups * len(sections)
     return pl.pallas_call(
-        pack_kernel,
-        out_shape=jax.ShapeDtypeStruct((slots, rows // groups, width), context.dtype),
+        functools.partial(pack_kernel, len(sections)),
+        out_shape=jax.ShapeDtypeStruct((slots, slot_rows, width), context.dtype),
         grid_spec=pltpu.PrefetchScalarGridSpec(
             num_scalar_prefetch=1,
             grid=(steps,),
-            in_specs=[pl.BlockSpec((rows, columns), lambda i, *_: (0, half))]
+            in_specs=[pl.BlockSpec((rows, columns), lambda i, *_, at=at: (0, at)) for at in sections]
             + [pl.BlockSpec(memory_space=pl.ANY)] * len(after),
-            out_specs=pl.BlockSpec((slots // steps, rows // groups, width), lambda i, *_: (i, 0, 0)),
+            out_specs=pl.BlockSpec((slots // steps, slot_rows, width), lambda i, *_: (i, 0, 0)),
         ),
         compiler_params=pltpu.CompilerParams(vmem_limit_bytes=60 * MIB),
-    )(codes, context, *after)
+    )(codes, *[context] * len(sections), *after)
 
 
 def row_sum_kernel(codes_ref, terms_ref, *refs):
@@ -252,21 +273,17 @@
     blocks = owners // pieces
     my_x, my_y = lax.axis_index("x"), lax.axis_index("y")
     my_piece = lax.axis_index(CTX).astype(jnp.int32)
+    half = piece_rows // 2
+    columns = heads * width
     column = lax.all_gather(
-        jnp.concatenate([context_keys, context_values], axis=1), "y", axis=0, tiled=True
+        jnp.concatenate([context_keys[half:], context_values[:half], context_values[half:]], axis=1),
+        "y",
+        axis=0,
+        tiled=True,
     )
     count = lax.axis_size("head")
     me = lax.axis_index("head").astype(jnp.int32)
     share_rows = rows // count
-    grads = shifted(
-        [
-            lax.dynamic_slice_in_dim(
-                out_grad, lax.rem(me + d, count) * heads * width, heads * width, 1
-            )
-            for d in range(count)
-        ],
-        count,
-    )
     base = jnp.stack([my_piece * rows, me])
     flat = selected.reshape(-1)
 
@@ -275,7 +292,16 @@
     wanted = jnp.max(jnp.where(hits, head_of[None, :], -1), axis=1)
     wanted = jnp.broadcast_to(jnp.pad(wanted, (0, 128 - blocks)), (owners, 128))
     codes = lax.all_to_all(wanted, CTX, split_axis=0, concat_axis=0, tiled=True)
+    settled = codes[0, 127]
+    grads = shifted(
+        [
+            lax.dynamic_slice_in_dim(out_grad, lax.rem(me + d, count) * columns + settled, columns, 1)
+            for d in range(count)
+        ],
+        count,
+    )
     own_x = blocks // SIZE_X
+    piece_codes = lax.dynamic_slice_in_dim(codes, my_piece // pieces, 1, 1)[:, 0]
     row_codes = lax.dynamic_slice(
         codes.reshape(SIZE_X, SIZE_Y, CORES, 128),
         (0, my_y, 0, my_x * own_x),
@@ -286,24 +312,43 @@
     row_shape = (SIZE_X, CORES, own_x, rows // CORES, width)
 
     def along_row(tiles):
-        tiles = tiles.reshape(peers, own_x, rows // CORES, width)
+        tiles = tiles.reshape(peers, own_x, -1, width)
         received = lax.all_to_all(tiles, ("x", "core"), split_axis=0, concat_axis=0, tiled=True)
-        return received.reshape(row_shape)
+        return received.reshape(*row_shape[:3], -1, width)
 
     early = count - 1
-    far_keys = along_row(pack(row_codes, column, 0, own_x, width, *grads[1:early]))
-    packed_values = pack(row_codes, column, 1, own_x, width, *grads[early:])
-    far_values = along_row(gate(packed_values, far_keys[0, 0, 0, :16]))
+    top_keys = lax.all_to_all(
+        pack(piece_codes, context_keys, half, columns, [0], 1, width),
+        CTX,
+        split_axis=0,
+        concat_axis=0,
+        tiled=True,
+    ).reshape(blocks, pieces, half, width)
+    column_rows = SIZE_Y * half
+    packed_keys = pack(row_codes, column, column_rows, columns, [0], own_x, width, *grads[1:early])
+    bottom_keys = along_row(gate(packed_keys, top_keys[0, 0, :16]))
+    packed_values = pack(row_codes, column, column_rows, columns, [1, 2], own_x, width, *grads[early:])
+    far_values = along_row(gate(packed_values, bottom_keys[0, 0, 0, :16]))
 
     by_head = pl.BlockSpec((rows, width), lambda h, *_: (0, h))
     all_far = pl.BlockSpec(row_shape, lambda h, *_: (0, 0, 0, 0, 0))
-    far = [
-        pl.BlockSpec(
-            (1, CORES, 1, rows // CORES, width),
-            lambda h, sel, *_, j=j: (sel[h * picks + j] // own_x, 0, sel[h * picks + j] % own_x, 0, 0),
-        )
+    far_top = [
+        pl.BlockSpec((1, pieces, half, width), lambda h, sel, *_, j=j: (sel[h * picks + j], 0, 0, 0))
         for j in range(picks)
     ]
+
+    def by_row(block_rows):
+        return [
+            pl.BlockSpec(
+                (1, CORES, 1, block_rows, width),
+                lambda h, sel, *_, j=j: (
+                    sel[h * picks + j] // own_x, 0, sel[h * picks + j] % own_x, 0, 0
+                ),
+            )
+            for j in range(picks)
+        ]
+
+    far_bottom, far = by_row(2 * half), by_row(rows // CORES)
     shares = [pl.BlockSpec((share_rows, width), lambda h, *_: (0, h))] * count
     by_stat = pl.BlockSpec((1, 1, rows), lambda h, *_: (h, 0, 0))
     near_shape = jax.ShapeDtypeStruct(queries.shape, jnp.bfloat16)
@@ -321,7 +366,7 @@
         grid_spec=pltpu.PrefetchScalarGridSpec(
             num_scalar_prefetch=3,
             grid=(heads,),
-            in_specs=[by_head, by_head, *far, *shares],
+            in_specs=[by_head, by_head, *far_top, *far_bottom, *shares],
             out_specs=[by_head, all_far, by_stat, by_stat],
             scratch_shapes=scratch,
         ),
@@ -329,7 +374,7 @@
         cost_estimate=pl.CostEstimate(
             flops=2 * tile_flops, bytes_accessed=8 << 20, transcendentals=heads * 4 * rows * rows
         ),
-    )(flat, doc_lengths, base, queries, keys, *[far_keys] * picks, *grads)
+    )(flat, doc_lengths, base, queries, keys, *[top_keys] * picks, *[bottom_keys] * picks, *grads)
     value_terms = along_row(gate(far_value_grads, far_values[0, 0, 0, :16]))
     value_sums = row_sum(row_codes, value_terms.reshape(peers, *row_shape[2:]), heads)
     context_value_grad = lax.psum_scatter(value_sums, "y", scatter_dimension=0, tiled=True)
@@ -340,7 +385,9 @@
         grid_spec=pltpu.PrefetchScalarGridSpec(
             num_scalar_prefetch=3,
             grid=(heads,),
-            in_specs=[by_head, by_head, by_head, *far, *far, by_stat, by_stat, *shares],
+            in_specs=[
+                by_head, by_head, by_head, *far_top, *far_bottom, *far, by_stat, by_stat, *shares
+            ],
             out_specs=[by_head, by_head, by_head, all_far],
             scratch_shapes=scratch,
         ),
@@ -350,7 +397,7 @@
         ),
     )(
         flat, doc_lengths, base, queries, keys, values,
-        *[far_keys] * picks, *[far_values] * picks, top, inverse, *grads,
+        *[top_keys] * picks, *[bottom_keys] * picks, *[far_values] * picks, top, inverse, *grads,
     )
     output_parts = shifted(
         [

time: 241 us -> 254 us (1.054)
  between operations: 14.5 us -> 19.7 us
  local copies, waits for them, and re-layouts: 9.77 us -> 13.5 us
  Pallas kernels: 47.1 us -> 50.1 us
    all_to_all x4, waiting for transfers between devices: 37 us -> 27.1 us  [along_row(): lax.all_to_all(tiles, ('x', 'core'), split_axis=0, concat_axis=0, tiled=T...]
    all_to_all x1, waiting for transfers between devices: 0.01 us -> 9.18 us  [on_device(): codes = lax.all_to_all(wanted, CTX, split_axis=0, concat_axis=0, tiled=True)]
    all_to_all x0 -> x1, starting transfers between devices: none -> 4.76 us  [on_device(): lax.all_to_all(pack(piece_codes, context_keys, half, columns, [0], 1, wid...]
    ppermute x14, starting transfers between devices: 65.2 us -> 61.2 us  [shifted(): lax.ppermute(parts[d], 'head', [(i, (i + d) % count) for i in range(count)])]
    pallas_call x2 -> x3, Pallas kernels: 7.79 us -> 10.4 us  [pack(): pl.pallas_call(functools.partial(pack_kernel, len(sections)), out_shape=j...]
  transfers between devices with their start and end apart: 22 -> 23, of which waited for: 10 -> 12; matrix products, arithmetic and copies ran while one was open for 3% -> 3% of each run, Pallas kernels for 18% -> 19%
where the time goes in v6:
time: 254 us; the launch traced here: 250 us
  starting transfers between devices  104 us (41%)
  waiting for transfers between devices  61.2 us (24%)
  Pallas kernels  50.1 us (20%)
  between operations  19.7 us (8%)
  local copies, waits for them, and re-layouts  13.5 us (5%)
    ppermute x14, starting transfers between devices, shifted(): lax.ppermute(parts[d], 'head', [(i, (i + d) % count) for i in range(count)])  61.2 us
    all_to_all x4, waiting for transfers between devices, along_row(): lax.all_to_all(tiles, ('x', 'core'), split_axis=0, concat_axis=0, tiled=T...  27.1 us
    all_to_all x4, starting transfers between devices, along_row(): lax.all_to_all(tiles, ('x', 'core'), split_axis=0, concat_axis=0, tiled=T...  19.5 us
    pallas_call x1, Pallas kernels, on_device(): pl.pallas_call(other_grads_kernel, out_shape=(near_shape, near_shape, nea...  17.6 us
    pallas_call x1, Pallas kernels, on_device(): pl.pallas_call(value_grad_kernel, out_shape=(near_shape, far_shape, stat_...  12.8 us
    ppermute x14, waiting for transfers between devices, shifted(): lax.ppermute(parts[d], 'head', [(i, (i + d) % count) for i in range(count)])  12.8 us
    all_to_all x1, waiting for transfers between devices, on_device(): lax.all_to_all(key_sums, 'y', split_axis=0, concat_axis=0, tiled=True)  12.1 us
    all_to_all x1, starting transfers between devices, on_device(): codes = lax.all_to_all(wanted, CTX, split_axis=0, concat_axis=0, tiled=True)  11.6 us
  transfers between devices with their start and end apart: 23, of which 12 were waited for; matrix products, arithmetic and copies ran while one was open for 3% of the time, Pallas kernels for 19%

profile of v6, /device:TPU:1, one launch (start us, length us, event | category | flops | bytes accessed | tf_op | source)
XLA Modules:
  0.0 250.4 jit_solution(10297357020456479486)
XLA Ops:
  7.2 0.9 fusion
  8.1 0.8 slice.24
  8.9 0.7 pad_maximum_fusion
  9.7 0.8 copy.22
  11.3 11.6 %all-to-all-start = ((s32[64,1,128]{2,1,0:T(1,128)}), s32[64,1,128]{2,1,0:T(1,128)S(1)}, u32[]{:S(2)}, u32[]{:S(2)}) async-start(s32[64,1,128]{2,1,0:T(1,128)} %broadcast_in_dim.19), calls=%async_computation | async-start | bytes 65536 | tf_op jit(solution)/shard_map/all_to_all | solution.py:294
  22.9 9.2 %all-to-all-done = s32[64,1,128]{2,1,0:T(1,128)S(1)} async-done(((s32[64,1,128]{2,1,0:T(1,128)}), s32[64,1,128]{2,1,0:T(1,128)S(1)}, u32[]{:S(2)}, u32[]{:S(2)}) %all-to-all-start) | async-done | bytes 32800 | tf_op jit(solution)/shard_map/all_to_all | solution.py:294
  32.1 1.8 dynamic-slice_reduce_fusion.codes_ref
  34.0 3.2 %shard_map.127 = bf16[64,64,128]{2,1,0:T(8,128)(2,1)} custom-call(s32[64]{0:T(128)} %dynamic-slice_reduce_fusion.codes_ref, bf16[128,512]{1,0:T(8,128)(2,1)} %refs_0_.1), custom_call_target="tpu_custom_call" | custom-call | tf_op jit(solution)/shard_map/pallas_call | solution.py:200
  37.1 4.8 %all-to-all-start.1 = ((bf16[64,64,128]{2,1,0:T(8,128)(2,1)}), bf16[64,64,128]{2,1,0:T(8,128)(2,1)S(1)}, u32[]{:S(2)}, u32[]{:S(2)}) async-start(bf16[64,64,128]{2,1,0:T(8,128)(2,1)} %shard_map.127), calls=%async_computation.1 | async-start | bytes 2097152 | tf_op jit(solution)/shard_map/all_to_all | solution.py:320
  47.7 0.9 constant_dynamic-slice_fusion.8
  48.6 4.0 %collective-permute-start = (bf16[64,512]{1,0:T(8,128)(2,1)S(1)}, bf16[64,512]{1,0:T(8,128)(2,1)S(1)}, u32[]{:S(2)}, u32[]{:S(2)}) collective-permute-start(bf16[64,512]{1,0:T(8,128)(2,1)S(1)} %get-tuple-element.36), channel_id=1, source_target_pairs={{0,1},{1,2},{2,3},{3,4},{4,5},{5,6},{6,7},{7,0},{8,9},{9,10},{10,1... | collective-permute-start | bytes 196616 | tf_op jit(solution)/shard_map/ppermute | solution.py:251
  53.4 5.8 %collective-permute-start.1 = (bf16[64,512]{1,0:T(8,128)(2,1)S(1)}, bf16[64,512]{1,0:T(8,128)(2,1)S(1)}, u32[]{:S(2)}, u32[]{:S(2)}) collective-permute-start(bf16[64,512]{1,0:T(8,128)(2,1)S(1)} %get-tuple-element.35), channel_id=1, source_target_pairs={{0,2},{1,3},{2,4},{3,5},{4,6},{5,7},{6,0},{7,1},{8,10},{9,11},{10,... | collective-permute-start | bytes 196616 | tf_op jit(solution)/shard_map/ppermute | solution.py:251
  59.2 7.0 %collective-permute-start.2 = (bf16[64,512]{1,0:T(8,128)(2,1)S(1)}, bf16[64,512]{1,0:T(8,128)(2,1)S(1)}, u32[]{:S(2)}, u32[]{:S(2)}) collective-permute-start(bf16[64,512]{1,0:T(8,128)(2,1)S(1)} %get-tuple-element.34), channel_id=1, source_target_pairs={{0,3},{1,4},{2,5},{3,6},{4,7},{5,0},{6,1},{7,2},{8,11},{9,12},{10,... | collective-permute-start | bytes 196616 | tf_op jit(solution)/shard_map/ppermute | solution.py:251
  66.2 2.8 %collective-permute-start.3 = (bf16[64,512]{1,0:T(8,128)(2,1)S(1)}, bf16[64,512]{1,0:T(8,128)(2,1)S(1)}, u32[]{:S(2)}, u32[]{:S(2)}) collective-permute-start(bf16[64,512]{1,0:T(8,128)(2,1)S(1)} %get-tuple-element.33), channel_id=1, source_target_pairs={{0,4},{1,5},{2,6},{3,7},{4,0},{5,1},{6,2},{7,3},{8,12},{9,13},{10,... | collective-permute-start | bytes 196616 | tf_op jit(solution)/shard_map/ppermute | solution.py:251
  69.1 6.4 %collective-permute-start.4 = (bf16[64,512]{1,0:T(8,128)(2,1)S(1)}, bf16[64,512]{1,0:T(8,128)(2,1)S(1)}, u32[]{:S(2)}, u32[]{:S(2)}) collective-permute-start(bf16[64,512]{1,0:T(8,128)(2,1)S(1)} %get-tuple-element.32), channel_id=1, source_target_pairs={{0,5},{1,6},{2,7},{3,0},{4,1},{5,2},{6,3},{7,4},{8,13},{9,14},{10,... | collective-permute-start | bytes 196616 | tf_op jit(solution)/shard_map/ppermute | solution.py:251
  75.5 3.4 %collective-permute-start.5 = (bf16[64,512]{1,0:T(8,128)(2,1)S(1)}, bf16[64,512]{1,0:T(8,128)(2,1)S(1)}, u32[]{:S(2)}, u32[]{:S(2)}) collective-permute-start(bf16[64,512]{1,0:T(8,128)(2,1)S(1)} %get-tuple-element.31), channel_id=1, source_target_pairs={{0,6},{1,7},{2,0},{3,1},{4,2},{5,3},{6,4},{7,5},{8,14},{9,15},{10,... | collective-permute-start | bytes 196616 | tf_op jit(solution)/shard_map/ppermute | solution.py:251
  79.6 0.7 collective-permute-done.4.refs_5_.refs_11_.refs_16_
  80.3 3.9 %collective-permute-done.5.refs_6_.refs_12_.refs_17_ = bf16[64,512]{1,0:T(8,128)(2,1)S(1)} collective-permute-done((bf16[64,512]{1,0:T(8,128)(2,1)S(1)}, bf16[64,512]{1,0:T(8,128)(2,1)S(1)}, u32[]{:S(2)}, u32[]{:S(2)}) %collective-permute-start.5) | collective-permute-done | bytes 65568 | tf_op jit(solution)/shard_map/ppermute | solution.py:251
  84.7 3.4 %shard_map.128.kept_ref = bf16[32,128,128]{2,1,0:T(8,128)(2,1)} custom-call(s32[32]{0:T(128)} %reshape.77.codes_ref, bf16[512,1536]{1,0:T(8,128)(2,1)} %all-gather.2.cloned.1.call-done.refs_0_.refs_1_, bf16[64,512]{1,0:T(8,128)(2,1)} %copy-done.12, bf16[64,512]{1,0:T(8,128)(2,1)} %copy-done.13, bf16[64,512]{1,0:T(8,128)(2,1)} %copy-done.14, ...), custom_call_target="tpu_custom_call" | custom-call | tf_op jit(solution)/shard_map/pallas_call | solution.py:200
  88.1 5.6 %all-to-all-start.2 = ((bf16[8,4,128,128]{3,2,1,0:T(8,128)(2,1)}), bf16[8,4,128,128]{3,2,1,0:T(8,128)(2,1)S(1)}, u32[]{:S(2)}, u32[]{:S(2)}) async-start(bf16[8,4,128,128]{3,2,1,0:T(8,128)(2,1)} %bitcast.26), calls=%async_computation.2 | async-start | bytes 2097152 | tf_op jit(solution)/shard_map/all_to_all | solution.py:316
  93.7 3.7 %collective-permute-start.6 = (bf16[64,512]{1,0:T(8,128)(2,1)S(1)}, bf16[64,512]{1,0:T(8,128)(2,1)S(1)}, u32[]{:S(2)}, u32[]{:S(2)}) collective-permute-start(bf16[64,512]{1,0:T(8,128)(2,1)S(1)} %get-tuple-element.37), channel_id=1, source_target_pairs={{0,7},{1,0},{2,1},{3,2},{4,3},{5,4},{6,5},{7,6},{8,15},{9,8},{10,9... | collective-permute-start | bytes 196616 | tf_op jit(solution)/shard_map/ppermute | solution.py:251
  97.4 1.9 collective-permute-done.6.refs_2_.refs_13_.refs_18_
  99.9 3.9 %shard_map.130.kept_ref = bf16[32,256,128]{2,1,0:T(8,128)(2,1)} custom-call(s32[32]{0:T(128)} %reshape.77.codes_ref, bf16[512,1536]{1,0:T(8,128)(2,1)} %all-gather.2.cloned.1.call-done.refs_0_.refs_1_, bf16[512,1536]{1,0:T(8,128)(2,1)} %all-gather.2.cloned.1.call-done.refs_0_.refs_1_, bf16[64,512]{1,0:T(8,128)(2,1)} %copy-done.11), custom_call_target="tpu_custom_call" | custom-call | tf_op jit(solution)/shard_map/pallas_call | solution.py:200
  103.8 5.0 %all-to-all-done.2 = bf16[8,4,128,128]{3,2,1,0:T(8,128)(2,1)S(1)} async-done(((bf16[8,4,128,128]{3,2,1,0:T(8,128)(2,1)}), bf16[8,4,128,128]{3,2,1,0:T(8,128)(2,1)S(1)}, u32[]{:S(2)}, u32[]{:S(2)}) %all-to-all-start.2) | async-done | bytes 1048608 | tf_op jit(solution)/shard_map/all_to_all | solution.py:316
  109.8 4.4 %all-to-all-start.3 = ((bf16[8,4,256,128]{3,2,1,0:T(8,128)(2,1)}), bf16[8,4,256,128]{3,2,1,0:T(8,128)(2,1)S(1)}, u32[]{:S(2)}, u32[]{:S(2)}) async-start(bf16[8,4,256,128]{3,2,1,0:T(8,128)(2,1)} %bitcast.25), calls=%async_computation.3 | async-start | bytes 4194304 | tf_op jit(solution)/shard_map/all_to_all | solution.py:316
  114.8 12.8 %shard_map.132 = (bf16[512,512]{1,0:T(8,128)(2,1)}, bf16[4,2,4,256,128]{4,3,2,1,0:T(8,128)(2,1)}, f32[4,1,512]{2,1,0:T(1,128)}, f32[4,1,512]{2,1,0:T(1,128)}) custom-call(s32[12]{0:T(128)} %copy-done.20, s32[64]{0:T(128)} %lens_ref.3, s32[2]{0:T(128)} %pad_add_fusion.base_ref, bf16[512,512]{1,0:T(8,128)(2,1)} %q_ref.3, bf16[512,512]{1,0:T(8,128)(2,1)} %k_ref.3, ...), custom_call_target="tpu_custom_call" | custom-call | flops 2147483648 | bytes 8388608 | tf_op jit(solution)/shard_map/pallas_call | solution.py:363
  127.7 12.9 %all-to-all-done.3 = bf16[8,4,256,128]{3,2,1,0:T(8,128)(2,1)S(1)} async-done(((bf16[8,4,256,128]{3,2,1,0:T(8,128)(2,1)}), bf16[8,4,256,128]{3,2,1,0:T(8,128)(2,1)S(1)}, u32[]{:S(2)}, u32[]{:S(2)}) %all-to-all-start.3) | async-done | bytes 2097184 | tf_op jit(solution)/shard_map/all_to_all | solution.py:316
  141.1 0.7 copy-done.6
  141.9 4.4 %all-to-all-start.4 = ((bf16[8,4,256,128]{3,2,1,0:T(8,128)(2,1)}), bf16[8,4,256,128]{3,2,1,0:T(8,128)(2,1)S(1)}, u32[]{:S(2)}, u32[]{:S(2)}) async-start(bf16[8,4,256,128]{3,2,1,0:T(8,128)(2,1)} %bitcast.28), calls=%async_computation.4 | async-start | bytes 4194304 | tf_op jit(solution)/shard_map/all_to_all | solution.py:316
  146.2 17.6 %shard_map.133 = (bf16[512,512]{1,0:T(8,128)(2,1)}, bf16[512,512]{1,0:T(8,128)(2,1)}, bf16[512,512]{1,0:T(8,128)(2,1)}, bf16[4,2,4,256,128]{4,3,2,1,0:T(8,128)(2,1)}) custom-call(s32[12]{0:T(128)} %copy-done.20, s32[64]{0:T(128)} %lens_ref.3, s32[2]{0:T(128)} %pad_add_fusion.base_ref, bf16[512,512]{1,0:T(8,128)(2,1)} %q_ref.3, bf16[512,512]{1,0:T(8,128)(2,1)} %k_ref.3, ...), custom_call_target="tpu_custom_call" | custom-call | flops 5368709120 | bytes 8388608 | tf_op jit(solution)/shard_map/pallas_call | solution.py:382
  163.8 8.8 %all-to-all-done.4.terms_ref = bf16[8,4,256,128]{3,2,1,0:T(8,128)(2,1)S(1)} async-done(((bf16[8,4,256,128]{3,2,1,0:T(8,128)(2,1)}), bf16[8,4,256,128]{3,2,1,0:T(8,128)(2,1)S(1)}, u32[]{:S(2)}, u32[]{:S(2)}) %all-to-all-start.4) | async-done | bytes 2097184 | tf_op jit(solution)/shard_map/all_to_all | solution.py:316
  173.2 5.2 %all-to-all-start.5 = ((bf16[8,4,256,128]{3,2,1,0:T(8,128)(2,1)}), bf16[8,4,256,128]{3,2,1,0:T(8,128)(2,1)}, u32[]{:S(2)}, u32[]{:S(2)}) async-start(bf16[8,4,256,128]{3,2,1,0:T(8,128)(2,1)} %bitcast.27), calls=%async_computation.5 | async-start | bytes 4194304 | tf_op jit(solution)/shard_map/all_to_all | solution.py:316
  178.4 2.8 %shard_map.138 = bf16[1024,512]{1,0:T(8,128)(2,1)} custom-call(s32[32]{0:T(128)S(1)} %copy-done.5, bf16[8,4,256,128]{3,2,1,0:T(8,128)(2,1)S(1)} %all-to-all-done.4.terms_ref), custom_call_target="tpu_custom_call" | custom-call | tf_op jit(solution)/shard_map/pallas_call | solution.py:234
  182.0 1.9 collective-permute-start.7
  183.9 3.2 %collective-permute-start.8 = (bf16[64,512]{1,0:T(8,128)(2,1)S(1)}, bf16[64,512]{1,0:T(8,128)(2,1)S(1)}, u32[]{:S(2)}, u32[]{:S(2)}) collective-permute-start(bf16[64,512]{1,0:T(8,128)(2,1)S(1)} %get-tuple-element.27), channel_id=1, source_target_pairs={{0,2},{1,3},{2,4},{3,5},{4,6},{5,7},{6,0},{7,1},{8,10},{9,11},{10,... | collective-permute-start | bytes 196616 | tf_op jit(solution)/shard_map/ppermute | solution.py:251
  187.2 5.7 %collective-permute-start.9 = (bf16[64,512]{1,0:T(8,128)(2,1)S(1)}, bf16[64,512]{1,0:T(8,128)(2,1)S(1)}, u32[]{:S(2)}, u32[]{:S(2)}) collective-permute-start(bf16[64,512]{1,0:T(8,128)(2,1)S(1)} %get-tuple-element.26), channel_id=1, source_target_pairs={{0,3},{1,4},{2,5},{3,6},{4,7},{5,0},{6,1},{7,2},{8,11},{9,12},{10,... | collective-permute-start | bytes 196616 | tf_op jit(solution)/shard_map/ppermute | solution.py:251
  192.9 3.8 %collective-permute-start.10 = (bf16[64,512]{1,0:T(8,128)(2,1)S(1)}, bf16[64,512]{1,0:T(8,128)(2,1)S(1)}, u32[]{:S(2)}, u32[]{:S(2)}) collective-permute-start(bf16[64,512]{1,0:T(8,128)(2,1)S(1)} %get-tuple-element.25), channel_id=1, source_target_pairs={{0,4},{1,5},{2,6},{3,7},{4,0},{5,1},{6,2},{7,3},{8,12},{9,13},{10,... | collective-permute-start | bytes 196616 | tf_op jit(solution)/shard_map/ppermute | solution.py:251
  196.6 4.5 %collective-permute-start.11 = (bf16[64,512]{1,0:T(8,128)(2,1)S(1)}, bf16[64,512]{1,0:T(8,128)(2,1)S(1)}, u32[]{:S(2)}, u32[]{:S(2)}) collective-permute-start(bf16[64,512]{1,0:T(8,128)(2,1)S(1)} %get-tuple-element.24), channel_id=1, source_target_pairs={{0,5},{1,6},{2,7},{3,0},{4,1},{5,2},{6,3},{7,4},{8,13},{9,14},{10,... | collective-permute-start | bytes 196616 | tf_op jit(solution)/shard_map/ppermute | solution.py:251
  201.2 1.2 collective-permute-done.10.refs_4_.refs_3_
  202.4 1.9 collective-permute-done.11.refs_5_.refs_4_
  204.9 4.5 %shard_map.137 = bf16[1024,512]{1,0:T(8,128)(2,1)} custom-call(s32[32]{0:T(128)S(1)} %copy-done.5, bf16[8,4,256,128]{3,2,1,0:T(8,128)(2,1)} %all-to-all-done.5.terms_ref, bf16[64,512]{1,0:T(8,128)(2,1)S(1)} %collective-permute-done.7.refs_1_.refs_0_, bf16[64,512]{1,0:T(8,128)(2,1)S(1)} %collective-permute-done.8.refs_2_.refs_1_, ...), custom_call_target="tpu_custom_call" | custom-call | tf_op jit(solution)/shard_map/pallas_call | solution.py:234
  209.4 6.4 %all-to-all-start.6 = ((bf16[8,128,512]{2,1,0:T(8,128)(2,1)}), bf16[8,128,512]{2,1,0:T(8,128)(2,1)S(1)}, u32[]{:S(2)}, u32[]{:S(2)}) async-start(bf16[8,128,512]{2,1,0:T(8,128)(2,1)} %bitcast.17), calls=%async_computation.6 | async-start | bytes 2097152 | tf_op jit(solution)/shard_map/all_to_all | solution.py:411
  215.9 4.7 %collective-permute-start.12 = (bf16[64,512]{1,0:T(8,128)(2,1)S(1)}, bf16[64,512]{1,0:T(8,128)(2,1)S(1)}, u32[]{:S(2)}, u32[]{:S(2)}) collective-permute-start(bf16[64,512]{1,0:T(8,128)(2,1)S(1)} %get-tuple-element.23), channel_id=1, source_target_pairs={{0,6},{1,7},{2,0},{3,1},{4,2},{5,3},{6,4},{7,5},{8,14},{9,15},{10,... | collective-permute-start | bytes 196616 | tf_op jit(solution)/shard_map/ppermute | solution.py:251
  220.6 4.3 %collective-permute-start.13 = (bf16[64,512]{1,0:T(8,128)(2,1)S(1)}, bf16[64,512]{1,0:T(8,128)(2,1)S(1)}, u32[]{:S(2)}, u32[]{:S(2)}) collective-permute-start(bf16[64,512]{1,0:T(8,128)(2,1)S(1)} %get-tuple-element.22), channel_id=1, source_target_pairs={{0,7},{1,0},{2,1},{3,2},{4,3},{5,4},{6,5},{7,6},{8,15},{9,8},{10,9... | collective-permute-start | bytes 196616 | tf_op jit(solution)/shard_map/ppermute | solution.py:251
  224.9 3.3 %collective-permute-done.13.refs_7_ = bf16[64,512]{1,0:T(8,128)(2,1)S(1)} collective-permute-done((bf16[64,512]{1,0:T(8,128)(2,1)S(1)}, bf16[64,512]{1,0:T(8,128)(2,1)S(1)}, u32[]{:S(2)}, u32[]{:S(2)}) %collective-permute-start.13) | collective-permute-done | bytes 65568 | tf_op jit(solution)/shard_map/ppermute | solution.py:251
  228.8 1.9 shard_map.134
  230.7 12.1 %all-to-all-done.6 = bf16[8,128,512]{2,1,0:T(8,128)(2,1)S(1)} async-done(((bf16[8,128,512]{2,1,0:T(8,128)(2,1)}), bf16[8,128,512]{2,1,0:T(8,128)(2,1)S(1)}, u32[]{:S(2)}, u32[]{:S(2)}) %all-to-all-start.6) | async-done | bytes 1048608 | tf_op jit(solution)/shard_map/all_to_all | solution.py:411
  242.7 0.8 reduce_sum.12
  (75 shorter events, 8.9 us)
Async XLA Ops:
  7.2 77.0 %all-gather.2.cloned.1.call-start = ((), (), s32[]{:S(2)}) async-start(), calls=%async_computation.8 | async-start | bytes 1769472 | tf_op jit(solution)/shard_map/all_gather | solution.py:278
  8.9 38.8 %copy-start.9 = (bf16[64,4096]{1,0:T(8,128)(2,1)S(1)}, bf16[64,4096]{1,0:T(8,128)(2,1)}, u32[]{:S(2)}) copy-start(bf16[64,4096]{1,0:T(8,128)(2,1)} %param.11) | copy-start | bytes 1572868
  10.5 38.1 %copy-start.20 = (s32[12]{0:T(128)}, s32[12]{0:T(128)S(1)}, u32[]{:S(2)}) copy-start(s32[12]{0:T(128)S(1)} %reshape.74.sel_ref) | copy-start | bytes 148
  11.3 20.8 %all-to-all-start = ((s32[64,1,128]{2,1,0:T(1,128)}), s32[64,1,128]{2,1,0:T(1,128)S(1)}, u32[]{:S(2)}, u32[]{:S(2)}) async-start(s32[64,1,128]{2,1,0:T(1,128)} %broadcast_in_dim.19), calls=%async_computation | async-start | bytes 65536 | tf_op jit(solution)/shard_map/all_to_all | solution.py:294
  37.1 41.7 %all-to-all-start.1 = ((bf16[64,64,128]{2,1,0:T(8,128)(2,1)}), bf16[64,64,128]{2,1,0:T(8,128)(2,1)S(1)}, u32[]{:S(2)}, u32[]{:S(2)}) async-start(bf16[64,64,128]{2,1,0:T(8,128)(2,1)} %shard_map.127), calls=%async_computation.1 | async-start | bytes 2097152 | tf_op jit(solution)/shard_map/all_to_all | solution.py:320
  48.6 26.8 %collective-permute-start = (bf16[64,512]{1,0:T(8,128)(2,1)S(1)}, bf16[64,512]{1,0:T(8,128)(2,1)S(1)}, u32[]{:S(2)}, u32[]{:S(2)}) collective-permute-start(bf16[64,512]{1,0:T(8,128)(2,1)S(1)} %get-tuple-element.36), channel_id=1, source_target_pairs={{0,1},{1,2},{2,3},{3,4},{4,5},{5,6},{6,7},{7,0},{8,9},{9,10},{10,1... | collective-permute-start | bytes 196616 | tf_op jit(solution)/shard_map/ppermute | solution.py:251
  53.4 26.1 %collective-permute-start.1 = (bf16[64,512]{1,0:T(8,128)(2,1)S(1)}, bf16[64,512]{1,0:T(8,128)(2,1)S(1)}, u32[]{:S(2)}, u32[]{:S(2)}) collective-permute-start(bf16[64,512]{1,0:T(8,128)(2,1)S(1)} %get-tuple-element.35), channel_id=1, source_target_pairs={{0,2},{1,3},{2,4},{3,5},{4,6},{5,7},{6,0},{7,1},{8,10},{9,11},{10,... | collective-permute-start | bytes 196616 | tf_op jit(solution)/shard_map/ppermute | solution.py:251
  59.2 20.3 %collective-permute-start.2 = (bf16[64,512]{1,0:T(8,128)(2,1)S(1)}, bf16[64,512]{1,0:T(8,128)(2,1)S(1)}, u32[]{:S(2)}, u32[]{:S(2)}) collective-permute-start(bf16[64,512]{1,0:T(8,128)(2,1)S(1)} %get-tuple-element.34), channel_id=1, source_target_pairs={{0,3},{1,4},{2,5},{3,6},{4,7},{5,0},{6,1},{7,2},{8,11},{9,12},{10,... | collective-permute-start | bytes 196616 | tf_op jit(solution)/shard_map/ppermute | solution.py:251
  66.2 13.3 %collective-permute-start.3 = (bf16[64,512]{1,0:T(8,128)(2,1)S(1)}, bf16[64,512]{1,0:T(8,128)(2,1)S(1)}, u32[]{:S(2)}, u32[]{:S(2)}) collective-permute-start(bf16[64,512]{1,0:T(8,128)(2,1)S(1)} %get-tuple-element.33), channel_id=1, source_target_pairs={{0,4},{1,5},{2,6},{3,7},{4,0},{5,1},{6,2},{7,3},{8,12},{9,13},{10,... | collective-permute-start | bytes 196616 | tf_op jit(solution)/shard_map/ppermute | solution.py:251
  69.1 11.2 %collective-permute-start.4 = (bf16[64,512]{1,0:T(8,128)(2,1)S(1)}, bf16[64,512]{1,0:T(8,128)(2,1)S(1)}, u32[]{:S(2)}, u32[]{:S(2)}) collective-permute-start(bf16[64,512]{1,0:T(8,128)(2,1)S(1)} %get-tuple-element.32), channel_id=1, source_target_pairs={{0,5},{1,6},{2,7},{3,0},{4,1},{5,2},{6,3},{7,4},{8,13},{9,14},{10,... | collective-permute-start | bytes 196616 | tf_op jit(solution)/shard_map/ppermute | solution.py:251
  75.5 8.7 %copy-start.12 = (bf16[64,512]{1,0:T(8,128)(2,1)}, bf16[64,512]{1,0:T(8,128)(2,1)S(1)}, u32[]{:S(2)}) copy-start(bf16[64,512]{1,0:T(8,128)(2,1)S(1)} %collective-permute-done.refs_1_.refs_7_.refs_12_) | copy-start | bytes 196612
  75.5 8.6 %collective-permute-start.5 = (bf16[64,512]{1,0:T(8,128)(2,1)S(1)}, bf16[64,512]{1,0:T(8,128)(2,1)S(1)}, u32[]{:S(2)}, u32[]{:S(2)}) collective-permute-start(bf16[64,512]{1,0:T(8,128)(2,1)S(1)} %get-tuple-element.31), channel_id=1, source_target_pairs={{0,6},{1,7},{2,0},{3,1},{4,2},{5,3},{6,4},{7,5},{8,14},{9,15},{10,... | collective-permute-start | bytes 196616 | tf_op jit(solution)/shard_map/ppermute | solution.py:251
  78.9 9.2 %copy-start.7 = (bf16[64,64,128]{2,1,0:T(8,128)(2,1)}, bf16[64,64,128]{2,1,0:T(8,128)(2,1)S(1)}, u32[]{:S(2)}) copy-start(bf16[64,64,128]{2,1,0:T(8,128)(2,1)S(1)} %all-to-all-done.1) | copy-start | bytes 3145732
  79.5 4.6 %copy-start.13 = (bf16[64,512]{1,0:T(8,128)(2,1)}, bf16[64,512]{1,0:T(8,128)(2,1)S(1)}, u32[]{:S(2)}) copy-start(bf16[64,512]{1,0:T(8,128)(2,1)S(1)} %collective-permute-done.1.refs_2_.refs_8_.refs_13_) | copy-start | bytes 196612
  79.5 4.6 %copy-start.14 = (bf16[64,512]{1,0:T(8,128)(2,1)}, bf16[64,512]{1,0:T(8,128)(2,1)S(1)}, u32[]{:S(2)}) copy-start(bf16[64,512]{1,0:T(8,128)(2,1)S(1)} %collective-permute-done.2.refs_3_.refs_9_.refs_14_) | copy-start | bytes 196612
  79.6 4.6 %copy-start.15 = (bf16[64,512]{1,0:T(8,128)(2,1)}, bf16[64,512]{1,0:T(8,128)(2,1)S(1)}, u32[]{:S(2)}) copy-start(bf16[64,512]{1,0:T(8,128)(2,1)S(1)} %collective-permute-done.3.refs_4_.refs_10_.refs_15_) | copy-start | bytes 196612
  80.3 3.9 %copy-start.16 = (bf16[64,512]{1,0:T(8,128)(2,1)}, bf16[64,512]{1,0:T(8,128)(2,1)S(1)}, u32[]{:S(2)}) copy-start(bf16[64,512]{1,0:T(8,128)(2,1)S(1)} %collective-permute-done.4.refs_5_.refs_11_.refs_16_) | copy-start | bytes 196612
  84.1 0.6 copy-start.17
  88.1 20.7 %all-to-all-start.2 = ((bf16[8,4,128,128]{3,2,1,0:T(8,128)(2,1)}), bf16[8,4,128,128]{3,2,1,0:T(8,128)(2,1)S(1)}, u32[]{:S(2)}, u32[]{:S(2)}) async-start(bf16[8,4,128,128]{3,2,1,0:T(8,128)(2,1)} %bitcast.26), calls=%async_computation.2 | async-start | bytes 2097152 | tf_op jit(solution)/shard_map/all_to_all | solution.py:316
  93.7 5.6 %collective-permute-start.6 = (bf16[64,512]{1,0:T(8,128)(2,1)S(1)}, bf16[64,512]{1,0:T(8,128)(2,1)S(1)}, u32[]{:S(2)}, u32[]{:S(2)}) collective-permute-start(bf16[64,512]{1,0:T(8,128)(2,1)S(1)} %get-tuple-element.37), channel_id=1, source_target_pairs={{0,7},{1,0},{2,1},{3,2},{4,3},{5,4},{6,5},{7,6},{8,15},{9,8},{10,9... | collective-permute-start | bytes 196616 | tf_op jit(solution)/shard_map/ppermute | solution.py:251
  99.3 0.6 copy-start.11
  108.8 1.0 copy-start.8
  109.8 30.7 %all-to-all-start.3 = ((bf16[8,4,256,128]{3,2,1,0:T(8,128)(2,1)}), bf16[8,4,256,128]{3,2,1,0:T(8,128)(2,1)S(1)}, u32[]{:S(2)}, u32[]{:S(2)}) async-start(bf16[8,4,256,128]{3,2,1,0:T(8,128)(2,1)} %bitcast.25), calls=%async_computation.3 | async-start | bytes 4194304 | tf_op jit(solution)/shard_map/all_to_all | solution.py:316
  140.5 1.3 copy-start.6
  141.9 30.7 %all-to-all-start.4 = ((bf16[8,4,256,128]{3,2,1,0:T(8,128)(2,1)}), bf16[8,4,256,128]{3,2,1,0:T(8,128)(2,1)S(1)}, u32[]{:S(2)}, u32[]{:S(2)}) async-start(bf16[8,4,256,128]{3,2,1,0:T(8,128)(2,1)} %bitcast.28), calls=%async_computation.4 | async-start | bytes 4194304 | tf_op jit(solution)/shard_map/all_to_all | solution.py:316
  173.2 5.2 %copy-start.5 = (s32[32]{0:T(128)S(1)}, s32[32]{0:T(128)}, u32[]{:S(2)}) copy-start(s32[32]{0:T(128)} %reshape.77.codes_ref) | copy-start | bytes 388
  173.2 31.7 %all-to-all-start.5 = ((bf16[8,4,256,128]{3,2,1,0:T(8,128)(2,1)}), bf16[8,4,256,128]{3,2,1,0:T(8,128)(2,1)}, u32[]{:S(2)}, u32[]{:S(2)}) async-start(bf16[8,4,256,128]{3,2,1,0:T(8,128)(2,1)} %bitcast.27), calls=%async_computation.5 | async-start | bytes 4194304 | tf_op jit(solution)/shard_map/all_to_all | solution.py:316
  178.4 2.9 %copy-start.10 = (bf16[512,512]{1,0:T(8,128)(2,1)S(1)}, bf16[512,512]{1,0:T(8,128)(2,1)}, u32[]{:S(2)}) copy-start(bf16[512,512]{1,0:T(8,128)(2,1)} %get-tuple-element.16) | copy-start | bytes 1572868
  178.4 65.1 %reduce-scatter.2.cloned.1.call-start = ((), (), s32[]{:S(2)}) async-start(), calls=%async_computation.9 | async-start | bytes 1179648 | tf_op jit(solution)/shard_map/reduce_scatter | solution.py:380
  182.0 19.1 %collective-permute-start.7 = (bf16[64,512]{1,0:T(8,128)(2,1)S(1)}, bf16[64,512]{1,0:T(8,128)(2,1)S(1)}, u32[]{:S(2)}, u32[]{:S(2)}) collective-permute-start(bf16[64,512]{1,0:T(8,128)(2,1)S(1)} %get-tuple-element.28), channel_id=1, source_target_pairs={{0,1},{1,2},{2,3},{3,4},{4,5},{5,6},{6,7},{7,0},{8,9},{9,10},{10,1... | collective-permute-start | bytes 196616 | tf_op jit(solution)/shard_map/ppermute | solution.py:251
  183.9 17.3 %collective-permute-start.8 = (bf16[64,512]{1,0:T(8,128)(2,1)S(1)}, bf16[64,512]{1,0:T(8,128)(2,1)S(1)}, u32[]{:S(2)}, u32[]{:S(2)}) collective-permute-start(bf16[64,512]{1,0:T(8,128)(2,1)S(1)} %get-tuple-element.27), channel_id=1, source_target_pairs={{0,2},{1,3},{2,4},{3,5},{4,6},{5,7},{6,0},{7,1},{8,10},{9,11},{10,... | collective-permute-start | bytes 196616 | tf_op jit(solution)/shard_map/ppermute | solution.py:251
  187.2 14.0 %collective-permute-start.9 = (bf16[64,512]{1,0:T(8,128)(2,1)S(1)}, bf16[64,512]{1,0:T(8,128)(2,1)S(1)}, u32[]{:S(2)}, u32[]{:S(2)}) collective-permute-start(bf16[64,512]{1,0:T(8,128)(2,1)S(1)} %get-tuple-element.26), channel_id=1, source_target_pairs={{0,3},{1,4},{2,5},{3,6},{4,7},{5,0},{6,1},{7,2},{8,11},{9,12},{10,... | collective-permute-start | bytes 196616 | tf_op jit(solution)/shard_map/ppermute | solution.py:251
  192.9 9.5 %collective-permute-start.10 = (bf16[64,512]{1,0:T(8,128)(2,1)S(1)}, bf16[64,512]{1,0:T(8,128)(2,1)S(1)}, u32[]{:S(2)}, u32[]{:S(2)}) collective-permute-start(bf16[64,512]{1,0:T(8,128)(2,1)S(1)} %get-tuple-element.25), channel_id=1, source_target_pairs={{0,4},{1,5},{2,6},{3,7},{4,0},{5,1},{6,2},{7,3},{8,12},{9,13},{10,... | collective-permute-start | bytes 196616 | tf_op jit(solution)/shard_map/ppermute | solution.py:251
  196.6 7.7 %collective-permute-start.11 = (bf16[64,512]{1,0:T(8,128)(2,1)S(1)}, bf16[64,512]{1,0:T(8,128)(2,1)S(1)}, u32[]{:S(2)}, u32[]{:S(2)}) collective-permute-start(bf16[64,512]{1,0:T(8,128)(2,1)S(1)} %get-tuple-element.24), channel_id=1, source_target_pairs={{0,5},{1,6},{2,7},{3,0},{4,1},{5,2},{6,3},{7,4},{8,13},{9,14},{10,... | collective-permute-start | bytes 196616 | tf_op jit(solution)/shard_map/ppermute | solution.py:251
  201.2 8.3 %copy-start = (bf16[64,512]{1,0:T(8,128)(2,1)}, bf16[64,512]{1,0:T(8,128)(2,1)S(1)}, u32[]{:S(2)}) copy-start(bf16[64,512]{1,0:T(8,128)(2,1)S(1)} %collective-permute-done.7.refs_1_.refs_0_) | copy-start | bytes 196612
  201.2 8.2 %copy-start.1 = (bf16[64,512]{1,0:T(8,128)(2,1)}, bf16[64,512]{1,0:T(8,128)(2,1)S(1)}, u32[]{:S(2)}) copy-start(bf16[64,512]{1,0:T(8,128)(2,1)S(1)} %collective-permute-done.8.refs_2_.refs_1_) | copy-start | bytes 196612
  201.2 8.2 %copy-start.2 = (bf16[64,512]{1,0:T(8,128)(2,1)}, bf16[64,512]{1,0:T(8,128)(2,1)S(1)}, u32[]{:S(2)}) copy-start(bf16[64,512]{1,0:T(8,128)(2,1)S(1)} %collective-permute-done.9.refs_3_.refs_2_) | copy-start | bytes 196612
  202.4 7.0 %copy-start.3 = (bf16[64,512]{1,0:T(8,128)(2,1)}, bf16[64,512]{1,0:T(8,128)(2,1)S(1)}, u32[]{:S(2)}) copy-start(bf16[64,512]{1,0:T(8,128)(2,1)S(1)} %collective-permute-done.10.refs_4_.refs_3_) | copy-start | bytes 196612
  204.3 5.1 %copy-start.4 = (bf16[64,512]{1,0:T(8,128)(2,1)}, bf16[64,512]{1,0:T(8,128)(2,1)S(1)}, u32[]{:S(2)}) copy-start(bf16[64,512]{1,0:T(8,128)(2,1)S(1)} %collective-permute-done.11.refs_5_.refs_4_) | copy-start | bytes 196612
  209.4 33.3 %all-to-all-start.6 = ((bf16[8,128,512]{2,1,0:T(8,128)(2,1)}), bf16[8,128,512]{2,1,0:T(8,128)(2,1)S(1)}, u32[]{:S(2)}, u32[]{:S(2)}) async-start(bf16[8,128,512]{2,1,0:T(8,128)(2,1)} %bitcast.17), calls=%async_computation.6 | async-start | bytes 2097152 | tf_op jit(solution)/shard_map/all_to_all | solution.py:411
  215.9 9.0 %collective-permute-start.12 = (bf16[64,512]{1,0:T(8,128)(2,1)S(1)}, bf16[64,512]{1,0:T(8,128)(2,1)S(1)}, u32[]{:S(2)}, u32[]{:S(2)}) collective-permute-start(bf16[64,512]{1,0:T(8,128)(2,1)S(1)} %get-tuple-element.23), channel_id=1, source_target_pairs={{0,6},{1,7},{2,0},{3,1},{4,2},{5,3},{6,4},{7,5},{8,14},{9,15},{10,... | collective-permute-start | bytes 196616 | tf_op jit(solution)/shard_map/ppermute | solution.py:251
  220.6 7.6 %collective-permute-start.13 = (bf16[64,512]{1,0:T(8,128)(2,1)S(1)}, bf16[64,512]{1,0:T(8,128)(2,1)S(1)}, u32[]{:S(2)}, u32[]{:S(2)}) collective-permute-start(bf16[64,512]{1,0:T(8,128)(2,1)S(1)} %get-tuple-element.22), channel_id=1, source_target_pairs={{0,7},{1,0},{2,1},{3,2},{4,3},{5,4},{6,5},{7,6},{8,15},{9,8},{10,9... | collective-permute-start | bytes 196616 | tf_op jit(solution)/shard_map/ppermute | solution.py:251
  224.9 3.3 %copy-start.18 = (bf16[64,512]{1,0:T(8,128)(2,1)}, bf16[64,512]{1,0:T(8,128)(2,1)S(1)}, u32[]{:S(2)}) copy-start(bf16[64,512]{1,0:T(8,128)(2,1)S(1)} %collective-permute-done.12.refs_6_) | copy-start | bytes 196612
  228.2 0.6 copy-start.19
Sparse Core Ops, SparseCore 0:
  10.7 56.5 all-gather.1
  182.6 35.0 reduce-scatter.1

commit v7 on v5

--- a/solution.py
+++ b/solution.py
@@ -39,13 +39,16 @@
 
 def pack_kernel(codes_ref, context_ref, *refs):
     out_ref = refs[-1]
-    count, rows, width = out_ref.shape
+    count, out_rows, width = out_ref.shape
+    pieces, _, rows, _ = context_ref.shape
     first = pl.program_id(0) * count
-    groups = context_ref.shape[0] // rows
+    each = out_rows // rows
     for j in range(count):
         column = pl.multiple_of(jnp.maximum(codes_ref[first + j], 0) * width, width)
-        start = (j % groups) * rows
-        out_ref[j] = context_ref[start : start + rows, pl.ds(column, width)]
+        for p in range(each):
+            out_ref[j, p * rows : (p + 1) * rows] = context_ref[
+                (j * each + p) % pieces, 0, :, pl.ds(column, width)
+            ]
 
 
 def in_token_order(me, shares, out_ref):
@@ -174,17 +177,18 @@
 
 def pack(codes, context, half, groups, width, *after):
     slots = codes.shape[0]
-    rows, columns = context.shape[0], context.shape[1] // 2
+    pieces, _, rows, columns = context.shape
+    slot_rows = pieces // groups * rows
     steps = 4
     return pl.pallas_call(
         pack_kernel,
-        out_shape=jax.ShapeDtypeStruct((slots, rows // groups, width), context.dtype),
+        out_shape=jax.ShapeDtypeStruct((slots, slot_rows, width), context.dtype),
         grid_spec=pltpu.PrefetchScalarGridSpec(
             num_scalar_prefetch=1,
             grid=(steps,),
-            in_specs=[pl.BlockSpec((rows, columns), lambda i, *_: (0, half))]
+            in_specs=[pl.BlockSpec((pieces, 1, rows, columns), lambda i, *_: (0, half, 0, 0))]
             + [pl.BlockSpec(memory_space=pl.ANY)] * len(after),
-            out_specs=pl.BlockSpec((slots // steps, rows // groups, width), lambda i, *_: (i, 0, 0)),
+            out_specs=pl.BlockSpec((slots // steps, slot_rows, width), lambda i, *_: (i, 0, 0)),
         ),
         compiler_params=pltpu.CompilerParams(vmem_limit_bytes=60 * MIB),
     )(codes, context, *after)
@@ -252,9 +256,7 @@
     blocks = owners // pieces
     my_x, my_y = lax.axis_index("x"), lax.axis_index("y")
     my_piece = lax.axis_index(CTX).astype(jnp.int32)
-    column = lax.all_gather(
-        jnp.concatenate([context_keys, context_values], axis=1), "y", axis=0, tiled=True
-    )
+    column = lax.all_gather(jnp.stack([context_keys, context_values]), "y", axis=0)
     count = lax.axis_size("head")
     me = lax.axis_index("head").astype(jnp.int32)
     share_rows = rows // count
@@ -360,7 +362,7 @@
         count,
     )
     key_terms = along_row(gate(far_key_grads, value_terms[0, 0, 0, :16]))
-    key_sums = row_sum(row_codes, key_terms.reshape(peers, *row_shape[2:]), heads, *output_parts[1:6])
+    key_sums = row_sum(row_codes, key_terms.reshape(peers, *row_shape[2:]), heads, *output_parts[1:4])
     key_sums = lax.all_to_all(key_sums, "y", split_axis=0, concat_axis=0, tiled=True)
     key_sums = key_sums.reshape(SIZE_Y, piece_rows, heads * width).astype(jnp.float32)
     context_key_grad = jnp.sum(key_sums, axis=0).astype(jnp.bfloat16)

time: 241 us -> 239 us (level)
    all_to_all x1, waiting for transfers between devices: 12.7 us -> 5.81 us  [on_device(): lax.all_to_all(key_sums, 'y', split_axis=0, concat_axis=0, tiled=True)]
    all_to_all x4, waiting for transfers between devices: 37 us -> 43.6 us  [along_row(): lax.all_to_all(tiles, ('x', 'core'), split_axis=0, concat_axis=0, tiled=T...]
  transfers between devices with their start and end apart: 22 -> 22, of which waited for: 10 -> 11; matrix products, arithmetic and copies ran while one was open for 3% -> 3% of each run, Pallas kernels for 18% -> 18%
where the time goes in v7:
time: 239 us; the launch traced here: 238 us
  starting transfers between devices  101 us (42%)
  waiting for transfers between devices  61.6 us (26%)
  Pallas kernels  47.1 us (20%)
  between operations  14.5 us (6%)
  local copies, waits for them, and re-layouts  9.76 us (4%)
  other arithmetic  3.29 us (1%)
    ppermute x14, starting transfers between devices, shifted(): lax.ppermute(parts[d], 'head', [(i, (i + d) % count) for i in range(count)])  64.2 us
    all_to_all x4, waiting for transfers between devices, along_row(): lax.all_to_all(tiles, ('x', 'core'), split_axis=0, concat_axis=0, tiled=T...  43.6 us
    all_to_all x4, starting transfers between devices, along_row(): lax.all_to_all(tiles, ('x', 'core'), split_axis=0, concat_axis=0, tiled=T...  20 us
    pallas_call x1, Pallas kernels, on_device(): pl.pallas_call(other_grads_kernel, out_shape=(near_shape, near_shape, nea...  17.4 us
    pallas_call x1, Pallas kernels, on_device(): pl.pallas_call(value_grad_kernel, out_shape=(near_shape, far_shape, stat_...  12.7 us
    ppermute x14, waiting for transfers between devices, shifted(): lax.ppermute(parts[d], 'head', [(i, (i + d) % count) for i in range(count)])  12.1 us
    all_to_all x1, starting transfers between devices, on_device(): codes = lax.all_to_all(wanted, CTX, split_axis=0, concat_axis=0, tiled=True)  11.1 us
    pallas_call x2, Pallas kernels, pack(): pl.pallas_call(pack_kernel, out_shape=jax.ShapeDtypeStruct((slots, slot_r...  7.81 us
  transfers between devices with their start and end apart: 22, of which 11 were waited for; matrix products, arithmetic and copies ran while one was open for 3% of the time, Pallas kernels for 18%

profile of v7, /device:TPU:1, one launch (start us, length us, event | category | flops | bytes accessed | tf_op | source)
XLA Modules:
  0.0 237.5 jit_solution(5560714693976916494)
XLA Ops:
  7.2 1.7 pad_maximum_fusion
  9.0 1.7 constant_dynamic-slice_fusion.8
  10.7 4.8 %collective-permute-start = (bf16[64,512]{1,0:T(8,128)(2,1)S(1)}, bf16[64,512]{1,0:T(8,128)(2,1)S(1)}, u32[]{:S(2)}, u32[]{:S(2)}) collective-permute-start(bf16[64,512]{1,0:T(8,128)(2,1)S(1)} %get-tuple-element.36), channel_id=1, source_target_pairs={{0,1},{1,2},{2,3},{3,4},{4,5},{5,6},{6,7},{7,0},{8,9},{9,10},{10,1... | collective-permute-start | bytes 196616 | tf_op jit(solution)/shard_map/ppermute | solution.py:234
  15.6 0.8 copy.20
  16.6 0.6 broadcast_in_dim.19
  17.2 11.1 %all-to-all-start = ((s32[64,1,128]{2,1,0:T(1,128)}), s32[64,1,128]{2,1,0:T(1,128)S(1)}, u32[]{:S(2)}, u32[]{:S(2)}) async-start(s32[64,1,128]{2,1,0:T(1,128)} %broadcast_in_dim.19), calls=%async_computation | async-start | bytes 65536 | tf_op jit(solution)/shard_map/all_to_all | solution.py:279
  28.3 5.8 %collective-permute-start.1 = (bf16[64,512]{1,0:T(8,128)(2,1)S(1)}, bf16[64,512]{1,0:T(8,128)(2,1)S(1)}, u32[]{:S(2)}, u32[]{:S(2)}) collective-permute-start(bf16[64,512]{1,0:T(8,128)(2,1)S(1)} %get-tuple-element.35), channel_id=1, source_target_pairs={{0,2},{1,3},{2,4},{3,5},{4,6},{5,7},{6,0},{7,1},{8,10},{9,11},{10,... | collective-permute-start | bytes 196616 | tf_op jit(solution)/shard_map/ppermute | solution.py:234
  34.1 7.0 %collective-permute-start.2 = (bf16[64,512]{1,0:T(8,128)(2,1)S(1)}, bf16[64,512]{1,0:T(8,128)(2,1)S(1)}, u32[]{:S(2)}, u32[]{:S(2)}) collective-permute-start(bf16[64,512]{1,0:T(8,128)(2,1)S(1)} %get-tuple-element.34), channel_id=1, source_target_pairs={{0,3},{1,4},{2,5},{3,6},{4,7},{5,0},{6,1},{7,2},{8,11},{9,12},{10,... | collective-permute-start | bytes 196616 | tf_op jit(solution)/shard_map/ppermute | solution.py:234
  41.1 2.8 %collective-permute-start.3 = (bf16[64,512]{1,0:T(8,128)(2,1)S(1)}, bf16[64,512]{1,0:T(8,128)(2,1)S(1)}, u32[]{:S(2)}, u32[]{:S(2)}) collective-permute-start(bf16[64,512]{1,0:T(8,128)(2,1)S(1)} %get-tuple-element.33), channel_id=1, source_target_pairs={{0,4},{1,5},{2,6},{3,7},{4,0},{5,1},{6,2},{7,3},{8,12},{9,13},{10,... | collective-permute-start | bytes 196616 | tf_op jit(solution)/shard_map/ppermute | solution.py:234
  44.0 6.4 %collective-permute-start.4 = (bf16[64,512]{1,0:T(8,128)(2,1)S(1)}, bf16[64,512]{1,0:T(8,128)(2,1)S(1)}, u32[]{:S(2)}, u32[]{:S(2)}) collective-permute-start(bf16[64,512]{1,0:T(8,128)(2,1)S(1)} %get-tuple-element.32), channel_id=1, source_target_pairs={{0,5},{1,6},{2,7},{3,0},{4,1},{5,2},{6,3},{7,4},{8,13},{9,14},{10,... | collective-permute-start | bytes 196616 | tf_op jit(solution)/shard_map/ppermute | solution.py:234
  50.4 3.4 %collective-permute-start.5 = (bf16[64,512]{1,0:T(8,128)(2,1)S(1)}, bf16[64,512]{1,0:T(8,128)(2,1)S(1)}, u32[]{:S(2)}, u32[]{:S(2)}) collective-permute-start(bf16[64,512]{1,0:T(8,128)(2,1)S(1)} %get-tuple-element.31), channel_id=1, source_target_pairs={{0,6},{1,7},{2,0},{3,1},{4,2},{5,3},{6,4},{7,5},{8,14},{9,15},{10,... | collective-permute-start | bytes 196616 | tf_op jit(solution)/shard_map/ppermute | solution.py:234
  54.5 0.9 collective-permute-done.4.refs_4_.refs_5_
  55.5 3.1 %collective-permute-done.5.refs_5_.refs_6_ = bf16[64,512]{1,0:T(8,128)(2,1)S(1)} collective-permute-done((bf16[64,512]{1,0:T(8,128)(2,1)S(1)}, bf16[64,512]{1,0:T(8,128)(2,1)S(1)}, u32[]{:S(2)}, u32[]{:S(2)}) %collective-permute-start.5) | collective-permute-done | bytes 65568 | tf_op jit(solution)/shard_map/ppermute | solution.py:234
  59.2 3.9 %shard_map.127 = bf16[32,256,128]{2,1,0:T(8,128)(2,1)} custom-call(s32[32]{0:T(128)} %reshape.71.codes_ref, bf16[8,2,128,512]{3,2,1,0:T(8,128)(2,1)} %bitcast.24, bf16[64,512]{1,0:T(8,128)(2,1)} %copy-done.7, bf16[64,512]{1,0:T(8,128)(2,1)} %copy-done.8, bf16[64,512]{1,0:T(8,128)(2,1)} %copy-done.9, bf16[64,512]{1,0:T(8,128)(2,1)} %copy-done.10, ...), custom_call_target="tpu_custom_call" | custom-call | tf_op jit(solution)/shard_map/pallas_call | solution.py:183
  63.1 6.0 %all-to-all-start.1 = ((bf16[8,4,256,128]{3,2,1,0:T(8,128)(2,1)}), bf16[8,4,256,128]{3,2,1,0:T(8,128)(2,1)S(1)}, u32[]{:S(2)}, u32[]{:S(2)}) async-start(bf16[8,4,256,128]{3,2,1,0:T(8,128)(2,1)} %bitcast.27), calls=%async_computation.1 | async-start | bytes 4194304 | tf_op jit(solution)/shard_map/all_to_all | solution.py:292
  69.1 5.2 %collective-permute-start.6 = (bf16[64,512]{1,0:T(8,128)(2,1)S(1)}, bf16[64,512]{1,0:T(8,128)(2,1)S(1)}, u32[]{:S(2)}, u32[]{:S(2)}) collective-permute-start(bf16[64,512]{1,0:T(8,128)(2,1)S(1)} %get-tuple-element.37), channel_id=1, source_target_pairs={{0,7},{1,0},{2,1},{3,2},{4,3},{5,4},{6,5},{7,6},{8,15},{9,8},{10,9... | collective-permute-start | bytes 196616 | tf_op jit(solution)/shard_map/ppermute | solution.py:234
  74.4 1.5 collective-permute-done.6.refs_0_.refs_7_
  76.5 3.9 %shard_map.128.kept_ref = bf16[32,256,128]{2,1,0:T(8,128)(2,1)} custom-call(s32[32]{0:T(128)} %reshape.71.codes_ref, bf16[8,2,128,512]{3,2,1,0:T(8,128)(2,1)} %bitcast.25, bf16[64,512]{1,0:T(8,128)(2,1)} %copy-done.13), custom_call_target="tpu_custom_call" | custom-call | tf_op jit(solution)/shard_map/pallas_call | solution.py:183
  80.4 15.1 %all-to-all-done.1 = bf16[8,4,256,128]{3,2,1,0:T(8,128)(2,1)S(1)} async-done(((bf16[8,4,256,128]{3,2,1,0:T(8,128)(2,1)}), bf16[8,4,256,128]{3,2,1,0:T(8,128)(2,1)S(1)}, u32[]{:S(2)}, u32[]{:S(2)}) %all-to-all-start.1) | async-done | bytes 2097184 | tf_op jit(solution)/shard_map/all_to_all | solution.py:292
  95.5 0.6 slice_bitcast_fusion.2.after_ref
  96.1 0.7 copy-done.4
  96.8 4.4 %all-to-all-start.2 = ((bf16[8,4,256,128]{3,2,1,0:T(8,128)(2,1)}), bf16[8,4,256,128]{3,2,1,0:T(8,128)(2,1)S(1)}, u32[]{:S(2)}, u32[]{:S(2)}) async-start(bf16[8,4,256,128]{3,2,1,0:T(8,128)(2,1)} %bitcast.23), calls=%async_computation.2 | async-start | bytes 4194304 | tf_op jit(solution)/shard_map/all_to_all | solution.py:292
  101.2 0.7 pad_add_fusion.base_ref
  101.8 12.7 %shard_map.130 = (bf16[512,512]{1,0:T(8,128)(2,1)}, bf16[4,2,4,256,128]{4,3,2,1,0:T(8,128)(2,1)}, f32[4,1,512]{2,1,0:T(1,128)}, f32[4,1,512]{2,1,0:T(1,128)}) custom-call(s32[12]{0:T(128)} %copy-done.18, s32[64]{0:T(128)} %lens_ref.3, s32[2]{0:T(128)} %pad_add_fusion.base_ref, bf16[512,512]{1,0:T(8,128)(2,1)} %q_ref.3, bf16[512,512]{1,0:T(8,128)(2,1)} %k_ref.3, ...), custom_call_target="tpu_custom_call" | custom-call | flops 2147483648 | bytes 8388608 | tf_op jit(solution)/shard_map/pallas_call | solution.py:320
  114.6 13.0 %all-to-all-done.2 = bf16[8,4,256,128]{3,2,1,0:T(8,128)(2,1)S(1)} async-done(((bf16[8,4,256,128]{3,2,1,0:T(8,128)(2,1)}), bf16[8,4,256,128]{3,2,1,0:T(8,128)(2,1)S(1)}, u32[]{:S(2)}, u32[]{:S(2)}) %all-to-all-start.2) | async-done | bytes 2097184 | tf_op jit(solution)/shard_map/all_to_all | solution.py:292
  128.2 0.7 copy-done.5
  128.9 4.4 %all-to-all-start.3 = ((bf16[8,4,256,128]{3,2,1,0:T(8,128)(2,1)}), bf16[8,4,256,128]{3,2,1,0:T(8,128)(2,1)S(1)}, u32[]{:S(2)}, u32[]{:S(2)}) async-start(bf16[8,4,256,128]{3,2,1,0:T(8,128)(2,1)} %bitcast.28), calls=%async_computation.3 | async-start | bytes 4194304 | tf_op jit(solution)/shard_map/all_to_all | solution.py:292
  133.2 17.4 %shard_map.131 = (bf16[512,512]{1,0:T(8,128)(2,1)}, bf16[512,512]{1,0:T(8,128)(2,1)}, bf16[512,512]{1,0:T(8,128)(2,1)}, bf16[4,2,4,256,128]{4,3,2,1,0:T(8,128)(2,1)}) custom-call(s32[12]{0:T(128)} %copy-done.18, s32[64]{0:T(128)} %lens_ref.3, s32[2]{0:T(128)} %pad_add_fusion.base_ref, bf16[512,512]{1,0:T(8,128)(2,1)} %q_ref.3, bf16[512,512]{1,0:T(8,128)(2,1)} %k_ref.3, ...), custom_call_target="tpu_custom_call" | custom-call | flops 5368709120 | bytes 8388608 | tf_op jit(solution)/shard_map/pallas_call | solution.py:339
  150.6 9.0 %all-to-all-done.3.terms_ref = bf16[8,4,256,128]{3,2,1,0:T(8,128)(2,1)S(1)} async-done(((bf16[8,4,256,128]{3,2,1,0:T(8,128)(2,1)}), bf16[8,4,256,128]{3,2,1,0:T(8,128)(2,1)S(1)}, u32[]{:S(2)}, u32[]{:S(2)}) %all-to-all-start.3) | async-done | bytes 2097184 | tf_op jit(solution)/shard_map/all_to_all | solution.py:292
  160.2 5.2 %all-to-all-start.4 = ((bf16[8,4,256,128]{3,2,1,0:T(8,128)(2,1)}), bf16[8,4,256,128]{3,2,1,0:T(8,128)(2,1)}, u32[]{:S(2)}, u32[]{:S(2)}) async-start(bf16[8,4,256,128]{3,2,1,0:T(8,128)(2,1)} %bitcast.26), calls=%async_computation.4 | async-start | bytes 4194304 | tf_op jit(solution)/shard_map/all_to_all | solution.py:292
  165.4 2.8 %shard_map.136 = bf16[1024,512]{1,0:T(8,128)(2,1)} custom-call(s32[32]{0:T(128)S(1)} %copy-done.3, bf16[8,4,256,128]{3,2,1,0:T(8,128)(2,1)S(1)} %all-to-all-done.3.terms_ref), custom_call_target="tpu_custom_call" | custom-call | tf_op jit(solution)/shard_map/pallas_call | solution.py:217
  168.3 0.7 constant_dynamic-slice_fusion
  169.0 3.5 %collective-permute-start.7 = (bf16[64,512]{1,0:T(8,128)(2,1)S(1)}, bf16[64,512]{1,0:T(8,128)(2,1)S(1)}, u32[]{:S(2)}, u32[]{:S(2)}) collective-permute-start(bf16[64,512]{1,0:T(8,128)(2,1)S(1)} %get-tuple-element.28), channel_id=1, source_target_pairs={{0,1},{1,2},{2,3},{3,4},{4,5},{5,6},{6,7},{7,0},{8,9},{9,10},{10,1... | collective-permute-start | bytes 196616 | tf_op jit(solution)/shard_map/ppermute | solution.py:234
  172.5 4.1 %collective-permute-start.8 = (bf16[64,512]{1,0:T(8,128)(2,1)S(1)}, bf16[64,512]{1,0:T(8,128)(2,1)S(1)}, u32[]{:S(2)}, u32[]{:S(2)}) collective-permute-start(bf16[64,512]{1,0:T(8,128)(2,1)S(1)} %get-tuple-element.27), channel_id=1, source_target_pairs={{0,2},{1,3},{2,4},{3,5},{4,6},{5,7},{6,0},{7,1},{8,10},{9,11},{10,... | collective-permute-start | bytes 196616 | tf_op jit(solution)/shard_map/ppermute | solution.py:234
  176.6 4.9 %collective-permute-start.9 = (bf16[64,512]{1,0:T(8,128)(2,1)S(1)}, bf16[64,512]{1,0:T(8,128)(2,1)S(1)}, u32[]{:S(2)}, u32[]{:S(2)}) collective-permute-start(bf16[64,512]{1,0:T(8,128)(2,1)S(1)} %get-tuple-element.26), channel_id=1, source_target_pairs={{0,3},{1,4},{2,5},{3,6},{4,7},{5,0},{6,1},{7,2},{8,11},{9,12},{10,... | collective-permute-start | bytes 196616 | tf_op jit(solution)/shard_map/ppermute | solution.py:234
  181.5 3.7 %collective-permute-done.9.refs_3_.refs_2_ = bf16[64,512]{1,0:T(8,128)(2,1)S(1)} collective-permute-done((bf16[64,512]{1,0:T(8,128)(2,1)S(1)}, bf16[64,512]{1,0:T(8,128)(2,1)S(1)}, u32[]{:S(2)}, u32[]{:S(2)}) %collective-permute-start.9) | collective-permute-done | bytes 65568 | tf_op jit(solution)/shard_map/ppermute | solution.py:234
  185.2 6.7 %all-to-all-done.4.terms_ref = bf16[8,4,256,128]{3,2,1,0:T(8,128)(2,1)} async-done(((bf16[8,4,256,128]{3,2,1,0:T(8,128)(2,1)}), bf16[8,4,256,128]{3,2,1,0:T(8,128)(2,1)}, u32[]{:S(2)}, u32[]{:S(2)}) %all-to-all-start.4) | async-done | bytes 2097184 | tf_op jit(solution)/shard_map/all_to_all | solution.py:292
  191.9 4.6 %shard_map.135 = bf16[1024,512]{1,0:T(8,128)(2,1)} custom-call(s32[32]{0:T(128)S(1)} %copy-done.3, bf16[8,4,256,128]{3,2,1,0:T(8,128)(2,1)} %all-to-all-done.4.terms_ref, bf16[64,512]{1,0:T(8,128)(2,1)S(1)} %collective-permute-done.7.refs_1_.refs_0_, bf16[64,512]{1,0:T(8,128)(2,1)S(1)} %collective-permute-done.8.refs_2_.refs_1_, ...), custom_call_target="tpu_custom_call" | custom-call | tf_op jit(solution)/shard_map/pallas_call | solution.py:217
  196.5 6.0 %all-to-all-start.5 = ((bf16[8,128,512]{2,1,0:T(8,128)(2,1)}), bf16[8,128,512]{2,1,0:T(8,128)(2,1)S(1)}, u32[]{:S(2)}, u32[]{:S(2)}) async-start(bf16[8,128,512]{2,1,0:T(8,128)(2,1)} %bitcast.16), calls=%async_computation.5 | async-start | bytes 2097152 | tf_op jit(solution)/shard_map/all_to_all | solution.py:366
  202.4 6.3 %collective-permute-start.10 = (bf16[64,512]{1,0:T(8,128)(2,1)S(1)}, bf16[64,512]{1,0:T(8,128)(2,1)S(1)}, u32[]{:S(2)}, u32[]{:S(2)}) collective-permute-start(bf16[64,512]{1,0:T(8,128)(2,1)S(1)} %get-tuple-element.25), channel_id=1, source_target_pairs={{0,4},{1,5},{2,6},{3,7},{4,0},{5,1},{6,2},{7,3},{8,12},{9,13},{10,... | collective-permute-start | bytes 196616 | tf_op jit(solution)/shard_map/ppermute | solution.py:234
  208.7 2.2 collective-permute-start.11
  211.0 5.0 %collective-permute-start.12 = (bf16[64,512]{1,0:T(8,128)(2,1)S(1)}, bf16[64,512]{1,0:T(8,128)(2,1)S(1)}, u32[]{:S(2)}, u32[]{:S(2)}) collective-permute-start(bf16[64,512]{1,0:T(8,128)(2,1)S(1)} %get-tuple-element.23), channel_id=1, source_target_pairs={{0,6},{1,7},{2,0},{3,1},{4,2},{5,3},{6,4},{7,5},{8,14},{9,15},{10,... | collective-permute-start | bytes 196616 | tf_op jit(solution)/shard_map/ppermute | solution.py:234
  216.0 2.7 %collective-permute-start.13 = (bf16[64,512]{1,0:T(8,128)(2,1)S(1)}, bf16[64,512]{1,0:T(8,128)(2,1)S(1)}, u32[]{:S(2)}, u32[]{:S(2)}) collective-permute-start(bf16[64,512]{1,0:T(8,128)(2,1)S(1)} %get-tuple-element.22), channel_id=1, source_target_pairs={{0,7},{1,0},{2,1},{3,2},{4,3},{5,4},{6,5},{7,6},{8,15},{9,8},{10,9... | collective-permute-start | bytes 196616 | tf_op jit(solution)/shard_map/ppermute | solution.py:234
  218.7 1.5 collective-permute-done.12.refs_6_
  220.3 1.3 collective-permute-done.13.refs_7_
  222.2 1.9 shard_map.132
  224.1 5.8 %all-to-all-done.5 = bf16[8,128,512]{2,1,0:T(8,128)(2,1)S(1)} async-done(((bf16[8,128,512]{2,1,0:T(8,128)(2,1)}), bf16[8,128,512]{2,1,0:T(8,128)(2,1)S(1)}, u32[]{:S(2)}, u32[]{:S(2)}) %all-to-all-start.5) | async-done | bytes 1048608 | tf_op jit(solution)/shard_map/all_to_all | solution.py:366
  229.9 0.8 reduce_sum.12
  (62 shorter events, 4.1 us)
Async XLA Ops:
  7.2 51.4 %all-gather.3.cloned.1.call-start = ((), (), s32[]{:S(2)}) async-start(), calls=%async_computation.8 | async-start | bytes 2359296 | tf_op jit(solution)/shard_map/all_gather | solution.py:259
  10.7 39.6 %collective-permute-start = (bf16[64,512]{1,0:T(8,128)(2,1)S(1)}, bf16[64,512]{1,0:T(8,128)(2,1)S(1)}, u32[]{:S(2)}, u32[]{:S(2)}) collective-permute-start(bf16[64,512]{1,0:T(8,128)(2,1)S(1)} %get-tuple-element.36), channel_id=1, source_target_pairs={{0,1},{1,2},{2,3},{3,4},{4,5},{5,6},{6,7},{7,0},{8,9},{9,10},{10,1... | collective-permute-start | bytes 196616 | tf_op jit(solution)/shard_map/ppermute | solution.py:234
  16.4 46.7 %copy-start.18 = (s32[12]{0:T(128)}, s32[12]{0:T(128)S(1)}, u32[]{:S(2)}) copy-start(s32[12]{0:T(128)S(1)} %reshape.69.sel_ref) | copy-start | bytes 148
  17.2 36.6 %all-to-all-start = ((s32[64,1,128]{2,1,0:T(1,128)}), s32[64,1,128]{2,1,0:T(1,128)S(1)}, u32[]{:S(2)}, u32[]{:S(2)}) async-start(s32[64,1,128]{2,1,0:T(1,128)} %broadcast_in_dim.19), calls=%async_computation | async-start | bytes 65536 | tf_op jit(solution)/shard_map/all_to_all | solution.py:279
  28.3 26.2 %collective-permute-start.1 = (bf16[64,512]{1,0:T(8,128)(2,1)S(1)}, bf16[64,512]{1,0:T(8,128)(2,1)S(1)}, u32[]{:S(2)}, u32[]{:S(2)}) collective-permute-start(bf16[64,512]{1,0:T(8,128)(2,1)S(1)} %get-tuple-element.35), channel_id=1, source_target_pairs={{0,2},{1,3},{2,4},{3,5},{4,6},{5,7},{6,0},{7,1},{8,10},{9,11},{10,... | collective-permute-start | bytes 196616 | tf_op jit(solution)/shard_map/ppermute | solution.py:234
  34.1 20.4 %collective-permute-start.2 = (bf16[64,512]{1,0:T(8,128)(2,1)S(1)}, bf16[64,512]{1,0:T(8,128)(2,1)S(1)}, u32[]{:S(2)}, u32[]{:S(2)}) collective-permute-start(bf16[64,512]{1,0:T(8,128)(2,1)S(1)} %get-tuple-element.34), channel_id=1, source_target_pairs={{0,3},{1,4},{2,5},{3,6},{4,7},{5,0},{6,1},{7,2},{8,11},{9,12},{10,... | collective-permute-start | bytes 196616 | tf_op jit(solution)/shard_map/ppermute | solution.py:234
  41.1 13.4 %collective-permute-start.3 = (bf16[64,512]{1,0:T(8,128)(2,1)S(1)}, bf16[64,512]{1,0:T(8,128)(2,1)S(1)}, u32[]{:S(2)}, u32[]{:S(2)}) collective-permute-start(bf16[64,512]{1,0:T(8,128)(2,1)S(1)} %get-tuple-element.33), channel_id=1, source_target_pairs={{0,4},{1,5},{2,6},{3,7},{4,0},{5,1},{6,2},{7,3},{8,12},{9,13},{10,... | collective-permute-start | bytes 196616 | tf_op jit(solution)/shard_map/ppermute | solution.py:234
  44.0 11.5 %collective-permute-start.4 = (bf16[64,512]{1,0:T(8,128)(2,1)S(1)}, bf16[64,512]{1,0:T(8,128)(2,1)S(1)}, u32[]{:S(2)}, u32[]{:S(2)}) collective-permute-start(bf16[64,512]{1,0:T(8,128)(2,1)S(1)} %get-tuple-element.32), channel_id=1, source_target_pairs={{0,5},{1,6},{2,7},{3,0},{4,1},{5,2},{6,3},{7,4},{8,13},{9,14},{10,... | collective-permute-start | bytes 196616 | tf_op jit(solution)/shard_map/ppermute | solution.py:234
  50.4 8.2 %copy-start.7 = (bf16[64,512]{1,0:T(8,128)(2,1)}, bf16[64,512]{1,0:T(8,128)(2,1)S(1)}, u32[]{:S(2)}) copy-start(bf16[64,512]{1,0:T(8,128)(2,1)S(1)} %collective-permute-done.refs_0_.refs_1_) | copy-start | bytes 196612
  50.4 8.2 %collective-permute-start.5 = (bf16[64,512]{1,0:T(8,128)(2,1)S(1)}, bf16[64,512]{1,0:T(8,128)(2,1)S(1)}, u32[]{:S(2)}, u32[]{:S(2)}) collective-permute-start(bf16[64,512]{1,0:T(8,128)(2,1)S(1)} %get-tuple-element.31), channel_id=1, source_target_pairs={{0,6},{1,7},{2,0},{3,1},{4,2},{5,3},{6,4},{7,5},{8,14},{9,15},{10,... | collective-permute-start | bytes 196616 | tf_op jit(solution)/shard_map/ppermute | solution.py:234
  54.5 4.1 %copy-start.8 = (bf16[64,512]{1,0:T(8,128)(2,1)}, bf16[64,512]{1,0:T(8,128)(2,1)S(1)}, u32[]{:S(2)}) copy-start(bf16[64,512]{1,0:T(8,128)(2,1)S(1)} %collective-permute-done.1.refs_1_.refs_2_) | copy-start | bytes 196612
  54.5 4.1 %copy-start.9 = (bf16[64,512]{1,0:T(8,128)(2,1)}, bf16[64,512]{1,0:T(8,128)(2,1)S(1)}, u32[]{:S(2)}) copy-start(bf16[64,512]{1,0:T(8,128)(2,1)S(1)} %collective-permute-done.2.refs_2_.refs_3_) | copy-start | bytes 196612
  54.5 4.1 %copy-start.10 = (bf16[64,512]{1,0:T(8,128)(2,1)}, bf16[64,512]{1,0:T(8,128)(2,1)S(1)}, u32[]{:S(2)}) copy-start(bf16[64,512]{1,0:T(8,128)(2,1)S(1)} %collective-permute-done.3.refs_3_.refs_4_) | copy-start | bytes 196612
  55.5 3.1 %copy-start.11 = (bf16[64,512]{1,0:T(8,128)(2,1)}, bf16[64,512]{1,0:T(8,128)(2,1)S(1)}, u32[]{:S(2)}) copy-start(bf16[64,512]{1,0:T(8,128)(2,1)S(1)} %collective-permute-done.4.refs_4_.refs_5_) | copy-start | bytes 196612
  58.5 0.6 copy-start.12
  63.1 32.4 %all-to-all-start.1 = ((bf16[8,4,256,128]{3,2,1,0:T(8,128)(2,1)}), bf16[8,4,256,128]{3,2,1,0:T(8,128)(2,1)S(1)}, u32[]{:S(2)}, u32[]{:S(2)}) async-start(bf16[8,4,256,128]{3,2,1,0:T(8,128)(2,1)} %bitcast.27), calls=%async_computation.1 | async-start | bytes 4194304 | tf_op jit(solution)/shard_map/all_to_all | solution.py:292
  69.1 6.8 %collective-permute-start.6 = (bf16[64,512]{1,0:T(8,128)(2,1)S(1)}, bf16[64,512]{1,0:T(8,128)(2,1)S(1)}, u32[]{:S(2)}, u32[]{:S(2)}) collective-permute-start(bf16[64,512]{1,0:T(8,128)(2,1)S(1)} %get-tuple-element.37), channel_id=1, source_target_pairs={{0,7},{1,0},{2,1},{3,2},{4,3},{5,4},{6,5},{7,6},{8,15},{9,8},{10,9... | collective-permute-start | bytes 196616 | tf_op jit(solution)/shard_map/ppermute | solution.py:234
  75.9 0.6 copy-start.13
  95.5 1.3 copy-start.4
  96.8 30.7 %all-to-all-start.2 = ((bf16[8,4,256,128]{3,2,1,0:T(8,128)(2,1)}), bf16[8,4,256,128]{3,2,1,0:T(8,128)(2,1)S(1)}, u32[]{:S(2)}, u32[]{:S(2)}) async-start(bf16[8,4,256,128]{3,2,1,0:T(8,128)(2,1)} %bitcast.23), calls=%async_computation.2 | async-start | bytes 4194304 | tf_op jit(solution)/shard_map/all_to_all | solution.py:292
  127.5 1.3 copy-start.5
  128.9 30.7 %all-to-all-start.3 = ((bf16[8,4,256,128]{3,2,1,0:T(8,128)(2,1)}), bf16[8,4,256,128]{3,2,1,0:T(8,128)(2,1)S(1)}, u32[]{:S(2)}, u32[]{:S(2)}) async-start(bf16[8,4,256,128]{3,2,1,0:T(8,128)(2,1)} %bitcast.28), calls=%async_computation.3 | async-start | bytes 4194304 | tf_op jit(solution)/shard_map/all_to_all | solution.py:292
  160.2 5.2 %copy-start.3 = (s32[32]{0:T(128)S(1)}, s32[32]{0:T(128)}, u32[]{:S(2)}) copy-start(s32[32]{0:T(128)} %reshape.71.codes_ref) | copy-start | bytes 388
  160.2 31.7 %all-to-all-start.4 = ((bf16[8,4,256,128]{3,2,1,0:T(8,128)(2,1)}), bf16[8,4,256,128]{3,2,1,0:T(8,128)(2,1)}, u32[]{:S(2)}, u32[]{:S(2)}) async-start(bf16[8,4,256,128]{3,2,1,0:T(8,128)(2,1)} %bitcast.26), calls=%async_computation.4 | async-start | bytes 4194304 | tf_op jit(solution)/shard_map/all_to_all | solution.py:292
  165.4 2.9 %copy-start.6 = (bf16[512,512]{1,0:T(8,128)(2,1)S(1)}, bf16[512,512]{1,0:T(8,128)(2,1)}, u32[]{:S(2)}) copy-start(bf16[512,512]{1,0:T(8,128)(2,1)} %get-tuple-element.16) | copy-start | bytes 1572868
  165.4 65.3 %reduce-scatter.2.cloned.1.call-start = ((), (), s32[]{:S(2)}) async-start(), calls=%async_computation.7 | async-start | bytes 1179648 | tf_op jit(solution)/shard_map/reduce_scatter | solution.py:337
  169.0 12.5 %collective-permute-start.7 = (bf16[64,512]{1,0:T(8,128)(2,1)S(1)}, bf16[64,512]{1,0:T(8,128)(2,1)S(1)}, u32[]{:S(2)}, u32[]{:S(2)}) collective-permute-start(bf16[64,512]{1,0:T(8,128)(2,1)S(1)} %get-tuple-element.28), channel_id=1, source_target_pairs={{0,1},{1,2},{2,3},{3,4},{4,5},{5,6},{6,7},{7,0},{8,9},{9,10},{10,1... | collective-permute-start | bytes 196616 | tf_op jit(solution)/shard_map/ppermute | solution.py:234
  172.5 9.0 %collective-permute-start.8 = (bf16[64,512]{1,0:T(8,128)(2,1)S(1)}, bf16[64,512]{1,0:T(8,128)(2,1)S(1)}, u32[]{:S(2)}, u32[]{:S(2)}) collective-permute-start(bf16[64,512]{1,0:T(8,128)(2,1)S(1)} %get-tuple-element.27), channel_id=1, source_target_pairs={{0,2},{1,3},{2,4},{3,5},{4,6},{5,7},{6,0},{7,1},{8,10},{9,11},{10,... | collective-permute-start | bytes 196616 | tf_op jit(solution)/shard_map/ppermute | solution.py:234
  176.6 8.6 %collective-permute-start.9 = (bf16[64,512]{1,0:T(8,128)(2,1)S(1)}, bf16[64,512]{1,0:T(8,128)(2,1)S(1)}, u32[]{:S(2)}, u32[]{:S(2)}) collective-permute-start(bf16[64,512]{1,0:T(8,128)(2,1)S(1)} %get-tuple-element.26), channel_id=1, source_target_pairs={{0,3},{1,4},{2,5},{3,6},{4,7},{5,0},{6,1},{7,2},{8,11},{9,12},{10,... | collective-permute-start | bytes 196616 | tf_op jit(solution)/shard_map/ppermute | solution.py:234
  181.5 15.0 %copy-start = (bf16[64,512]{1,0:T(8,128)(2,1)}, bf16[64,512]{1,0:T(8,128)(2,1)S(1)}, u32[]{:S(2)}) copy-start(bf16[64,512]{1,0:T(8,128)(2,1)S(1)} %collective-permute-done.7.refs_1_.refs_0_) | copy-start | bytes 196612
  181.5 14.9 %copy-start.1 = (bf16[64,512]{1,0:T(8,128)(2,1)}, bf16[64,512]{1,0:T(8,128)(2,1)S(1)}, u32[]{:S(2)}) copy-start(bf16[64,512]{1,0:T(8,128)(2,1)S(1)} %collective-permute-done.8.refs_2_.refs_1_) | copy-start | bytes 196612
  185.2 11.2 %copy-start.2 = (bf16[64,512]{1,0:T(8,128)(2,1)}, bf16[64,512]{1,0:T(8,128)(2,1)S(1)}, u32[]{:S(2)}) copy-start(bf16[64,512]{1,0:T(8,128)(2,1)S(1)} %collective-permute-done.9.refs_3_.refs_2_) | copy-start | bytes 196612
  196.5 33.4 %all-to-all-start.5 = ((bf16[8,128,512]{2,1,0:T(8,128)(2,1)}), bf16[8,128,512]{2,1,0:T(8,128)(2,1)S(1)}, u32[]{:S(2)}, u32[]{:S(2)}) async-start(bf16[8,128,512]{2,1,0:T(8,128)(2,1)} %bitcast.16), calls=%async_computation.5 | async-start | bytes 2097152 | tf_op jit(solution)/shard_map/all_to_all | solution.py:366
  202.4 16.3 %collective-permute-start.10 = (bf16[64,512]{1,0:T(8,128)(2,1)S(1)}, bf16[64,512]{1,0:T(8,128)(2,1)S(1)}, u32[]{:S(2)}, u32[]{:S(2)}) collective-permute-start(bf16[64,512]{1,0:T(8,128)(2,1)S(1)} %get-tuple-element.25), channel_id=1, source_target_pairs={{0,4},{1,5},{2,6},{3,7},{4,0},{5,1},{6,2},{7,3},{8,12},{9,13},{10,... | collective-permute-start | bytes 196616 | tf_op jit(solution)/shard_map/ppermute | solution.py:234
  208.7 10.0 %collective-permute-start.11 = (bf16[64,512]{1,0:T(8,128)(2,1)S(1)}, bf16[64,512]{1,0:T(8,128)(2,1)S(1)}, u32[]{:S(2)}, u32[]{:S(2)}) collective-permute-start(bf16[64,512]{1,0:T(8,128)(2,1)S(1)} %get-tuple-element.24), channel_id=1, source_target_pairs={{0,5},{1,6},{2,7},{3,0},{4,1},{5,2},{6,3},{7,4},{8,13},{9,14},{10,... | collective-permute-start | bytes 196616 | tf_op jit(solution)/shard_map/ppermute | solution.py:234
  211.0 9.3 %collective-permute-start.12 = (bf16[64,512]{1,0:T(8,128)(2,1)S(1)}, bf16[64,512]{1,0:T(8,128)(2,1)S(1)}, u32[]{:S(2)}, u32[]{:S(2)}) collective-permute-start(bf16[64,512]{1,0:T(8,128)(2,1)S(1)} %get-tuple-element.23), channel_id=1, source_target_pairs={{0,6},{1,7},{2,0},{3,1},{4,2},{5,3},{6,4},{7,5},{8,14},{9,15},{10,... | collective-permute-start | bytes 196616 | tf_op jit(solution)/shard_map/ppermute | solution.py:234
  216.0 5.6 %collective-permute-start.13 = (bf16[64,512]{1,0:T(8,128)(2,1)S(1)}, bf16[64,512]{1,0:T(8,128)(2,1)S(1)}, u32[]{:S(2)}, u32[]{:S(2)}) collective-permute-start(bf16[64,512]{1,0:T(8,128)(2,1)S(1)} %get-tuple-element.22), channel_id=1, source_target_pairs={{0,7},{1,0},{2,1},{3,2},{4,3},{5,4},{6,5},{7,6},{8,15},{9,8},{10,9... | collective-permute-start | bytes 196616 | tf_op jit(solution)/shard_map/ppermute | solution.py:234
  218.7 2.8 %copy-start.14 = (bf16[64,512]{1,0:T(8,128)(2,1)}, bf16[64,512]{1,0:T(8,128)(2,1)S(1)}, u32[]{:S(2)}) copy-start(bf16[64,512]{1,0:T(8,128)(2,1)S(1)} %collective-permute-done.10.refs_4_) | copy-start | bytes 196612
  218.7 2.8 %copy-start.15 = (bf16[64,512]{1,0:T(8,128)(2,1)}, bf16[64,512]{1,0:T(8,128)(2,1)S(1)}, u32[]{:S(2)}) copy-start(bf16[64,512]{1,0:T(8,128)(2,1)S(1)} %collective-permute-done.11.refs_5_) | copy-start | bytes 196612
  220.3 1.3 copy-start.16
  221.5 0.6 copy-start.17
Sparse Core Ops, SparseCore 0:
  10.7 45.4 all-gather.2
  169.7 36.0 reduce-scatter.1
